TPU v7x, 128 devices: a whole 4x4x4 slice. The times are simulated.
128 devices in a mesh: pipe: 2 (over core), ctx: 8 (over x, z_lo), tp: 8 (over y, z_hi).
Axes of the slice: x: 4, y: 4, z: 4 (z_hi: 2, z_lo: 2; z = z_hi * 2 + z_lo), core: 2. Of those that a mesh axis runs over, the one named last changes fastest.
Arguments:
- latents: float32 [3, 1024, 1024], P(None, 'ctx'), may hold values from -6 to 6
- cotangent: float32 [3, 1024, 1024], P(None, 'ctx'), may hold values from -6 to 6
- labels: int32 [3], replicated, may hold values from 0 to 999
- steps: int32 [3], replicated, may hold values from 0 to 999
- label_table: bfloat16 [1000, 1024], replicated, may hold values from -5 to 5
- w_ada: bfloat16 [2, 1024, 6, 1024], P('pipe', None, None, ('ctx', 'tp')), may hold values from -0.1875 to 0.1875
- w_qkv: bfloat16 [2, 1024, 3, 1024], P('pipe', 'ctx', None, 'tp'), may hold values from -0.1875 to 0.1875
- w_out: bfloat16 [2, 1024, 1024], P('pipe', 'tp', 'ctx'), may hold values from -0.75 to 0.75
- w_up: bfloat16 [2, 1024, 4096], P('pipe', 'ctx', 'tp'), may hold values from -0.1875 to 0.1875
- w_down: bfloat16 [2, 4096, 1024], P('pipe', 'tp', 'ctx'), may hold values from -0.09375 to 0.09375
Outputs:
- ends: float32 [2, 3, 1024, 1024], P('pipe', None, 'ctx')
- grad_table: float32 [1000, 1024], replicated
- grad_ada: float32 [2, 1024, 6, 1024], P('pipe', None, None, ('ctx', 'tp'))
- grad_qkv: float32 [2, 1024, 3, 1024], P('pipe', 'ctx', None, 'tp')
- grad_out: float32 [2, 1024, 1024], P('pipe', 'tp', 'ctx')
- grad_up: float32 [2, 1024, 4096], P('pipe', 'ctx', 'tp')
- grad_down: float32 [2, 4096, 1024], P('pipe', 'tp', 'ctx')
All inputs are finite; a program needn't handle non-finite values.
Results may differ from a plain program's by a relative error of at most 0.025.
Values may be sent and summed in bfloat16 or wider, within the bound.
No kernel may reach another device: no remote copies, remote signals or barrier semaphores. Data moves between devices by JAX's collectives and lax.ppermute only.
A program may use at most 128 MiB of HBM per device.

v0:
```python
from functools import partial
import math

import jax
import jax.numpy as jnp
from jax import lax
from jax.sharding import PartitionSpec as P

HEAD_DIM = 64
MICRO = 3
LAT_MB = 1


highest = lax.Precision.HIGHEST
epsilon = 1e-06


def in_one_piece(arrays, axis, dim, along):
    widths = [a.shape[along] for a in arrays]
    both = jnp.concatenate(arrays, axis=along)
    out = lax.all_gather(both, axis, axis=dim, tiled=True)
    return tuple(jnp.split(out, [sum(widths[:k]) for k in range(1, len(widths))], axis=along))


def sent_to_all(array, axis):
    size = lax.axis_size(axis)
    return lax.all_to_all(
        jnp.broadcast_to(array[None], (size, *array.shape)), axis, 0, 0, tiled=True
    )


def over_copies(array, axis):
    return sent_to_all(array, axis).astype(jnp.float32).sum(axis=0)


def split_up(array, dim, size):
    lengths = array.shape
    pieces = array.reshape(*lengths[:dim], size, lengths[dim] // size, *lengths[dim + 1 :])
    return jnp.moveaxis(pieces, dim, 0)


def sum_at_owner(array, axis, dim):
    pieces = split_up(array, dim, lax.axis_size(axis))
    arrived = lax.all_to_all(pieces, axis, split_axis=0, concat_axis=0, tiled=True)
    return arrived.astype(jnp.float32).sum(axis=0)


def sent_together(arrays, axis, dim, along):
    ends, at = ([], 0)
    for a in arrays[:-1]:
        at += a.shape[along]
        ends.append(at)
    both = jnp.concatenate(arrays, axis=along)
    return tuple(jnp.split(sum_at_owner(both, axis, dim), ends, axis=along))


def laid_out(pieces, dim):
    pieces = jnp.moveaxis(pieces, 0, dim)
    lengths = pieces.shape
    return pieces.reshape(*lengths[:dim], lengths[dim] * lengths[dim + 1], *lengths[dim + 2 :])


def collect(array, axis, dim):
    pieces = sent_to_all(array, axis)
    return laid_out(pieces, dim)


def gather_turned(arrays, axis, dims):
    turned = [jnp.moveaxis(a, dim, 0) for a, dim in zip(arrays, dims)]
    both = jnp.concatenate([t.reshape(len(t), -1) for t in turned], axis=1)
    out, at, outs = (lax.all_gather(both, axis, axis=0, tiled=True), 0, [])
    for t, dim in zip(turned, dims):
        piece = out[:, at : at + t[0].size].reshape(-1, *t.shape[1:])
        outs.append(jnp.moveaxis(piece, 0, dim))
        at += t[0].size
    return tuple(outs)


def from_behind(block, axis, distance):
    devices = range(lax.axis_size(axis))
    route = [(i - distance, i) for i in devices if i - distance in devices]
    return lax.ppermute(block, axis, route)


def sum_packed(arrays, axis, dims):
    size = lax.axis_size(axis)
    pieces = [split_up(a, dim, size) for a, dim in zip(arrays, dims)]
    lines = jnp.concatenate([b.reshape(size, -1) for b in pieces], axis=1)
    rows = max(16, -(-lines.shape[1] // 1024) * 8)
    lines = jnp.pad(lines, ((0, 0), (0, rows * 128 - lines.shape[1]))).reshape(-1, 128)
    flat, at, outs = (lax.psum_scatter(lines, axis, tiled=True).reshape(-1), 0, [])
    for b in pieces:
        part = b[0]
        outs.append(flat[at : at + part.size].reshape(part.shape))
        at += part.size
    return tuple(outs)


def total_of_pieces(array, axis):
    pieces = lax.all_gather(array, axis)
    return pieces.sum(axis=0)


def sinus_embed(steps_in, width):
    half_width = width // 2
    frequency = jnp.exp(-math.log(10000.0) * jnp.arange(half_width, dtype=jnp.float32) / half_width)
    angles = steps_in.astype(jnp.float32)[:, None] * frequency[None, :]
    return jnp.concatenate([jnp.cos(angles), jnp.sin(angles)], axis=1)


def norm_mod(values, shifts, scales):
    centre = jnp.mean(values, axis=-1, keepdims=True)
    centred = values - centre
    spread = jnp.mean(centred * centred, axis=-1, keepdims=True)
    return centred * lax.rsqrt(spread + epsilon) * (1.0 + scales) + shifts


def split_mod(mod_rows):
    return [mod_rows[:, member][:, None, :] for member in range(6)]


def heads_view(tensor, head_dim):
    return tensor.reshape(tensor.shape[0], tensor.shape[1], tensor.shape[2] // head_dim, head_dim)


def attention(queries, kv_all, head_dim):
    score_scale = 1.0 / math.sqrt(head_dim)
    query_heads = heads_view(queries, head_dim)
    key_heads = heads_view(kv_all[0], head_dim)
    value_heads = heads_view(kv_all[1], head_dim)
    scores = (
        jnp.einsum("bqhd,bkhd->bhqk", query_heads, key_heads, preferred_element_type=jnp.float32)
        * score_scale
    )
    attn_probs = jax.nn.softmax(scores, axis=-1)
    attended = jnp.einsum(
        "bhqk,bkhd->bqhd",
        attn_probs.astype(jnp.bfloat16),
        value_heads,
        preferred_element_type=jnp.float32,
    )
    attended = attended.astype(jnp.bfloat16).reshape(queries.shape)
    return (attended, attn_probs, query_heads, key_heads, value_heads)


def project_triple(inputs, shift_one, scale_one, w_qkv):
    normed = norm_mod(inputs, shift_one, scale_one).astype(jnp.bfloat16)
    triple = jnp.einsum("bsd,dcn->bscn", normed, w_qkv, preferred_element_type=jnp.float32).astype(
        jnp.bfloat16
    )
    return (normed, triple)


def layer_forward(inputs, mod_rows, weights, head_dim):
    shift_one, scale_one, gate_one, shift_two, scale_two, gate_two = split_mod(mod_rows)
    w_qkv, w_out, w_up, w_down = weights
    normed, triple = project_triple(inputs, shift_one, scale_one, w_qkv)
    kv_all = in_one_piece((triple[:, :, 1], triple[:, :, 2]), "ctx", 1, 0)
    attended = attention(triple[:, :, 0], kv_all, head_dim)[0]
    branch = over_copies(
        jnp.einsum("bsn,nd->bsd", attended, w_out, preferred_element_type=jnp.float32).astype(
            jnp.bfloat16
        ),
        "tp",
    ).astype(jnp.float32)
    middle = inputs + gate_one * branch
    normed_two = norm_mod(middle, shift_two, scale_two).astype(jnp.bfloat16)
    pre_act = jnp.einsum("bsd,df->bsf", normed_two, w_up, preferred_element_type=jnp.float32)
    hidden = jax.nn.gelu(pre_act, approximate=True).astype(jnp.bfloat16)
    mlp_out = over_copies(
        jnp.einsum("bsf,fd->bsd", hidden, w_down, preferred_element_type=jnp.float32).astype(
            jnp.bfloat16
        ),
        "tp",
    ).astype(jnp.float32)
    return (middle + gate_two * mlp_out, branch, mlp_out, kv_all)


def layer_backward(inputs, branch, mlp_out, kv_kept, grad_result, mod_rows, weights, head_dim):
    shift_one, scale_one, gate_one, shift_two, scale_two, gate_two = split_mod(mod_rows)
    w_qkv, w_out, w_up, w_down = weights
    score_scale = 1.0 / math.sqrt(head_dim)
    normed, triple = project_triple(inputs, shift_one, scale_one, w_qkv)
    attended, attn_probs, query_heads, key_heads, value_heads = attention(
        triple[:, :, 0], kv_kept, head_dim
    )
    middle = inputs + gate_one * branch
    normed_two = norm_mod(middle, shift_two, scale_two).astype(jnp.bfloat16)
    pre_act = jnp.einsum("bsd,df->bsf", normed_two, w_up, preferred_element_type=jnp.float32)
    hidden = jax.nn.gelu(pre_act, approximate=True).astype(jnp.bfloat16)
    grad_gate_two = jnp.sum(grad_result * mlp_out, axis=1)
    grad_mlp = (gate_two * grad_result).astype(jnp.bfloat16)
    grad_hidden = jnp.einsum("bsd,fd->bsf", grad_mlp, w_down, preferred_element_type=jnp.float32)
    gelu_back = jax.vjp(partial(jax.nn.gelu, approximate=True), pre_act)[1]
    grad_pre = gelu_back(grad_hidden)[0].astype(jnp.bfloat16)
    grad_normed_two = over_copies(
        jnp.einsum("bsf,df->bsd", grad_pre, w_up, preferred_element_type=jnp.float32).astype(
            jnp.bfloat16
        ),
        "tp",
    ).astype(jnp.float32)
    norm_back_two = jax.vjp(norm_mod, middle, shift_two, scale_two)[1]
    grad_mid_norm, grad_shift_two, grad_scale_two = norm_back_two(grad_normed_two)
    grad_middle = grad_result + grad_mid_norm
    grad_gate_one = jnp.sum(grad_middle * branch, axis=1)
    grad_branch = (gate_one * grad_middle).astype(jnp.bfloat16)
    grad_attended = jnp.einsum(
        "bsd,nd->bsn", grad_branch, w_out, preferred_element_type=jnp.float32
    ).astype(jnp.bfloat16)
    grad_heads = heads_view(grad_attended, head_dim)
    grad_probs = jnp.einsum(
        "bqhd,bkhd->bhqk", grad_heads, value_heads, preferred_element_type=jnp.float32
    )
    grad_values_all = jnp.einsum(
        "bhqk,bqhd->bkhd",
        attn_probs.astype(jnp.bfloat16),
        grad_heads,
        preferred_element_type=jnp.float32,
    )
    weighted = jnp.sum(attn_probs * grad_probs, axis=-1, keepdims=True)
    grad_scores = (attn_probs * (grad_probs - weighted)).astype(jnp.bfloat16)
    grad_queries = (
        jnp.einsum("bhqk,bkhd->bqhd", grad_scores, key_heads, preferred_element_type=jnp.float32)
        * score_scale
    )
    grad_queries = grad_queries.astype(jnp.bfloat16).reshape(attended.shape)
    grad_keys_all = (
        jnp.einsum("bhqk,bqhd->bkhd", grad_scores, query_heads, preferred_element_type=jnp.float32)
        * score_scale
    )
    full_shape = kv_kept[0].shape
    grad_keys, grad_values = sent_together(
        (
            grad_keys_all.reshape(full_shape).astype(jnp.bfloat16),
            grad_values_all.reshape(full_shape).astype(jnp.bfloat16),
        ),
        "ctx",
        1,
        0,
    )
    grad_triple = jnp.stack(
        [grad_queries, grad_keys.astype(jnp.bfloat16), grad_values.astype(jnp.bfloat16)], axis=2
    )
    grad_normed = over_copies(
        jnp.einsum("bscn,dcn->bsd", grad_triple, w_qkv, preferred_element_type=jnp.float32).astype(
            jnp.bfloat16
        ),
        "tp",
    ).astype(jnp.float32)
    norm_back_one = jax.vjp(norm_mod, inputs, shift_one, scale_one)[1]
    grad_in_norm, grad_shift_one, grad_scale_one = norm_back_one(grad_normed)
    grad_inputs = grad_middle + grad_in_norm
    grad_mod = jnp.stack(
        [
            grad_shift_one[:, 0],
            grad_scale_one[:, 0],
            grad_gate_one,
            grad_shift_two[:, 0],
            grad_scale_two[:, 0],
            grad_gate_two,
        ],
        axis=1,
    )
    saved = (normed, grad_triple, attended, grad_branch, normed_two, grad_pre, hidden, grad_mlp)
    return (grad_inputs, grad_mod, saved)


def weight_part(saved):
    normed, grad_triple, attended, grad_branch, normed_two, grad_pre, hidden, grad_mlp = saved
    grad_w_qkv = jnp.einsum(
        "bsd,bscn->dcn", normed, grad_triple, preferred_element_type=jnp.float32
    )
    grad_w_out = jnp.einsum(
        "bsn,bsd->nd", attended, grad_branch, preferred_element_type=jnp.float32
    )
    grad_w_up = jnp.einsum("bsd,bsf->df", normed_two, grad_pre, preferred_element_type=jnp.float32)
    grad_w_down = jnp.einsum("bsf,bsd->fd", hidden, grad_mlp, preferred_element_type=jnp.float32)
    return (grad_w_qkv, grad_w_out, grad_w_up, grad_w_down)


def body(latents, cotangent, labels, steps, label_table, w_ada, w_qkv, w_out, w_up, w_down):
    head_dim = HEAD_DIM
    micro_count = MICRO
    batch_size = LAT_MB
    section_no = lax.axis_index("pipe")
    is_first = section_no == 0
    class_ids = jnp.arange(label_table.shape[0], dtype=jnp.int32)
    one_hot = (labels[:, None] == class_ids[None, :]).astype(jnp.float32)
    condition = jnp.dot(
        one_hot.astype(jnp.bfloat16), label_table, preferred_element_type=jnp.float32
    )
    condition = condition + sinus_embed(steps, label_table.shape[1])
    cond_act = jax.nn.silu(condition).astype(jnp.bfloat16)
    mod_piece = jnp.einsum(
        "ld,dkn->lkn", cond_act, w_ada[0], preferred_element_type=jnp.float32
    ).astype(jnp.bfloat16)
    modulations = collect(mod_piece, ("ctx", "tp"), 2).astype(jnp.float32)
    gathered = gather_turned((w_qkv, w_out, w_up, w_down), "ctx", (1, 2, 1, 2))
    weights = tuple((member[0] for member in gathered))
    received = jnp.zeros((batch_size, latents.shape[1], latents.shape[2]), jnp.float32)
    kept_list = []
    outputs = []
    for moment in range(micro_count + 1):
        mb_index = jnp.clip(moment - section_no, 0, micro_count - 1)
        own_rows = lax.dynamic_slice_in_dim(latents, mb_index * batch_size, batch_size, 0)
        mod_rows = lax.dynamic_slice_in_dim(modulations, mb_index * batch_size, batch_size, 0)
        inputs = jnp.where(is_first, own_rows, received)
        result, branch, mlp_out, kv_all = layer_forward(inputs, mod_rows, weights, head_dim)
        kept_list.append((inputs, branch, mlp_out, kv_all))
        outputs.append(result)
        if moment < micro_count:
            received = from_behind(result.astype(jnp.bfloat16), "pipe", 1).astype(result.dtype)
    finals = jnp.concatenate(outputs[1:], axis=0)
    totals = tuple((jnp.zeros(member.shape, jnp.float32) for member in weights))
    mod_total = jnp.zeros(modulations.shape, jnp.float32)
    returned = jnp.zeros_like(received)
    grad_list = []
    for moment in range(micro_count + 1):
        raw_index = moment - 1 + section_no
        in_use = ((raw_index >= 0) & (raw_index < micro_count)).astype(jnp.float32)
        mb_index = jnp.clip(raw_index, 0, micro_count - 1)
        later = kept_list[min(moment + 1, micro_count)]
        earlier = kept_list[max(moment - 1, 0)]
        kept_state = jax.tree.map(
            lambda upper_v, lower_v: jnp.where(is_first, lower_v, upper_v), later, earlier
        )
        own_grad = lax.dynamic_slice_in_dim(cotangent, mb_index * batch_size, batch_size, 0)
        grad_result = jnp.where(is_first, returned, own_grad)
        mod_rows = lax.dynamic_slice_in_dim(modulations, mb_index * batch_size, batch_size, 0)
        grad_inputs, grad_mod, saved = layer_backward(
            kept_state[0],
            kept_state[1],
            kept_state[2],
            kept_state[3],
            grad_result,
            mod_rows,
            weights,
            head_dim,
        )
        current = lax.dynamic_slice_in_dim(mod_total, mb_index * batch_size, batch_size, 0)
        mod_total = lax.dynamic_update_slice_in_dim(
            mod_total, current + in_use * grad_mod, mb_index * batch_size, 0
        )
        grad_list.append(grad_inputs)
        if moment < micro_count:
            returned = from_behind(grad_inputs.astype(jnp.bfloat16), "pipe", -1).astype(
                grad_inputs.dtype
            )
        layer_grads = tuple((in_use * member for member in weight_part(saved)))
        totals = tuple((total_v + piece_v for total_v, piece_v in zip(totals, layer_grads)))
    shards = tuple(
        (
            part.astype(jnp.float32)
            for part in sum_packed(
                (
                    totals[0].astype(jnp.bfloat16),
                    totals[1].astype(jnp.bfloat16),
                    totals[2].astype(jnp.bfloat16),
                    totals[3].astype(jnp.bfloat16),
                ),
                "ctx",
                (0, 1, 0, 1),
            )
        )
    )
    grad_latents = jnp.concatenate(grad_list[1:], axis=0)
    ends = jnp.where(is_first, grad_latents, finals)[None]
    mod_shard = sum_at_owner(mod_total.astype(jnp.bfloat16), "ctx", 2)
    piece_width = w_ada.shape[3]
    mod_grad = lax.dynamic_slice_in_dim(
        mod_shard, lax.axis_index("tp") * piece_width, piece_width, 2
    ).astype(jnp.bfloat16)
    grad_ada = jnp.einsum("ld,lkn->dkn", cond_act, mod_grad, preferred_element_type=jnp.float32)[
        None
    ]
    cond_part = jnp.einsum("lkn,dkn->ld", mod_grad, w_ada[0], preferred_element_type=jnp.float32)
    grad_cond_act = total_of_pieces(cond_part, ("pipe", "ctx", "tp"))
    silu_back = jax.vjp(jax.nn.silu, condition)[1]
    grad_condition = silu_back(grad_cond_act)[0]
    grad_table = jnp.dot(one_hot.T, grad_condition, precision=highest)
    return (
        ends,
        grad_table,
        grad_ada,
        shards[0][None],
        shards[1][None],
        shards[2][None],
        shards[3][None],
    )


def solution(mesh):
    return jax.shard_map(
        body,
        mesh=mesh,
        in_specs=(
            P(None, "ctx", None),
            P(None, "ctx", None),
            P(),
            P(),
            P(),
            P("pipe", None, None, ("ctx", "tp")),
            P("pipe", "ctx", None, "tp"),
            P("pipe", "tp", "ctx"),
            P("pipe", "ctx", "tp"),
            P("pipe", "tp", "ctx"),
        ),
        out_specs=(
            P("pipe", None, "ctx", None),
            P(),
            P("pipe", None, None, ("ctx", "tp")),
            P("pipe", "ctx", None, "tp"),
            P("pipe", "tp", "ctx"),
            P("pipe", "ctx", "tp"),
            P("pipe", "tp", "ctx"),
        ),
        check_vma=False,
    )
```

profile of v0, /device:TPU:1, one launch (start us, length us, event | category | flops | bytes accessed | tf_op | source)
XLA Modules:
  0.0 1216.9 jit_solution(5508308485134033601)
XLA Ops:
  14.5 12.0 all-to-all-start
  27.9 7.6 all-to-all-done
  37.2 52.0 %all-gather.5.cloned.1.call-done = bf16[1024,1536]{0,1:T(8,128)(2,1)} async-done(((bf16[128,1536]{0,1:T(8,128)(2,1)}), bf16[1024,1536]{0,1:T(8,128)(2,1)}) %all-gather.5.cloned.1.call-update) | async-done | bytes 3145744 | tf_op jit(solution)/shard_map/all_gather | solution.py:71
  90.9 22.3 %all_gather.22 = bf16[2,1024,128]{1,2,0:T(8,128)(2,1)S(1)} all-gather(bf16[2,128,128]{1,2,0:T(8,128)(2,1)S(1)} %pad_maximum_fusion.2), channel_id=1, replica_groups=mesh['pipe'=2,'ctx'=8,'tp'=8] {'ctx'}, dimensions={1}, use_global_device_ids=true | all-gather | bytes 589824 | tf_op jit(solution)/shard_map/all_gather | solution.py:21
  117.0 28.1 %all_to_all.110 = bf16[8,1,128,1024]{3,2,1,0:T(8,128)(2,1)S(1)} all-to-all(bf16[8,1,128,1024]{3,2,1,0:T(8,128)(2,1)S(1)} %broadcast_in_dim.71), channel_id=1, replica_groups=mesh['pipe'=2,'ctx'=8,'tp'=8] {'tp'}, dimensions={0} | all-to-all | bytes 4194304 | tf_op jit(solution)/shard_map/all_to_all | solution.py:27
  149.1 24.5 %all_to_all.111 = bf16[8,1,128,1024]{3,2,1,0:T(8,128)(2,1)S(1)} all-to-all(bf16[8,1,128,1024]{3,2,1,0:T(8,128)(2,1)S(1)} %broadcast_in_dim.72), channel_id=1, replica_groups=mesh['pipe'=2,'ctx'=8,'tp'=8] {'tp'}, dimensions={0} | all-to-all | bytes 4194304 | tf_op jit(solution)/shard_map/all_to_all | solution.py:27
  175.5 9.2 collective-permute-done
  187.0 20.8 %all_gather.23 = bf16[2,1024,128]{1,2,0:T(8,128)(2,1)S(1)} all-gather(bf16[2,128,128]{1,2,0:T(8,128)(2,1)S(1)} %pad_maximum_fusion.3), channel_id=1, replica_groups=mesh['pipe'=2,'ctx'=8,'tp'=8] {'ctx'}, dimensions={1}, use_global_device_ids=true | all-gather | bytes 589824 | tf_op jit(solution)/shard_map/all_gather | solution.py:21
  210.9 25.1 %all_to_all.112 = bf16[8,1,128,1024]{3,2,1,0:T(8,128)(2,1)S(1)} all-to-all(bf16[8,1,128,1024]{3,2,1,0:T(8,128)(2,1)S(1)} %broadcast_in_dim.73), channel_id=1, replica_groups=mesh['pipe'=2,'ctx'=8,'tp'=8] {'tp'}, dimensions={0} | all-to-all | bytes 4194304 | tf_op jit(solution)/shard_map/all_to_all | solution.py:27
  239.4 26.1 %all_to_all.113 = bf16[8,1,128,1024]{3,2,1,0:T(8,128)(2,1)S(1)} all-to-all(bf16[8,1,128,1024]{3,2,1,0:T(8,128)(2,1)S(1)} %broadcast_in_dim.80), channel_id=1, replica_groups=mesh['pipe'=2,'ctx'=8,'tp'=8] {'tp'}, dimensions={0} | all-to-all | bytes 4194304 | tf_op jit(solution)/shard_map/all_to_all | solution.py:27
  268.0 7.9 collective-permute-done.2
  278.1 21.7 %all_gather.24 = bf16[2,1024,128]{1,2,0:T(8,128)(2,1)S(1)} all-gather(bf16[2,128,128]{1,2,0:T(8,128)(2,1)S(1)} %pad_maximum_fusion.4), channel_id=1, replica_groups=mesh['pipe'=2,'ctx'=8,'tp'=8] {'ctx'}, dimensions={1}, use_global_device_ids=true | all-gather | bytes 589824 | tf_op jit(solution)/shard_map/all_gather | solution.py:21
  305.4 26.4 %all_to_all.114 = bf16[8,1,128,1024]{3,2,1,0:T(8,128)(2,1)S(1)} all-to-all(bf16[8,1,128,1024]{3,2,1,0:T(8,128)(2,1)S(1)} %broadcast_in_dim.81), channel_id=1, replica_groups=mesh['pipe'=2,'ctx'=8,'tp'=8] {'tp'}, dimensions={0} | all-to-all | bytes 4194304 | tf_op jit(solution)/shard_map/all_to_all | solution.py:27
  335.2 25.9 %all_to_all.115 = bf16[8,1,128,1024]{3,2,1,0:T(8,128)(2,1)S(1)} all-to-all(bf16[8,1,128,1024]{3,2,1,0:T(8,128)(2,1)S(1)} %broadcast_in_dim.88), channel_id=1, replica_groups=mesh['pipe'=2,'ctx'=8,'tp'=8] {'tp'}, dimensions={0} | all-to-all | bytes 4194304 | tf_op jit(solution)/shard_map/all_to_all | solution.py:27
  363.8 7.6 collective-permute-done.4
  375.0 20.9 %all_gather.25 = bf16[2,1024,128]{1,2,0:T(8,128)(2,1)S(1)} all-gather(bf16[2,128,128]{1,2,0:T(8,128)(2,1)S(1)} %pad_maximum_fusion.5), channel_id=1, replica_groups=mesh['pipe'=2,'ctx'=8,'tp'=8] {'ctx'}, dimensions={1}, use_global_device_ids=true | all-gather | bytes 589824 | tf_op jit(solution)/shard_map/all_gather | solution.py:21
  408.6 26.4 %all-to-all-done.13 = bf16[8,1,128,1024]{3,2,1,0:T(8,128)(2,1)} async-done(((bf16[8,1,128,1024]{3,2,1,0:T(8,128)(2,1)}), bf16[8,1,128,1024]{3,2,1,0:T(8,128)(2,1)}, u32[]{:S(2)}, u32[]{:S(2)}) %all-to-all-start.13) | async-done | bytes 2097184 | tf_op jit(solution)/shard_map/all_to_all | solution.py:27
  453.8 24.7 %all-to-all-done.4 = bf16[8,1,128,1024]{3,2,1,0:T(8,128)(2,1)} async-done(((bf16[8,1,128,1024]{3,2,1,0:T(8,128)(2,1)}), bf16[8,1,128,1024]{3,2,1,0:T(8,128)(2,1)}, u32[]{:S(2)}, u32[]{:S(2)}) %all-to-all-start.4) | async-done | bytes 2097184 | tf_op jit(solution)/shard_map/all_to_all | solution.py:27
  512.2 27.0 %all-to-all-done.6 = bf16[8,1,128,1024]{3,2,1,0:T(8,128)(2,1)} async-done(((bf16[8,1,128,1024]{3,2,1,0:T(8,128)(2,1)}), bf16[8,1,128,1024]{3,2,1,0:T(8,128)(2,1)}, u32[]{:S(2)}, u32[]{:S(2)}) %all-to-all-start.6) | async-done | bytes 2097184 | tf_op jit(solution)/shard_map/all_to_all | solution.py:27
  563.2 26.3 %all-to-all-done.9 = bf16[8,1,128,1024]{3,2,1,0:T(8,128)(2,1)} async-done(((bf16[8,1,128,1024]{3,2,1,0:T(8,128)(2,1)}), bf16[8,1,128,1024]{3,2,1,0:T(8,128)(2,1)}, u32[]{:S(2)}, u32[]{:S(2)}) %all-to-all-start.9) | async-done | bytes 2097184 | tf_op jit(solution)/shard_map/all_to_all | solution.py:27
  611.2 5.8 all-to-all-done.10
  633.5 26.0 %all-to-all-done.11 = bf16[8,1,128,1024]{3,2,1,0:T(8,128)(2,1)} async-done(((bf16[8,1,128,1024]{3,2,1,0:T(8,128)(2,1)}), bf16[8,1,128,1024]{3,2,1,0:T(8,128)(2,1)}, u32[]{:S(2)}, u32[]{:S(2)}) %all-to-all-start.11) | async-done | bytes 2097184 | tf_op jit(solution)/shard_map/all_to_all | solution.py:27
  688.8 21.3 %all-to-all-done.14 = bf16[8,1,128,1024]{3,2,1,0:T(8,128)(2,1)} async-done(((bf16[8,1,128,1024]{3,2,1,0:T(8,128)(2,1)}), bf16[8,1,128,1024]{3,2,1,0:T(8,128)(2,1)}, u32[]{:S(2)}, u32[]{:S(2)}) %all-to-all-start.14) | async-done | bytes 2097184 | tf_op jit(solution)/shard_map/all_to_all | solution.py:27
  764.1 8.9 all-to-all-done.20
  800.2 8.4 all-to-all-done.16
  842.8 19.1 %all-to-all-done.17 = bf16[8,1,128,1024]{3,2,1,0:T(8,128)(2,1)} async-done(((bf16[8,1,128,1024]{3,2,1,0:T(8,128)(2,1)}), bf16[8,1,128,1024]{3,2,1,0:T(8,128)(2,1)}, u32[]{:S(2)}, u32[]{:S(2)}) %all-to-all-start.17) | async-done | bytes 2097184 | tf_op jit(solution)/shard_map/all_to_all | solution.py:27
  871.8 7.4 all-to-all-start.18
  881.3 6.6 all-to-all-done.18
  904.9 19.5 %all-to-all-done.19 = bf16[8,1,128,1024]{3,2,1,0:T(8,128)(2,1)} async-done(((bf16[8,1,128,1024]{3,2,1,0:T(8,128)(2,1)}), bf16[8,1,128,1024]{3,2,1,0:T(8,128)(2,1)}, u32[]{:S(2)}, u32[]{:S(2)}) %all-to-all-start.19) | async-done | bytes 2097184 | tf_op jit(solution)/shard_map/all_to_all | solution.py:27
  940.4 7.8 pad_maximum_fusion
  957.4 176.2 %all-gather.7.cloned.1.call-done = f32[128,3,1024]{2,1,0:T(4,128)} async-done(((f32[1,3,1024]{2,1,0:T(4,128)}), f32[128,3,1024]{2,1,0:T(4,128)}) %all-gather.7.cloned.1.call-update) | async-done | bytes 1572880 | tf_op jit(solution)/shard_map/all_gather | solution.py:100
  1139.3 65.3 %reduce-scatter.2.cloned.1.call-done = bf16[1536,128]{1,0:T(8,128)(2,1)} async-done(((bf16[12288,128]{1,0:T(8,128)(2,1)}), bf16[1536,128]{1,0:T(8,128)(2,1)}) %reduce-scatter.2.cloned.1.call-update) | async-done | bytes 393232 | tf_op jit(solution)/shard_map/reduce_scatter | solution.py:91
  (879 shorter events, 384.3 us)
Async XLA Ops:
  7.2 82.0 %all-gather.5.cloned.1.call-start = ((), (), s32[]{:S(2)}) async-start(), calls=%async_computation.23 | async-start | bytes 3538944 | tf_op jit(solution)/shard_map/all_gather | solution.py:71
  14.5 21.0 %all-to-all-start = ((bf16[64,2,144]{2,1,0:T(2,128)(2,1)}), bf16[64,2,144]{2,1,0:T(2,128)(2,1)S(1)}, u32[]{:S(2)}, u32[]{:S(2)}) async-start(bf16[64,2,144]{2,1,0:T(2,128)(2,1)} %reshape.3600), calls=%async_computation | async-start | bytes 131072 | tf_op jit(solution)/shard_map/all_to_all | solution.py:27
  37.2 404.2 %copy-start.164 = (f32[1,1,1024]{2,1,0:T(1,128)}, f32[1,1,1024]{2,1,0:T(1,128)S(1)}, u32[]{:S(2)}) copy-start(f32[1,1,1024]{2,1,0:T(1,128)S(1)} %get-tuple-element.201) | copy-start | bytes 12292
  37.2 404.7 %copy-start.166 = (f32[1,1,1024]{2,1,0:T(1,128)}, f32[1,1,1024]{2,1,0:T(1,128)S(1)}, u32[]{:S(2)}) copy-start(f32[1,1,1024]{2,1,0:T(1,128)S(1)} %get-tuple-element.211) | copy-start | bytes 12292
  37.2 413.4 %copy-start.142 = (f32[1,1,1024]{2,1,0:T(1,128)}, f32[1,1,1024]{2,1,0:T(1,128)S(1)}, u32[]{:S(2)}) copy-start(f32[1,1,1024]{2,1,0:T(1,128)S(1)} %get-tuple-element.200) | copy-start | bytes 12292
  37.2 413.4 %copy-start.162 = (f32[1,1,1024]{2,1,0:T(1,128)}, f32[1,1,1024]{2,1,0:T(1,128)S(1)}, u32[]{:S(2)}) copy-start(f32[1,1,1024]{2,1,0:T(1,128)S(1)} %get-tuple-element.219) | copy-start | bytes 12292
  37.2 445.2 %copy-start.145 = (f32[1,1,1024]{2,1,0:T(1,128)}, f32[1,1,1024]{2,1,0:T(1,128)S(1)}, u32[]{:S(2)}) copy-start(f32[1,1,1024]{2,1,0:T(1,128)S(1)} %get-tuple-element.202) | copy-start | bytes 12292
  174.1 10.7 collective-permute-start
  184.9 265.7 %copy-start.204 = (f32[128]{0:T(128)}, f32[128]{0:T(128)S(1)}, u32[]{:S(2)}) copy-start(f32[128]{0:T(128)S(1)} %broadcast_multiply_fusion.11) | copy-start | bytes 1540
  185.3 265.3 %copy-start.243 = (f32[128]{0:T(128)}, f32[128]{0:T(128)S(1)}, u32[]{:S(2)}) copy-start(f32[128]{0:T(128)S(1)} %get-tuple-element.258) | copy-start | bytes 1540
  266.7 9.2 collective-permute-start.2
  362.5 8.9 collective-permute-start.4
  404.2 30.9 %all-to-all-start.13 = ((bf16[8,1,128,1024]{3,2,1,0:T(8,128)(2,1)}), bf16[8,1,128,1024]{3,2,1,0:T(8,128)(2,1)}, u32[]{:S(2)}, u32[]{:S(2)}) async-start(bf16[8,1,128,1024]{3,2,1,0:T(8,128)(2,1)} %broadcast_in_dim.89), calls=%async_computation.13 | async-start | bytes 4194304 | tf_op jit(solution)/shard_map/all_to_all | solution.py:27
  445.8 32.7 %all-to-all-start.4 = ((bf16[8,1,128,1024]{3,2,1,0:T(8,128)(2,1)}), bf16[8,1,128,1024]{3,2,1,0:T(8,128)(2,1)}, u32[]{:S(2)}, u32[]{:S(2)}) async-start(bf16[8,1,128,1024]{3,2,1,0:T(8,128)(2,1)} %broadcast_in_dim.74), calls=%async_computation.4 | async-start | bytes 4194304 | tf_op jit(solution)/shard_map/all_to_all | solution.py:27
  490.0 11.3 all-to-all-start.5
  505.9 33.4 %all-to-all-start.6 = ((bf16[8,1,128,1024]{3,2,1,0:T(8,128)(2,1)}), bf16[8,1,128,1024]{3,2,1,0:T(8,128)(2,1)}, u32[]{:S(2)}, u32[]{:S(2)}) async-start(bf16[8,1,128,1024]{3,2,1,0:T(8,128)(2,1)} %broadcast_in_dim.77), calls=%async_computation.6 | async-start | bytes 4194304 | tf_op jit(solution)/shard_map/all_to_all | solution.py:27
  543.7 5.6 collective-permute-start.1
  553.9 35.6 %all-to-all-start.9 = ((bf16[8,1,128,1024]{3,2,1,0:T(8,128)(2,1)}), bf16[8,1,128,1024]{3,2,1,0:T(8,128)(2,1)}, u32[]{:S(2)}, u32[]{:S(2)}) async-start(bf16[8,1,128,1024]{3,2,1,0:T(8,128)(2,1)} %broadcast_in_dim.82), calls=%async_computation.9 | async-start | bytes 4194304 | tf_op jit(solution)/shard_map/all_to_all | solution.py:27
  604.0 13.0 %all-to-all-start.10 = ((bf16[8,2,128,128]{2,3,1,0:T(8,128)(2,1)}), bf16[8,2,128,128]{2,3,1,0:T(8,128)(2,1)}, u32[]{:S(2)}, u32[]{:S(2)}) async-start(bf16[8,2,128,128]{2,3,1,0:T(8,128)(2,1)} %maximum_bitcast_fusion.1), calls=%async_computation.10 | async-start | bytes 1048576 | tf_op jit(solution)/shard_map/all_to_all | solution.py:44
  625.7 33.8 %all-to-all-start.11 = ((bf16[8,1,128,1024]{3,2,1,0:T(8,128)(2,1)}), bf16[8,1,128,1024]{3,2,1,0:T(8,128)(2,1)}, u32[]{:S(2)}, u32[]{:S(2)}) async-start(bf16[8,1,128,1024]{3,2,1,0:T(8,128)(2,1)} %broadcast_in_dim.85), calls=%async_computation.11 | async-start | bytes 4194304 | tf_op jit(solution)/shard_map/all_to_all | solution.py:27
  664.8 5.1 collective-permute-start.3
  674.6 35.6 %all-to-all-start.14 = ((bf16[8,1,128,1024]{3,2,1,0:T(8,128)(2,1)}), bf16[8,1,128,1024]{3,2,1,0:T(8,128)(2,1)}, u32[]{:S(2)}, u32[]{:S(2)}) async-start(bf16[8,1,128,1024]{3,2,1,0:T(8,128)(2,1)} %broadcast_in_dim.90), calls=%async_computation.14 | async-start | bytes 4194304 | tf_op jit(solution)/shard_map/all_to_all | solution.py:27
  724.7 12.8 %all-to-all-start.15 = ((bf16[8,2,128,128]{2,3,1,0:T(8,128)(2,1)}), bf16[8,2,128,128]{2,3,1,0:T(8,128)(2,1)}, u32[]{:S(2)}, u32[]{:S(2)}) async-start(bf16[8,2,128,128]{2,3,1,0:T(8,128)(2,1)} %maximum_bitcast_fusion.2), calls=%async_computation.15 | async-start | bytes 1048576 | tf_op jit(solution)/shard_map/all_to_all | solution.py:44
  740.0 33.0 %all-to-all-start.20 = ((bf16[8,1,128,1024]{3,2,1,0:T(8,128)(2,1)}), bf16[8,1,128,1024]{3,2,1,0:T(8,128)(2,1)}, u32[]{:S(2)}, u32[]{:S(2)}) async-start(bf16[8,1,128,1024]{3,2,1,0:T(8,128)(2,1)} %broadcast_in_dim.102), calls=%async_computation.20 | async-start | bytes 4194304 | tf_op jit(solution)/shard_map/all_to_all | solution.py:27
  775.5 33.1 %all-to-all-start.16 = ((bf16[8,1,128,1024]{3,2,1,0:T(8,128)(2,1)}), bf16[8,1,128,1024]{3,2,1,0:T(8,128)(2,1)}, u32[]{:S(2)}, u32[]{:S(2)}) async-start(bf16[8,1,128,1024]{3,2,1,0:T(8,128)(2,1)} %broadcast_in_dim.93), calls=%async_computation.16 | async-start | bytes 4194304 | tf_op jit(solution)/shard_map/all_to_all | solution.py:27
  814.0 6.1 collective-permute-start.5
  825.4 36.5 %all-to-all-start.17 = ((bf16[8,1,128,1024]{3,2,1,0:T(8,128)(2,1)}), bf16[8,1,128,1024]{3,2,1,0:T(8,128)(2,1)}, u32[]{:S(2)}, u32[]{:S(2)}) async-start(bf16[8,1,128,1024]{3,2,1,0:T(8,128)(2,1)} %broadcast_in_dim.96), calls=%async_computation.17 | async-start | bytes 4194304 | tf_op jit(solution)/shard_map/all_to_all | solution.py:27
  871.8 16.1 %all-to-all-start.18 = ((bf16[8,2,128,128]{2,3,1,0:T(8,128)(2,1)}), bf16[8,2,128,128]{2,3,1,0:T(8,128)(2,1)S(1)}, u32[]{:S(2)}, u32[]{:S(2)}) async-start(bf16[8,2,128,128]{2,3,1,0:T(8,128)(2,1)} %maximum_bitcast_fusion.3), calls=%async_computation.18 | async-start | bytes 1048576 | tf_op jit(solution)/shard_map/all_to_all | solution.py:44
  890.1 34.3 %all-to-all-start.19 = ((bf16[8,1,128,1024]{3,2,1,0:T(8,128)(2,1)}), bf16[8,1,128,1024]{3,2,1,0:T(8,128)(2,1)}, u32[]{:S(2)}, u32[]{:S(2)}) async-start(bf16[8,1,128,1024]{3,2,1,0:T(8,128)(2,1)} %broadcast_in_dim.99), calls=%async_computation.19 | async-start | bytes 4194304 | tf_op jit(solution)/shard_map/all_to_all | solution.py:27
  928.5 10.0 all-to-all-start.21
  933.4 200.1 %all-gather.7.cloned.1.call-start = ((), (), s32[]{:S(2)}) async-start(), calls=%async_computation.25 | async-start | bytes 2113536 | tf_op jit(solution)/shard_map/all_gather | solution.py:100
  940.4 264.3 %reduce-scatter.2.cloned.1.call-start = ((), (), s32[]{:S(2)}) async-start(), calls=%async_computation.24 | async-start | bytes 3538944 | tf_op jit(solution)/shard_map/reduce_scatter | solution.py:91
  (248 other events, 2409.2 us)
Sparse Core Ops, SparseCore 0:
  11.3 77.9 all-gather.4
  940.5 192.9 all-gather.6
  1135.9 68.6 reduce-scatter.1
where the time goes:
time: 1230 us; the launch traced here: 1220 us
  waiting for transfers between devices  556 us (45%)
  blocking collectives  242 us (20%)
  matrix products  133 us (11%)
  starting transfers between devices  100 us (8%)
  other arithmetic  97.1 us (8%)
  local copies, waits for them, and re-layouts  70.6 us (6%)
  between operations  18 us (1%)
    all_to_all x11, waiting for transfers between devices, sent_to_all(): lax.all_to_all(jnp.broadcast_to(array[None], (size, *array.shape)), axis,...  215 us
    all_gather x1, waiting for transfers between devices, total_of_pieces(): pieces = lax.all_gather(array, axis)  176 us
    all_to_all x6, blocking collectives, sent_to_all(): lax.all_to_all(jnp.broadcast_to(array[None], (size, *array.shape)), axis,...  156 us
    all_gather x4, blocking collectives, in_one_piece(): out = lax.all_gather(both, axis, axis=dim, tiled=True)  85.7 us
    reduce_scatter x1, waiting for transfers between devices, sum_packed(): lax.psum_scatter(lines, axis, tiled=True).reshape(-1)  65.3 us
    all_to_all x11, starting transfers between devices, sent_to_all(): lax.all_to_all(jnp.broadcast_to(array[None], (size, *array.shape)), axis,...  57.7 us
    all_gather x1, waiting for transfers between devices, gather_turned(): out, at, outs = (lax.all_gather(both, axis, axis=0, tiled=True), 0, [])  52 us
    unnamed x533, local copies, waits for them, and re-layouts  31.6 us
  transfers between devices with their start and end apart: 25, of which 24 were waited for; matrix products, arithmetic and copies ran while one was open for 11% of the time, Pallas kernels for 0%

commit v1 on v0

v1 whole, which is shorter than its diff:
```python
import functools
import math

import jax
import jax.numpy as jnp
from jax import lax
from jax.experimental import pallas as pl
from jax.experimental.pallas import tpu as pltpu
from jax.sharding import PartitionSpec as P


LAT = 3
HEAD = 64
EPS = 1e-06
GELU_C = math.sqrt(2.0 / math.pi)
GELU_A = 0.044715

f32 = jnp.float32
bf16 = jnp.bfloat16


def sds(shape, dtype):
    return jax.ShapeDtypeStruct(shape, dtype)


def call(kernel, outs, *args):
    vmem = pl.BlockSpec(memory_space=pltpu.VMEM)
    return pl.pallas_call(
        kernel,
        out_shape=tuple(sds(*o) for o in outs),
        in_specs=[
            pl.BlockSpec(memory_space=pltpu.SMEM) if a.dtype == jnp.int32 else vmem for a in args
        ],
        out_specs=tuple(vmem for _ in outs),
        compiler_params=pltpu.CompilerParams(vmem_limit_bytes=48 * 1024 * 1024),
    )(*args)


def mm(a, b):
    return lax.dot_general(a, b, (((1,), (0,)), ((), ())), preferred_element_type=f32)


def mm_nt(a, b):
    return lax.dot_general(a, b, (((1,), (1,)), ((), ())), preferred_element_type=f32)


def mm_tn(a, b):
    return lax.dot_general(a, b, (((0,), (0,)), ((), ())), preferred_element_type=f32)


def part(mod, k):
    return jnp.concatenate(
        [jnp.broadcast_to(mod[3 * k + l : 3 * k + l + 1, :], (8, mod.shape[1])) for l in range(LAT)],
        axis=0,
    )


def centred(x):
    c = x - jnp.mean(x, axis=-1, keepdims=True)
    r = lax.rsqrt(jnp.mean(c * c, axis=-1, keepdims=True) + EPS)
    return c * r, r


def norm_back(x, dy, scale):
    xh, r = centred(x)
    g = dy * (1.0 + scale)
    dx = r * (
        g - jnp.mean(g, axis=-1, keepdims=True) - xh * jnp.mean(g * xh, axis=-1, keepdims=True)
    )
    return dx, dy, dy * xh


def row_sums(ref, at, v):
    for l in range(LAT):
        ref[3 * at + l : 3 * at + l + 1, :] = jnp.sum(v[8 * l : 8 * l + 8, :], axis=0, keepdims=True)


def summed(ref, *at):
    total = ref[(0, *at)].astype(f32)
    for j in range(1, 8):
        total = total + ref[(j, *at)].astype(f32)
    return total


def to_all(ref, v):
    for j in range(8):
        ref[j] = v


def by_latent(v):
    v = v.reshape(8, LAT, 8, v.shape[-1])
    return [v[:, l].reshape(64, v.shape[-1]) for l in range(LAT)]


def by_part(vs):
    w = vs[0].shape[-1]
    return jnp.stack([v.reshape(8, 8, w) for v in vs], axis=1).reshape(192, w)


def gelu_parts(x):
    t = jnp.tanh(GELU_C * (x + GELU_A * (x * x * x)))
    return t


def k_norm_first(x_ref, mod_ref, o_ref):
    mod = mod_ref[...].astype(f32)
    shift, scale = part(mod, 0), 1.0 + part(mod, 1)
    for j in range(8):
        xh, _ = centred(x_ref[j])
        o_ref[j] = (xh * scale + shift).astype(bf16)


def k_qkv(n_ref, w_ref, q_ref, kv_ref):
    y = mm(n_ref[...], w_ref[:, :384])
    for l, v in enumerate(by_latent(y)):
        q_ref[l] = v[:, :128].astype(bf16)
        kv_ref[l] = v[:, 128:].astype(bf16)


def head_rows(v):
    lane = lax.broadcasted_iota(jnp.int32, v.shape, 1)
    zero = jnp.zeros_like(v)
    return jnp.concatenate(
        [jnp.where(lane < HEAD, v, zero), jnp.where(lane < HEAD, zero, v)], axis=0
    )


def head_lanes(v):
    lane = lax.broadcasted_iota(jnp.int32, (64, 128), 1)
    return jnp.where(lane < HEAD, v[:64], v[64:])


def keys_values(a_ref, b_ref, l):
    kv = jnp.concatenate([a_ref[c, l] for c in range(8)] + [b_ref[c, l] for c in range(8)], axis=0)
    return kv[:, :128], kv[:, 128:]


def soft(qs, k):
    s = mm_nt(qs, k) * 0.125
    e = jnp.exp(s - jnp.max(s, axis=-1, keepdims=True))
    return e / jnp.sum(e, axis=-1, keepdims=True)


def k_attn(q_ref, a_ref, b_ref, w_ref, att_ref, o_ref):
    outs = []
    for l in range(LAT):
        k, v = keys_values(a_ref, b_ref, l)
        probs = soft(head_rows(q_ref[l].astype(f32)).astype(bf16), k)
        outs.append(head_lanes(mm(probs.astype(bf16), v)))
    att = by_part(outs).astype(bf16)
    att_ref[...] = att
    o_ref[...] = mm_nt(att, w_ref[:, 384:]).astype(bf16)


def k_attn_back(q_ref, a_ref, b_ref, w_ref, db_ref, dq_ref, da_ref, dp_ref):
    datt = by_latent(mm(db_ref[...], w_ref[:, 384:]))
    for l in range(LAT):
        k, v = keys_values(a_ref, b_ref, l)
        qs = head_rows(q_ref[l].astype(f32)).astype(bf16)
        do = head_rows(datt[l]).astype(bf16)
        probs = soft(qs, k)
        dprobs = mm_nt(do, v)
        dv = mm_tn(probs.astype(bf16), do)
        ds = probs * (dprobs - jnp.sum(probs * dprobs, axis=-1, keepdims=True))
        ds = ds.astype(bf16)
        dk = mm_tn(ds, qs) * 0.125
        dq_ref[l] = (head_lanes(mm(ds, k)) * 0.125).astype(bf16)
        dkv = jnp.concatenate([dk, dv], axis=1).astype(bf16)
        for c in range(8):
            da_ref[c, l] = dkv[64 * c : 64 * c + 64]
            dp_ref[c, l] = dkv[512 + 64 * c : 512 + 64 * c + 64]


def k_pair_sum(a_ref, b_ref, o_ref):
    o_ref[...] = (a_ref[...].astype(f32) + b_ref[...].astype(f32)).astype(bf16)


def k_qkv_back(dq_ref, r_ref, w_ref, dt_ref, o_ref):
    rows = []
    for l in range(LAT):
        dkv = summed(r_ref, l)
        rows.append(jnp.concatenate([dq_ref[l].astype(f32), dkv], axis=1))
    dt = by_part(rows).astype(bf16)
    dt_ref[...] = dt
    o_ref[...] = mm_nt(dt, w_ref[:, :384]).astype(bf16)


def k_mid(r_ref, x_ref, mod_ref, br_ref, mid_ref, o_ref):
    mod = mod_ref[...].astype(f32)
    branch = summed(r_ref)
    mid = x_ref[...] + part(mod, 2) * branch
    br_ref[...] = branch
    mid_ref[...] = mid
    xh, _ = centred(mid)
    to_all(o_ref, (xh * (1.0 + part(mod, 4)) + part(mod, 3)).astype(bf16))


def k_mlp(n_ref, w_ref, pre_ref, hid_ref, o_ref):
    pre = mm(n_ref[...], w_ref[:, :512])
    pre_ref[...] = pre
    hid = (0.5 * pre * (1.0 + gelu_parts(pre))).astype(bf16)
    hid_ref[...] = hid
    o_ref[...] = mm_nt(hid, w_ref[:, 512:]).astype(bf16)


def gelu_slope(pre, t):
    inner = GELU_C * (1.0 + 3.0 * GELU_A * pre * pre)
    return 0.5 * (1.0 + t) + 0.5 * pre * (1.0 - t * t) * inner


def k_mlp_both(n_ref, w_ref, dm_ref, hid_ref, dpre_ref, o_ref):
    pre = mm(n_ref[...], w_ref[:, :512])
    t = gelu_parts(pre)
    hid = (0.5 * pre * (1.0 + t)).astype(bf16)
    hid_ref[...] = hid
    out = mm_nt(hid, w_ref[:, 512:]).astype(bf16)
    dhid = mm(dm_ref[...], w_ref[:, 512:])
    dpre = (dhid * gelu_slope(pre, t)).astype(bf16)
    dpre_ref[...] = dpre
    back = mm_nt(dpre, w_ref[:, :512]).astype(bf16)
    for j in range(8):
        o_ref[j, 0] = out[24 * j : 24 * j + 24]
        o_ref[j, 1] = back[24 * j : 24 * j + 24]


def k_mlp_back(pre_ref, w_ref, dm_ref, dpre_ref, o_ref):
    pre = pre_ref[...]
    dhid = mm(dm_ref[...], w_ref[:, 512:])
    dpre = (dhid * gelu_slope(pre, gelu_parts(pre))).astype(bf16)
    dpre_ref[...] = dpre
    o_ref[...] = mm_nt(dpre, w_ref[:, :512]).astype(bf16)


def k_gate_rows(c_ref, mod_ref, o_ref):
    gate = part(mod_ref[...].astype(f32), 5)
    for j in range(8):
        o_ref[j] = (gate * c_ref[j]).astype(bf16)


def k_next(r_ref, mid_ref, mod_ref, mod_next_ref, mlp_ref, x_ref, o_ref):
    mod, mod_next = mod_ref[...].astype(f32), mod_next_ref[...].astype(f32)
    mlp = summed(r_ref)
    mlp_ref[...] = mlp
    x = mid_ref[...] + part(mod, 5) * mlp
    x_ref[...] = x
    xh, _ = centred(x)
    to_all(o_ref, (xh * (1.0 + part(mod_next, 1)) + part(mod_next, 0)).astype(bf16))


def back_two(mod, mid, branch, dy, dn, mlp, dmid_ref, dmod_ref, o_ref):
    dx, ds, dc = norm_back(mid, dn, part(mod, 4))
    dmid = dy + dx
    dmid_ref[...] = dmid
    row_sums(dmod_ref, 0, dmid * branch)
    row_sums(dmod_ref, 1, ds)
    row_sums(dmod_ref, 2, dc)
    row_sums(dmod_ref, 3, dy * mlp)
    to_all(o_ref, (part(mod, 2) * dmid).astype(bf16))


def k_last(r_ref, mid_ref, br_ref, dy_ref, mod_ref, res_ref, dmid_ref, dmod_ref, o_ref):
    mod = mod_ref[...].astype(f32)
    mlp, dn = summed(r_ref, 0), summed(r_ref, 1)
    mid = mid_ref[...]
    res_ref[...] = (mid + part(mod, 5) * mlp).astype(bf16)
    back_two(mod, mid, br_ref[...], dy_ref[...], dn, mlp, dmid_ref, dmod_ref, o_ref)


def k_back_two(r_ref, mid_ref, br_ref, dy_ref, mlp_ref, mod_ref, dmid_ref, dmod_ref, o_ref):
    mod = mod_ref[...].astype(f32)
    back_two(
        mod, mid_ref[...], br_ref[...], dy_ref[...], summed(r_ref), mlp_ref[...],
        dmid_ref, dmod_ref, o_ref,
    )


def k_back_one(r_ref, x_ref, dmid_ref, mod_ref, mod_before_ref, dx_ref, dmod_ref, o_ref):
    dx, ds, dc = norm_back(x_ref[...], summed(r_ref), part(mod_ref[...].astype(f32), 1))
    dx = dmid_ref[...] + dx
    dx_ref[...] = dx
    row_sums(dmod_ref, 0, ds)
    row_sums(dmod_ref, 1, dc)
    to_all(o_ref, (part(mod_before_ref[...].astype(f32), 5) * dx).astype(bf16))


def k_back_first(r_ref, x_ref, dmid_ref, mod_ref, dx_ref, dmod_ref):
    dx, ds, dc = norm_back(x_ref[...], summed(r_ref), part(mod_ref[...].astype(f32), 1))
    dx_ref[...] = (dmid_ref[...] + dx).astype(bf16)
    row_sums(dmod_ref, 0, ds)
    row_sums(dmod_ref, 1, dc)


def k_grad_mlp(p_ref, n_ref, dpre_ref, dm_ref, hid_ref, keep_ref, send_ref):
    def put(up_ref, down_ref):
        up_ref[...] = mm_tn(n_ref[...], dpre_ref[...]).astype(bf16)
        down_ref[...] = mm_tn(dm_ref[...], hid_ref[...]).astype(bf16)

    @pl.when(p_ref[0] == 0)
    def _():
        put(keep_ref, send_ref)

    @pl.when(p_ref[0] == 1)
    def _():
        put(send_ref, keep_ref)


def k_grad_attn(p_ref, n_ref, dt_ref, db_ref, att_ref, keep_ref, send_ref):
    def put(a_ref, b_ref):
        a_ref[...] = mm_tn(n_ref[...], dt_ref[:, :256]).astype(bf16)
        b_ref[:, :128] = mm_tn(n_ref[...], dt_ref[:, 256:]).astype(bf16)
        b_ref[:, 128:] = mm_tn(db_ref[...], att_ref[...]).astype(bf16)

    @pl.when(p_ref[0] == 0)
    def _():
        put(keep_ref, send_ref)

    @pl.when(p_ref[0] == 1)
    def _():
        put(send_ref, keep_ref)


def exchange(x, axis):
    return lax.all_to_all(x, axis, 0, 0, tiled=True)


def swap(x):
    return lax.ppermute(x, "pipe", [(0, 1), (1, 0)])


def copies(x, n):
    return jnp.broadcast_to(x[None], (n, *x.shape))


def body(latents, cotangent, labels, steps, label_table, w_ada, w_qkv, w_out, w_up, w_down):
    p, t = lax.axis_index("pipe"), lax.axis_index("tp")
    first = p == 0
    who = p.astype(jnp.int32).reshape(1)
    width = latents.shape[2]

    def of_layer(own, other):
        return jnp.where(first, own, other), jnp.where(first, other, own)

    w_attn = jnp.concatenate([w_qkv[0].reshape(128, 384), w_out[0].T], axis=1)
    w_mlp = jnp.concatenate([w_up[0], w_down[0].T], axis=1)
    w_mlp = lax.all_gather(w_mlp, "ctx", axis=0, tiled=True)
    w_attn = exchange(copies(w_attn, 8), "ctx").reshape(1024, 512)
    wa = of_layer(w_attn, swap(w_attn))

    rows = [lax.dynamic_slice_in_dim(label_table, labels[l], 1, 0) for l in range(LAT)]
    half = width // 2
    freq = jnp.exp(-math.log(10000.0) * jnp.arange(half, dtype=f32) / half)
    angles = steps.astype(f32)[:, None] * freq[None, :]
    condition = jnp.concatenate(rows, axis=0).astype(f32) + jnp.concatenate(
        [jnp.cos(angles), jnp.sin(angles)], axis=1
    )
    cond_act = jax.nn.silu(condition).astype(bf16)
    ada = w_ada[0].transpose(1, 2, 0)
    mod_piece = jnp.einsum("ld,knd->kln", cond_act, ada, preferred_element_type=f32)
    mod_piece = mod_piece.astype(bf16).reshape(18, 16)
    placed = lax.dynamic_update_slice(jnp.zeros((18, 128), bf16), mod_piece, (0, 16 * t))
    placed = exchange(copies(placed, 64), ("ctx", "tp")).reshape(8, 8, 18, 128)
    mod_own = placed.astype(f32).sum(axis=1).transpose(1, 0, 2).reshape(18, 1024).astype(bf16)
    mods = of_layer(mod_own, swap(mod_own))

    def own_rows(a):
        a = lax.dynamic_slice_in_dim(a, 64 * p, 64, 1)
        a = a.reshape(LAT, 8, 8, width).transpose(1, 0, 2, 3).reshape(8, 24, width)
        return a, lax.dynamic_index_in_dim(a, t, 0, keepdims=False)

    x_all, x0 = own_rows(latents)
    cot_all, cot = own_rows(cotangent)

    bc = ((8, 24, 1024), bf16)
    rows24 = ((24, 1024), f32)
    wide = ((192, 1024), bf16)
    kv_shape = ((8, LAT, 64, 256), bf16)

    def attn_forward(normed, w):
        q, kv = call(k_qkv, [((LAT, 64, 128), bf16), ((LAT, 64, 256), bf16)], normed, w)
        kv_a = exchange(copies(kv, 8), "ctx")
        kv_b = swap(kv_a)
        att, branch = call(k_attn, [((192, 128), bf16), wide], q, kv_a, kv_b, w)
        return (q, kv_a, kv_b, att), exchange(branch.reshape(8, 24, 1024), "tp")

    def attn_back(kept, normed, dbranch, w):
        q, kv_a, kv_b, att = kept
        dq, da, dp = call(
            k_attn_back, [((LAT, 64, 128), bf16), kv_shape, kv_shape], q, kv_a, kv_b, w, dbranch
        )
        (both,) = call(k_pair_sum, [kv_shape], da, swap(dp))
        arrived = exchange(both, "ctx")
        dt, dn = call(k_qkv_back, [((192, 384), bf16), wide], dq, arrived, w)
        halves = call(
            k_grad_attn, [((1024, 256), bf16)] * 2, who, normed, dt, dbranch, att
        )
        return exchange(dn.reshape(8, 24, 1024), "tp"), halves

    def grads_mlp(n, dpre, dm, hid):
        return call(k_grad_mlp, [((1024, 512), bf16)] * 2, who, n, dpre, dm, hid)

    def to_rows(x):
        return exchange(x, "tp").reshape(192, 1024)

    (normed0,) = call(k_norm_first, [bc], x_all, mods[0])
    normed0 = normed0.reshape(192, 1024)
    kept0, arrived = attn_forward(normed0, wa[0])
    br0, mid0, n2 = call(k_mid, [rows24, rows24, bc], arrived, x0, mods[0])
    n2_0 = to_rows(n2)
    wm = of_layer(w_mlp, swap(w_mlp))
    pre0, hid0, out = call(
        k_mlp, [((192, 512), f32), ((192, 512), bf16), wide], n2_0, wm[0]
    )
    arrived = exchange(out.reshape(8, 24, 1024), "tp")
    mlp0, x1, n1 = call(k_next, [rows24, rows24, bc], arrived, mid0, mods[0], mods[1])

    normed1 = to_rows(n1)
    kept1, arrived = attn_forward(normed1, wa[1])
    br1, mid1, n2 = call(k_mid, [rows24, rows24, bc], arrived, x1, mods[1])
    n2_1 = to_rows(n2)
    (dm1,) = call(k_gate_rows, [bc], cot_all, mods[1])
    dm1 = dm1.reshape(192, 1024)
    hid1, dpre1, both = call(
        k_mlp_both,
        [((192, 512), bf16), ((192, 512), bf16), ((8, 2, 24, 1024), bf16)],
        n2_1, wm[1], dm1,
    )
    arrived = exchange(both, "tp")
    res1, dmid1, dmod1a, db = call(
        k_last,
        [((24, 1024), bf16), rows24, ((12, 1024), f32), bc],
        arrived, mid1, br1, cot, mods[1],
    )
    keep, send = grads_mlp(n2_1, dpre1, dm1, hid1)
    gm1 = lax.psum_scatter(call(k_pair_sum, [((1024, 512), bf16)], keep, swap(send))[0], "ctx", tiled=True)

    db1 = to_rows(db)
    arrived, halves1 = attn_back(kept1, normed1, db1, wa[1])
    dx1, dmod1b, dm = call(
        k_back_one, [rows24, ((6, 1024), f32), bc], arrived, x1, dmid1, mods[1], mods[0]
    )
    dm0 = to_rows(dm)

    dpre0, dn = call(k_mlp_back, [((192, 512), bf16), wide], pre0, wm[0], dm0)
    arrived = exchange(dn.reshape(8, 24, 1024), "tp")
    dmid0, dmod0a, db = call(
        k_back_two, [rows24, ((12, 1024), f32), bc], arrived, mid0, br0, dx1, mlp0, mods[0]
    )
    keep, send = grads_mlp(n2_0, dpre0, dm0, hid0)
    gm0 = call(k_pair_sum, [((1024, 512), bf16)], keep, swap(send))[0]
    ga1 = call(k_pair_sum, [((1024, 256), bf16)], halves1[0], swap(halves1[1]))[0]
    mixed = lax.psum_scatter(jnp.concatenate([gm0, ga1], axis=1), "ctx", tiled=True)
    gm0, ga1 = mixed[:, :512], mixed[:, 512:]

    db0 = to_rows(db)
    arrived, halves0 = attn_back(kept0, normed0, db0, wa[0])
    dx0, dmod0b = call(
        k_back_first, [((24, 1024), bf16), ((6, 1024), f32)], arrived, x0, dmid0, mods[0]
    )

    def stacked(a, b):
        return jnp.concatenate([b, a], axis=0)

    dmod_own, dmod_other = of_layer(stacked(dmod0a, dmod0b), stacked(dmod1a, dmod1b))
    dmod = (dmod_own + swap(dmod_other)).astype(bf16)
    dmod = dmod.reshape(18, 8, 128).transpose(1, 0, 2)
    dmod = jnp.broadcast_to(dmod[:, None], (8, 8, 18, 128)).reshape(64, 18, 128)
    dmod = exchange(dmod, ("ctx", "tp")).astype(f32).sum(axis=0)
    dmod = lax.dynamic_slice_in_dim(dmod, 16 * t, 16, 1).astype(bf16).reshape(6, 3, 16)
    grad_ada = jnp.einsum("kln,ld->knd", dmod, cond_act, preferred_element_type=f32)
    cond_part = jnp.einsum("kln,knd->ld", dmod, ada, preferred_element_type=f32)
    cond_part = (cond_part + swap(cond_part)).reshape(24, 128)
    grad_act = exchange(copies(cond_part, 64), ("ctx", "tp")).sum(axis=0).reshape(LAT, width)
    sig = jax.nn.sigmoid(condition)
    grad_cond = grad_act * (sig * (1.0 + condition * (1.0 - sig)))
    classes = jnp.arange(label_table.shape[0], dtype=jnp.int32)[:, None]
    grad_table = sum(
        jnp.where(classes == labels[l], grad_cond[l : l + 1], 0.0) for l in range(LAT)
    )

    ga0 = call(k_pair_sum, [((1024, 256), bf16)], halves0[0], swap(halves0[1]))[0]
    ga0 = exchange(ga0.reshape(8, 128, 256), "ctx").astype(f32).sum(axis=0).astype(bf16)

    mine = jnp.concatenate([jnp.where(first, gm0, gm1), jnp.where(first, ga0, ga1)], axis=1)
    send = jnp.concatenate([jnp.where(first, gm1, gm0), jnp.where(first, ga1, ga0)], axis=1)
    half0, half1 = of_layer(mine, swap(send))
    grad_up = half0[:, :512].astype(f32)
    grad_down = half1[:, :512].astype(f32).T
    grad_qkv = jnp.concatenate([half0[:, 512:], half1[:, 512:640]], axis=1).astype(f32)
    grad_out = half1[:, 640:].astype(f32).T

    mine = jnp.where(first, dx0, res1)
    other = swap(jnp.where(first, res1, dx0))
    pair = jnp.stack(of_layer(mine, other))
    ends = exchange(copies(pair, 8), "tp").reshape(8, 2, LAT, 8, width)
    ends = ends.transpose(2, 1, 0, 3, 4).reshape(LAT, 128, width).astype(f32)

    return (
        ends[None],
        grad_table,
        grad_ada.transpose(2, 0, 1)[None],
        grad_qkv.reshape(1, 128, 3, 128),
        grad_out[None],
        grad_up[None],
        grad_down[None],
    )


def solution(mesh):
    return jax.shard_map(
        body,
        mesh=mesh,
        in_specs=(
            P(None, "ctx", None),
            P(None, "ctx", None),
            P(),
            P(),
            P(),
            P("pipe", None, None, ("ctx", "tp")),
            P("pipe", "ctx", None, "tp"),
            P("pipe", "tp", "ctx"),
            P("pipe", "ctx", "tp"),
            P("pipe", "tp", "ctx"),
        ),
        out_specs=(
            P("pipe", None, "ctx", None),
            P(),
            P("pipe", None, None, ("ctx", "tp")),
            P("pipe", "ctx", None, "tp"),
            P("pipe", "tp", "ctx"),
            P("pipe", "ctx", "tp"),
            P("pipe", "tp", "ctx"),
        ),
        check_vma=False,
    )
```

time: 1230 us -> 489 us (0.40)
  waiting for transfers between devices: 556 us -> 109 us
  matrix products: 133 us -> 1.54 us
  blocking collectives: 242 us -> 157 us
  other arithmetic: 97.1 us -> 19.3 us
  Pallas kernels: 0 us -> 30.3 us
  local copies, waits for them, and re-layouts: 70.6 us -> 49.6 us
    all_gather x2 -> x1, waiting for transfers between devices: 228 us -> 3.16 us  [body(): w_mlp = lax.all_gather(w_mlp, 'ctx', axis=0, tiled=True)]
    all_to_all x16 -> x11, waiting for transfers between devices: 237 us -> 88.4 us  [exchange(): return lax.all_to_all(x, axis, 0, 0, tiled=True)]
    dot_general x77 -> x3, matrix products: 107 us -> 1.54 us  [the longest x1 1 us: body(): jnp.einsum('kln,ld->knd', dmod, cond_act, preferred_element_type=f32)]
    all_gather x4 -> x0, blocking collectives: 85.7 us -> none  [in_one_piece(): out = lax.all_gather(both, axis, axis=dim, tiled=True)]
    reduce_sum x63 -> x4, other arithmetic: 63 us -> 1.32 us  [the longest x1 1.1 us: body(): dmod = exchange(dmod, ('ctx', 'tp')).astype(f32).sum(axis=0)]
    reduce_scatter x1 -> x2, waiting for transfers between devices: 65.3 us -> 9.69 us  [the longest x1 9.67 us: body(): lax.psum_scatter(call(k_pair_sum, [((1024, 512), bf16)], keep, swap(send)...]
    pallas_call x0 -> x30, Pallas kernels: none -> 30.3 us  [call(): pl.pallas_call(kernel, out_shape=tuple((sds(*o) for o in outs)), in_specs...]
    all_to_all x16 -> x11, starting transfers between devices: 83.2 us -> 63.4 us  [exchange(): return lax.all_to_all(x, axis, 0, 0, tiled=True)]
  transfers between devices with their start and end apart: 25 -> 29, of which waited for: 24 -> 18; matrix products, arithmetic and copies ran while one was open for 11% -> 7% of each run, Pallas kernels for 0% -> 4%
where the time goes in v1:
time: 489 us; the launch traced here: 486 us
  blocking collectives  157 us (32%)
  waiting for transfers between devices  109 us (22%)
  starting transfers between devices  99.3 us (20%)
  local copies, waits for them, and re-layouts  49.6 us (10%)
  Pallas kernels  30.3 us (6%)
  between operations  20.5 us (4%)
  other arithmetic  19.3 us (4%)
    all_to_all x12, blocking collectives, exchange(): return lax.all_to_all(x, axis, 0, 0, tiled=True)  157 us
    all_to_all x11, waiting for transfers between devices, exchange(): return lax.all_to_all(x, axis, 0, 0, tiled=True)  88.4 us
    all_to_all x11, starting transfers between devices, exchange(): return lax.all_to_all(x, axis, 0, 0, tiled=True)  63.4 us
    ppermute x15, starting transfers between devices, swap(): return lax.ppermute(x, 'pipe', [(0, 1), (1, 0)])  35.8 us
    unnamed x204, local copies, waits for them, and re-layouts  35.5 us
    pallas_call x30, Pallas kernels, call(): pl.pallas_call(kernel, out_shape=tuple((sds(*o) for o in outs)), in_specs...  30.3 us
  transfers between devices with their start and end apart: 29, of which 18 were waited for; matrix products, arithmetic and copies ran while one was open for 7% of the time, Pallas kernels for 4%

profile of v1, /device:TPU:1, one launch (start us, length us, event | category | flops | bytes accessed | tf_op | source)
XLA Modules:
  0.0 486.0 jit_solution(14866797357564978555)
XLA Ops:
  12.9 6.2 %all-to-all-start.1 = ((bf16[8,128,512]{2,1,0:T(8,128)(2,1)}), bf16[8,128,512]{2,1,0:T(8,128)(2,1)S(1)}, u32[]{:S(2)}, u32[]{:S(2)}) async-start(bf16[8,128,512]{2,1,0:T(8,128)(2,1)} %broadcast_in_dim.124), calls=%async_computation.1 | async-start | bytes 2097152 | tf_op jit(solution)/shard_map/all_to_all | solution.py:323
  25.5 10.4 %all-to-all-done.1 = bf16[8,128,512]{2,1,0:T(8,128)(2,1)S(1)} async-done(((bf16[8,128,512]{2,1,0:T(8,128)(2,1)}), bf16[8,128,512]{2,1,0:T(8,128)(2,1)S(1)}, u32[]{:S(2)}, u32[]{:S(2)}) %all-to-all-start.1) | async-done | bytes 1048608 | tf_op jit(solution)/shard_map/all_to_all | solution.py:323
  42.0 13.7 %all-to-all-start = ((bf16[64,18,128]{2,1,0:T(8,128)(2,1)}), bf16[64,18,128]{2,1,0:T(8,128)(2,1)S(1)}, u32[]{:S(2)}, u32[]{:S(2)}) async-start(bf16[64,18,128]{2,1,0:T(8,128)(2,1)} %broadcast_in_dim.123), calls=%async_computation | async-start | bytes 786432 | tf_op jit(solution)/shard_map/all_to_all | solution.py:323
  55.8 13.2 %all-to-all-done = bf16[64,18,128]{2,1,0:T(8,128)(2,1)S(1)} async-done(((bf16[64,18,128]{2,1,0:T(8,128)(2,1)}), bf16[64,18,128]{2,1,0:T(8,128)(2,1)S(1)}, u32[]{:S(2)}, u32[]{:S(2)}) %all-to-all-start) | async-done | bytes 294944 | tf_op jit(solution)/shard_map/all_to_all | solution.py:323
  81.3 17.7 %all_to_all.115.a_ref = bf16[8,3,64,256]{3,2,1,0:T(8,128)(2,1)S(1)} all-to-all(bf16[8,3,64,256]{3,2,1,0:T(8,128)(2,1)S(1)} %broadcast_in_dim.125), channel_id=1, replica_groups=mesh['pipe'=2,'ctx'=8,'tp'=8] {'ctx'}, dimensions={0} | all-to-all | bytes 1572864 | tf_op jit(solution)/shard_map/all_to_all | solution.py:323
  106.2 6.0 %all-to-all-start.3 = ((bf16[8,24,1024]{2,1,0:T(8,128)(2,1)}), bf16[8,24,1024]{2,1,0:T(8,128)(2,1)S(1)}, u32[]{:S(2)}, u32[]{:S(2)}) async-start(bf16[8,24,1024]{2,1,0:T(8,128)(2,1)} %bitcast.128), calls=%async_computation.3 | async-start | bytes 786432 | tf_op jit(solution)/shard_map/all_to_all | solution.py:323
  113.7 7.6 %all-to-all-done.3.r_ref = bf16[8,24,1024]{2,1,0:T(8,128)(2,1)S(1)} async-done(((bf16[8,24,1024]{2,1,0:T(8,128)(2,1)}), bf16[8,24,1024]{2,1,0:T(8,128)(2,1)S(1)}, u32[]{:S(2)}, u32[]{:S(2)}) %all-to-all-start.3) | async-done | bytes 393248 | tf_op jit(solution)/shard_map/all_to_all | solution.py:323
  128.0 4.5 broadcast_select_fusion
  138.3 11.3 %all_to_all.116.r_ref = bf16[8,24,1024]{2,1,0:T(8,128)(2,1)S(1)} all-to-all(bf16[8,24,1024]{2,1,0:T(8,128)(2,1)S(1)} %bitcast.131), channel_id=1, replica_groups=mesh['pipe'=2,'ctx'=8,'tp'=8] {'tp'}, dimensions={0} | all-to-all | bytes 786432 | tf_op jit(solution)/shard_map/all_to_all | solution.py:323
  149.9 10.9 %all_to_all.117 = bf16[8,24,1024]{2,1,0:T(8,128)(2,1)S(1)} all-to-all(bf16[8,24,1024]{2,1,0:T(8,128)(2,1)S(1)} %get-tuple-element.69), channel_id=1, replica_groups=mesh['pipe'=2,'ctx'=8,'tp'=8] {'tp'}, dimensions={0} | all-to-all | bytes 786432 | tf_op jit(solution)/shard_map/all_to_all | solution.py:323
  161.7 11.1 %all_to_all.118.a_ref = bf16[8,3,64,256]{3,2,1,0:T(8,128)(2,1)S(1)} all-to-all(bf16[8,3,64,256]{3,2,1,0:T(8,128)(2,1)S(1)} %broadcast_in_dim.126), channel_id=1, replica_groups=mesh['pipe'=2,'ctx'=8,'tp'=8] {'ctx'}, dimensions={0} | all-to-all | bytes 1572864 | tf_op jit(solution)/shard_map/all_to_all | solution.py:323
  172.7 6.2 %collective-permute-start.4 = (bf16[8,3,64,256]{3,2,1,0:T(8,128)(2,1)S(1)}, bf16[8,3,64,256]{3,2,1,0:T(8,128)(2,1)S(1)}, u32[]{:S(2)}, u32[]{:S(2)}) collective-permute-start(bf16[8,3,64,256]{3,2,1,0:T(8,128)(2,1)S(1)} %all_to_all.118.a_ref), channel_id=1, source_target_pairs={{0,64},{64,0},{1,65},{65,1},{2,66},{66,2},{3,67},{67,3},{4,68},{68... | collective-permute-start | bytes 2359304 | tf_op jit(solution)/shard_map/ppermute | solution.py:327
  183.5 11.6 %all_to_all.119.r_ref = bf16[8,24,1024]{2,1,0:T(8,128)(2,1)S(1)} all-to-all(bf16[8,24,1024]{2,1,0:T(8,128)(2,1)S(1)} %bitcast.132), channel_id=1, replica_groups=mesh['pipe'=2,'ctx'=8,'tp'=8] {'tp'}, dimensions={0} | all-to-all | bytes 786432 | tf_op jit(solution)/shard_map/all_to_all | solution.py:323
  215.0 4.4 all-to-all-start.10
  220.3 9.0 %all-to-all-done.10.r_ref = bf16[8,2,24,1024]{3,2,1,0:T(8,128)(2,1)} async-done(((bf16[8,2,24,1024]{3,2,1,0:T(8,128)(2,1)}), bf16[8,2,24,1024]{3,2,1,0:T(8,128)(2,1)}, u32[]{:S(2)}, u32[]{:S(2)}) %all-to-all-start.10) | async-done | bytes 786464 | tf_op jit(solution)/shard_map/all_to_all | solution.py:323
  233.5 14.2 %all_to_all.120 = bf16[8,24,1024]{2,1,0:T(8,128)(2,1)S(1)} all-to-all(bf16[8,24,1024]{2,1,0:T(8,128)(2,1)S(1)} %get-tuple-element.78), channel_id=1, replica_groups=mesh['pipe'=2,'ctx'=8,'tp'=8] {'tp'}, dimensions={0} | all-to-all | bytes 786432 | tf_op jit(solution)/shard_map/all_to_all | solution.py:323
  256.6 14.2 %all_to_all.121.r_ref = bf16[8,3,64,256]{3,2,1,0:T(8,128)(2,1)S(1)} all-to-all(bf16[8,3,64,256]{3,2,1,0:T(8,128)(2,1)S(1)} %shard_map.166), channel_id=1, replica_groups=mesh['pipe'=2,'ctx'=8,'tp'=8] {'ctx'}, dimensions={0} | all-to-all | bytes 1572864 | tf_op jit(solution)/shard_map/all_to_all | solution.py:323
  271.3 11.3 %all_to_all.122.r_ref = bf16[8,24,1024]{2,1,0:T(8,128)(2,1)S(1)} all-to-all(bf16[8,24,1024]{2,1,0:T(8,128)(2,1)S(1)} %bitcast.129), channel_id=1, replica_groups=mesh['pipe'=2,'ctx'=8,'tp'=8] {'tp'}, dimensions={0} | all-to-all | bytes 786432 | tf_op jit(solution)/shard_map/all_to_all | solution.py:323
  282.9 10.6 %all_to_all.123 = bf16[8,24,1024]{2,1,0:T(8,128)(2,1)S(1)} all-to-all(bf16[8,24,1024]{2,1,0:T(8,128)(2,1)S(1)} %get-tuple-element.84), channel_id=1, replica_groups=mesh['pipe'=2,'ctx'=8,'tp'=8] {'tp'}, dimensions={0} | all-to-all | bytes 786432 | tf_op jit(solution)/shard_map/all_to_all | solution.py:323
  297.2 4.9 %collective-permute-start.10 = (bf16[1024,512]{1,0:T(8,128)(2,1)}, bf16[1024,512]{1,0:T(8,128)(2,1)}, u32[]{:S(2)}, u32[]{:S(2)}) collective-permute-start(bf16[1024,512]{1,0:T(8,128)(2,1)} %get-tuple-element.104), channel_id=1, source_target_pairs={{0,64},{64,0},{1,65},{65,1},{2,66},{66,2},{3,67},{67,3},{4,68},{68... | collective-permute-start | bytes 3145736 | tf_op jit(solution)/shard_map/ppermute | solution.py:327
  308.8 6.2 %all-to-all-done.15.r_ref = bf16[8,24,1024]{2,1,0:T(8,128)(2,1)S(1)} async-done(((bf16[8,24,1024]{2,1,0:T(8,128)(2,1)}), bf16[8,24,1024]{2,1,0:T(8,128)(2,1)S(1)}, u32[]{:S(2)}, u32[]{:S(2)}) %all-to-all-start.15) | async-done | bytes 393248 | tf_op jit(solution)/shard_map/all_to_all | solution.py:323
  318.9 11.7 %all_to_all.124 = bf16[8,24,1024]{2,1,0:T(8,128)(2,1)S(1)} all-to-all(bf16[8,24,1024]{2,1,0:T(8,128)(2,1)S(1)} %get-tuple-element.89), channel_id=1, replica_groups=mesh['pipe'=2,'ctx'=8,'tp'=8] {'tp'}, dimensions={0} | all-to-all | bytes 786432 | tf_op jit(solution)/shard_map/all_to_all | solution.py:323
  343.5 17.6 %all_to_all.125.r_ref = bf16[8,3,64,256]{3,2,1,0:T(8,128)(2,1)S(1)} all-to-all(bf16[8,3,64,256]{3,2,1,0:T(8,128)(2,1)S(1)} %shard_map.172), channel_id=1, replica_groups=mesh['pipe'=2,'ctx'=8,'tp'=8] {'ctx'}, dimensions={0} | all-to-all | bytes 1572864 | tf_op jit(solution)/shard_map/all_to_all | solution.py:323
  361.6 14.5 %all_to_all.126.r_ref = bf16[8,24,1024]{2,1,0:T(8,128)(2,1)S(1)} all-to-all(bf16[8,24,1024]{2,1,0:T(8,128)(2,1)S(1)} %bitcast.130), channel_id=1, replica_groups=mesh['pipe'=2,'ctx'=8,'tp'=8] {'tp'}, dimensions={0} | all-to-all | bytes 786432 | tf_op jit(solution)/shard_map/all_to_all | solution.py:323
  383.3 8.0 %all-to-all-start.20 = ((bf16[64,18,128]{2,1,0:T(8,128)(2,1)}), bf16[64,18,128]{2,1,0:T(8,128)(2,1)}, u32[]{:S(2)}, u32[]{:S(2)}) async-start(bf16[64,18,128]{2,1,0:T(8,128)(2,1)} %bitcast.135), calls=%async_computation.20 | async-start | bytes 786432 | tf_op jit(solution)/shard_map/all_to_all | solution.py:323
  392.3 10.5 %all-to-all-done.20 = bf16[64,18,128]{2,1,0:T(8,128)(2,1)} async-done(((bf16[64,18,128]{2,1,0:T(8,128)(2,1)}), bf16[64,18,128]{2,1,0:T(8,128)(2,1)}, u32[]{:S(2)}, u32[]{:S(2)}) %all-to-all-start.20) | async-done | bytes 294944 | tf_op jit(solution)/shard_map/all_to_all | solution.py:323
  408.6 6.2 %all-to-all-done.22 = bf16[8,128,256]{2,1,0:T(8,128)(2,1)S(1)} async-done(((bf16[8,128,256]{2,1,0:T(8,128)(2,1)}), bf16[8,128,256]{2,1,0:T(8,128)(2,1)S(1)}, u32[]{:S(2)}, u32[]{:S(2)}) %all-to-all-start.22) | async-done | bytes 524320 | tf_op jit(solution)/shard_map/all_to_all | solution.py:323
  424.9 6.5 %all-to-all-done.19 = bf16[8,2,24,1024]{3,2,1,0:T(8,128)(2,1)S(1)} async-done(((bf16[8,2,24,1024]{3,2,1,0:T(8,128)(2,1)}), bf16[8,2,24,1024]{3,2,1,0:T(8,128)(2,1)S(1)}, u32[]{:S(2)}, u32[]{:S(2)}) %all-to-all-start.19) | async-done | bytes 786464 | tf_op jit(solution)/shard_map/all_to_all | solution.py:323
  432.3 7.6 %all-to-all-start.21 = ((f32[64,24,128]{2,1,0:T(8,128)}), f32[64,24,128]{2,1,0:T(8,128)S(1)}, u32[]{:S(2)}, u32[]{:S(2)}) async-start(f32[64,24,128]{2,1,0:T(8,128)} %broadcast_in_dim.131), calls=%async_computation.21 | async-start | bytes 1572864 | tf_op jit(solution)/shard_map/all_to_all | solution.py:323
  444.4 11.6 %all-to-all-done.21 = f32[64,24,128]{2,1,0:T(8,128)S(1)} async-done(((f32[64,24,128]{2,1,0:T(8,128)}), f32[64,24,128]{2,1,0:T(8,128)S(1)}, u32[]{:S(2)}, u32[]{:S(2)}) %all-to-all-start.21) | async-done | bytes 786464 | tf_op jit(solution)/shard_map/all_to_all | solution.py:323
  457.0 9.7 %reduce-scatter.5.cloned.1.call-done = bf16[128,512]{1,0:T(8,128)(2,1)} async-done(((bf16[1024,512]{1,0:T(8,128)(2,1)}), bf16[128,512]{1,0:T(8,128)(2,1)}) %reduce-scatter.5.cloned.1.call-update) | async-done | bytes 131088 | tf_op jit(solution)/shard_map/reduce_scatter | solution.py:434
  467.6 6.0 %collective-permute-start.14 = (bf16[128,768]{1,0:T(8,128)(2,1)S(1)}, bf16[128,768]{1,0:T(8,128)(2,1)S(1)}, u32[]{:S(2)}, u32[]{:S(2)}) collective-permute-start(bf16[128,768]{1,0:T(8,128)(2,1)S(1)} %pad_maximum_fusion.3), channel_id=1, source_target_pairs={{0,64},{64,0},{1,65},{65,1},{2,66},{66,2},{3,67},{67,3},{4,68},{68... | collective-permute-start | bytes 589832 | tf_op jit(solution)/shard_map/ppermute | solution.py:327
  (339 shorter events, 150.5 us)
Async XLA Ops:
  7.2 70.5 %all-gather.2.cloned.1.call-start = ((), (), s32[]{:S(2)}) async-start(), calls=%async_computation.25 | async-start | bytes 2359296 | tf_op jit(solution)/shard_map/all_gather | solution.py:345
  12.9 23.0 %all-to-all-start.1 = ((bf16[8,128,512]{2,1,0:T(8,128)(2,1)}), bf16[8,128,512]{2,1,0:T(8,128)(2,1)S(1)}, u32[]{:S(2)}, u32[]{:S(2)}) async-start(bf16[8,128,512]{2,1,0:T(8,128)(2,1)} %broadcast_in_dim.124), calls=%async_computation.1 | async-start | bytes 2097152 | tf_op jit(solution)/shard_map/all_to_all | solution.py:323
  35.9 36.7 %copy-start.83 = (bf16[8,128,512]{2,1,0:T(8,128)(2,1)}, bf16[8,128,512]{2,1,0:T(8,128)(2,1)S(1)}, u32[]{:S(2)}) copy-start(bf16[8,128,512]{2,1,0:T(8,128)(2,1)S(1)} %all-to-all-done.1) | copy-start | bytes 3145732
  35.9 43.3 %collective-permute-start.1 = (bf16[1024,512]{1,0:T(8,128)(2,1)S(1)}, bf16[1024,512]{1,0:T(8,128)(2,1)}, u32[]{:S(2)}, u32[]{:S(2)}) collective-permute-start(bf16[1024,512]{1,0:T(8,128)(2,1)S(1)} %bitcast.133), channel_id=1, source_target_pairs={{0,64},{64,0},{1,65},{65,1},{2,66},{66,2},{3,67},{67,3},{4,68},{68... | collective-permute-start | bytes 3145736 | tf_op jit(solution)/shard_map/ppermute | solution.py:327
  42.0 27.0 %all-to-all-start = ((bf16[64,18,128]{2,1,0:T(8,128)(2,1)}), bf16[64,18,128]{2,1,0:T(8,128)(2,1)S(1)}, u32[]{:S(2)}, u32[]{:S(2)}) async-start(bf16[64,18,128]{2,1,0:T(8,128)(2,1)} %broadcast_in_dim.123), calls=%async_computation | async-start | bytes 786432 | tf_op jit(solution)/shard_map/all_to_all | solution.py:323
  69.1 3.6 collective-permute-start
  77.7 50.3 %collective-permute-start.3 = (bf16[1024,1024]{1,0:T(8,128)(2,1)}, bf16[1024,1024]{1,0:T(8,128)(2,1)}, u32[]{:S(2)}, u32[]{:S(2)}) collective-permute-start(bf16[1024,1024]{1,0:T(8,128)(2,1)} %all-gather.2.cloned.1.call-done), channel_id=1, source_target_pairs={{0,64},{64,0},{1,65},{65,1},{2,66},{66,2},{3,67},{67,3},{4,68},{68... | collective-permute-start | bytes 6291464 | tf_op jit(solution)/shard_map/ppermute | solution.py:327
  99.1 3.1 collective-permute-start.2
  106.2 15.2 %all-to-all-start.3 = ((bf16[8,24,1024]{2,1,0:T(8,128)(2,1)}), bf16[8,24,1024]{2,1,0:T(8,128)(2,1)S(1)}, u32[]{:S(2)}, u32[]{:S(2)}) async-start(bf16[8,24,1024]{2,1,0:T(8,128)(2,1)} %bitcast.128), calls=%async_computation.3 | async-start | bytes 786432 | tf_op jit(solution)/shard_map/all_to_all | solution.py:323
  124.5 11.2 %all-to-all-start.4 = ((bf16[8,24,1024]{2,1,0:T(8,128)(2,1)}), bf16[8,24,1024]{2,1,0:T(8,128)(2,1)S(1)}, u32[]{:S(2)}, u32[]{:S(2)}) async-start(bf16[8,24,1024]{2,1,0:T(8,128)(2,1)} %copy-done.43), calls=%async_computation.4 | async-start | bytes 786432 | tf_op jit(solution)/shard_map/all_to_all | solution.py:323
  149.9 45.1 %copy-start.47 = (f32[24,1024]{1,0:T(8,128)}, f32[24,1024]{1,0:T(8,128)S(1)}, u32[]{:S(2)}) copy-start(f32[24,1024]{1,0:T(8,128)S(1)} %get-tuple-element.73.x_ref) | copy-start | bytes 294916
  172.7 8.1 %collective-permute-start.4 = (bf16[8,3,64,256]{3,2,1,0:T(8,128)(2,1)S(1)}, bf16[8,3,64,256]{3,2,1,0:T(8,128)(2,1)S(1)}, u32[]{:S(2)}, u32[]{:S(2)}) collective-permute-start(bf16[8,3,64,256]{3,2,1,0:T(8,128)(2,1)S(1)} %all_to_all.118.a_ref), channel_id=1, source_target_pairs={{0,64},{64,0},{1,65},{65,1},{2,66},{66,2},{3,67},{67,3},{4,68},{68... | collective-permute-start | bytes 2359304 | tf_op jit(solution)/shard_map/ppermute | solution.py:327
  197.3 11.2 %all-to-all-start.9 = ((bf16[8,24,1024]{2,1,0:T(8,128)(2,1)}), bf16[8,24,1024]{2,1,0:T(8,128)(2,1)S(1)}, u32[]{:S(2)}, u32[]{:S(2)}) async-start(bf16[8,24,1024]{2,1,0:T(8,128)(2,1)} %copy-done.44), calls=%async_computation.9 | async-start | bytes 786432 | tf_op jit(solution)/shard_map/all_to_all | solution.py:323
  215.0 14.3 %all-to-all-start.10 = ((bf16[8,2,24,1024]{3,2,1,0:T(8,128)(2,1)}), bf16[8,2,24,1024]{3,2,1,0:T(8,128)(2,1)}, u32[]{:S(2)}, u32[]{:S(2)}) async-start(bf16[8,2,24,1024]{3,2,1,0:T(8,128)(2,1)} %copy-done.31), calls=%async_computation.10 | async-start | bytes 1572864 | tf_op jit(solution)/shard_map/all_to_all | solution.py:323
  251.0 5.4 %collective-permute-start.5 = (bf16[8,3,64,256]{3,2,1,0:T(8,128)(2,1)S(1)}, bf16[8,3,64,256]{3,2,1,0:T(8,128)(2,1)S(1)}, u32[]{:S(2)}, u32[]{:S(2)}) collective-permute-start(bf16[8,3,64,256]{3,2,1,0:T(8,128)(2,1)S(1)} %get-tuple-element.81), channel_id=1, source_target_pairs={{0,64},{64,0},{1,65},{65,1},{2,66},{66,2},{3,67},{67,3},{4,68},{68... | collective-permute-start | bytes 2359304 | tf_op jit(solution)/shard_map/ppermute | solution.py:327
  297.2 42.1 %collective-permute-start.10 = (bf16[1024,512]{1,0:T(8,128)(2,1)}, bf16[1024,512]{1,0:T(8,128)(2,1)}, u32[]{:S(2)}, u32[]{:S(2)}) collective-permute-start(bf16[1024,512]{1,0:T(8,128)(2,1)} %get-tuple-element.104), channel_id=1, source_target_pairs={{0,64},{64,0},{1,65},{65,1},{2,66},{66,2},{3,67},{67,3},{4,68},{68... | collective-permute-start | bytes 3145736 | tf_op jit(solution)/shard_map/ppermute | solution.py:327
  302.1 12.9 %all-to-all-start.15 = ((bf16[8,24,1024]{2,1,0:T(8,128)(2,1)}), bf16[8,24,1024]{2,1,0:T(8,128)(2,1)S(1)}, u32[]{:S(2)}, u32[]{:S(2)}) async-start(bf16[8,24,1024]{2,1,0:T(8,128)(2,1)} %bitcast.127), calls=%async_computation.15 | async-start | bytes 786432 | tf_op jit(solution)/shard_map/all_to_all | solution.py:323
  305.6 150.5 %reduce-scatter.3.cloned.1.call-start = ((), (), s32[]{:S(2)}) async-start(), calls=%async_computation.26 | async-start | bytes 1769472 | tf_op jit(solution)/shard_map/reduce_scatter | solution.py:451
  308.8 29.4 %collective-permute-start.11 = (bf16[1024,256]{1,0:T(8,128)(2,1)}, bf16[1024,256]{1,0:T(8,128)(2,1)}, u32[]{:S(2)}, u32[]{:S(2)}) collective-permute-start(bf16[1024,256]{1,0:T(8,128)(2,1)} %get-tuple-element.108), channel_id=1, source_target_pairs={{0,64},{64,0},{1,65},{65,1},{2,66},{66,2},{3,67},{67,3},{4,68},{68... | collective-permute-start | bytes 1572872 | tf_op jit(solution)/shard_map/ppermute | solution.py:327
  318.9 57.5 %copy-start.51 = (f32[12,1024]{1,0:T(8,128)}, f32[12,1024]{1,0:T(8,128)S(1)}, u32[]{:S(2)}) copy-start(f32[12,1024]{1,0:T(8,128)S(1)} %get-tuple-element.98) | copy-start | bytes 147460
  335.7 6.4 %collective-permute-start.6 = (bf16[8,3,64,256]{3,2,1,0:T(8,128)(2,1)}, bf16[8,3,64,256]{3,2,1,0:T(8,128)(2,1)}, u32[]{:S(2)}, u32[]{:S(2)}) collective-permute-start(bf16[8,3,64,256]{3,2,1,0:T(8,128)(2,1)} %get-tuple-element.92), channel_id=1, source_target_pairs={{0,64},{64,0},{1,65},{65,1},{2,66},{66,2},{3,67},{67,3},{4,68},{68... | collective-permute-start | bytes 2359304 | tf_op jit(solution)/shard_map/ppermute | solution.py:327
  376.4 6.0 %collective-permute-start.8 = (f32[18,1024]{1,0:T(8,128)S(1)}, f32[18,1024]{1,0:T(8,128)S(1)}, u32[]{:S(2)}, u32[]{:S(2)}) collective-permute-start(f32[18,1024]{1,0:T(8,128)S(1)} %fusion.4), channel_id=1, source_target_pairs={{0,64},{64,0},{1,65},{65,1},{2,66},{66,2},{3,67},{67,3},{4,68},{68... | collective-permute-start | bytes 221192 | tf_op jit(solution)/shard_map/ppermute | solution.py:327
  379.6 39.8 %collective-permute-start.12 = (bf16[1024,512]{1,0:T(8,128)(2,1)}, bf16[1024,512]{1,0:T(8,128)(2,1)S(1)}, u32[]{:S(2)}, u32[]{:S(2)}) collective-permute-start(bf16[1024,512]{1,0:T(8,128)(2,1)} %get-tuple-element.112), channel_id=1, source_target_pairs={{0,64},{64,0},{1,65},{65,1},{2,66},{66,2},{3,67},{67,3},{4,68},{68... | collective-permute-start | bytes 3145736 | tf_op jit(solution)/shard_map/ppermute | solution.py:327
  381.9 9.4 %collective-permute-start.13 = (bf16[1024,256]{1,0:T(8,128)(2,1)}, bf16[1024,256]{1,0:T(8,128)(2,1)S(1)}, u32[]{:S(2)}, u32[]{:S(2)}) collective-permute-start(bf16[1024,256]{1,0:T(8,128)(2,1)} %get-tuple-element.116), channel_id=1, source_target_pairs={{0,64},{64,0},{1,65},{65,1},{2,66},{66,2},{3,67},{67,3},{4,68},{68... | collective-permute-start | bytes 1572872 | tf_op jit(solution)/shard_map/ppermute | solution.py:327
  383.3 19.5 %all-to-all-start.20 = ((bf16[64,18,128]{2,1,0:T(8,128)(2,1)}), bf16[64,18,128]{2,1,0:T(8,128)(2,1)}, u32[]{:S(2)}, u32[]{:S(2)}) async-start(bf16[64,18,128]{2,1,0:T(8,128)(2,1)} %bitcast.135), calls=%async_computation.20 | async-start | bytes 786432 | tf_op jit(solution)/shard_map/all_to_all | solution.py:323
  402.8 12.0 %all-to-all-start.22 = ((bf16[8,128,256]{2,1,0:T(8,128)(2,1)}), bf16[8,128,256]{2,1,0:T(8,128)(2,1)S(1)}, u32[]{:S(2)}, u32[]{:S(2)}) async-start(bf16[8,128,256]{2,1,0:T(8,128)(2,1)} %bitcast.53), calls=%async_computation.24 | async-start | bytes 1048576 | tf_op jit(solution)/shard_map/all_to_all | solution.py:323
  406.3 2.2 collective-permute-start.7
  415.8 15.5 %all-to-all-start.19 = ((bf16[8,2,24,1024]{3,2,1,0:T(8,128)(2,1)}), bf16[8,2,24,1024]{3,2,1,0:T(8,128)(2,1)S(1)}, u32[]{:S(2)}, u32[]{:S(2)}) async-start(bf16[8,2,24,1024]{3,2,1,0:T(8,128)(2,1)} %broadcast_in_dim.127), calls=%async_computation.19 | async-start | bytes 1572864 | tf_op jit(solution)/shard_map/all_to_all | solution.py:323
  419.4 47.2 %reduce-scatter.5.cloned.1.call-start = ((), (), s32[]{:S(2)}) async-start(), calls=%async_computation.27 | async-start | bytes 1179648 | tf_op jit(solution)/shard_map/reduce_scatter | solution.py:434
  422.2 2.7 collective-permute-start.9
  432.3 23.6 %all-to-all-start.21 = ((f32[64,24,128]{2,1,0:T(8,128)}), f32[64,24,128]{2,1,0:T(8,128)S(1)}, u32[]{:S(2)}, u32[]{:S(2)}) async-start(f32[64,24,128]{2,1,0:T(8,128)} %broadcast_in_dim.131), calls=%async_computation.21 | async-start | bytes 1572864 | tf_op jit(solution)/shard_map/all_to_all | solution.py:323
  467.6 8.4 %collective-permute-start.14 = (bf16[128,768]{1,0:T(8,128)(2,1)S(1)}, bf16[128,768]{1,0:T(8,128)(2,1)S(1)}, u32[]{:S(2)}, u32[]{:S(2)}) collective-permute-start(bf16[128,768]{1,0:T(8,128)(2,1)S(1)} %pad_maximum_fusion.3), channel_id=1, source_target_pairs={{0,64},{64,0},{1,65},{65,1},{2,66},{66,2},{3,67},{67,3},{4,68},{68... | collective-permute-start | bytes 589832 | tf_op jit(solution)/shard_map/ppermute | solution.py:327
  (95 other events, 961.2 us)
Sparse Core Ops, SparseCore 0:
  10.2 67.3 all-gather.1
  342.2 49.6 reduce-scatter.2
  422.6 43.9 reduce-scatter.4

commit v2 on v1

v2 whole, which is shorter than its diff:
```python
import math

import jax
import jax.numpy as jnp
from jax import lax
from jax.experimental import pallas as pl
from jax.experimental.pallas import tpu as pltpu
from jax.sharding import PartitionSpec as P


LAT = 3
HEAD = 64
EPS = 1e-06
GELU_C = math.sqrt(2.0 / math.pi)
GELU_A = 0.044715
STORE_ROWS = 34048

f32 = jnp.float32
bf16 = jnp.bfloat16


def sds(shape, dtype):
    return jax.ShapeDtypeStruct(shape, dtype)


def up16(n):
    return -(-n // 16) * 16


class Slot:
    def __init__(self, row, shape, dtype):
        self.row, self.shape, self.dtype = row, shape, dtype
        self.rows = up16(shape[0]) * (2 if dtype == f32 else 1)

    def of(self, ref):
        return ref.at[pl.ds(self.row, self.rows), pl.ds(0, self.shape[1])]


class Store:
    def __init__(self):
        self.array, self.next = None, 0

    def slot(self, shape, dtype):
        s = Slot(self.next, shape, dtype)
        self.next += s.rows
        assert self.next <= STORE_ROWS
        return s


class Save:
    def __init__(self, array, slot):
        self.array, self.slot = array, slot


class Near:
    def __init__(self, array):
        self.array = array


class Half:
    def __init__(self, core, own, other, block, rows, at, width, slot):
        self.core, self.own, self.other = core, own, other
        self.block, self.rows, self.at, self.width, self.slot = block, rows, at, width, slot


class Held:
    def __init__(self, ref, wait, shape, dtype):
        self.ref, self.wait, self.shape, self.dtype = ref, wait, shape, dtype

    def ready(self):
        if self.wait is not None:
            self.wait()
            self.wait = None

    def __getitem__(self, at):
        self.ready()
        if self.dtype != f32 or self.ref.dtype == f32:
            return self.ref[at]
        n = self.shape[0]
        low = up16(n)
        return self.ref[:n].astype(f32) + self.ref[low : low + n].astype(f32)


class Kept:
    def __init__(self, ref, copy, shape, dtype):
        self.ref, self.copy, self.shape, self.dtype, self.gone = ref, copy, shape, dtype, False

    def send(self):
        if not self.gone:
            self.copy.start()
            self.gone = True

    def __setitem__(self, at, v):
        if self.dtype == f32:
            n = self.shape[0]
            low = up16(n)
            high = v.astype(bf16)
            self.ref[:n] = high
            self.ref[low : low + n] = (v - high.astype(f32)).astype(bf16)
            self.send()
        else:
            self.ref[at] = v
            if at is Ellipsis:
                self.send()


def ready(*refs):
    for r in refs:
        if isinstance(r, Held):
            r.ready()


def call(store, kernel, outs, *args):
    vmem = pl.BlockSpec(memory_space=pltpu.VMEM)
    smem = pl.BlockSpec(memory_space=pltpu.SMEM)
    far = pl.BlockSpec(memory_space=pltpu.HBM)
    uses = any(isinstance(a, (Slot, Save, Half)) for a in args) or any(
        isinstance(o, Slot) for o in outs
    )
    flat, in_specs, plan, scratch = [], [], [], []

    def hold(shape, dtype):
        scratch.append(pltpu.VMEM(shape, dtype))
        return len(scratch) - 1

    for a in args:
        if isinstance(a, Slot):
            plan.append(("slot", a, hold((a.rows, a.shape[1]), bf16)))
        elif isinstance(a, Near):
            plan.append(("near", len(flat), hold(a.array.shape, a.array.dtype)))
            flat.append(a.array)
            in_specs.append(far)
        elif isinstance(a, Half):
            plan.append(("half", len(flat), hold(a.slot.shape, bf16), a))
            flat += [a.own, a.other]
            in_specs += [far, far]
        else:
            v = a.array if isinstance(a, Save) else a
            plan.append(("here", len(flat), a))
            flat.append(v)
            in_specs.append(smem if v.dtype == jnp.int32 else vmem)
    out_shape, out_specs, out_plan = [], [], []
    for o in outs:
        if isinstance(o, Slot):
            out_plan.append((o, hold((o.rows, o.shape[1]), bf16)))
        else:
            out_plan.append((None, len(out_shape)))
            out_shape.append(sds(*o))
            out_specs.append(vmem)
    n_args, n_out, n_hold = len(flat), len(out_shape), len(scratch)
    n_saves = sum(isinstance(a, (Save, Half)) for a in args)
    alias = {}
    if uses:
        if store.array is not None:
            flat.append(store.array)
            in_specs.append(far)
            alias = {len(flat) - 1: n_out}
        out_shape.append(sds((STORE_ROWS, 1024), bf16))
        out_specs.append(far)
    n_in = len(flat)
    n_sems = n_hold + n_saves

    def wrapped(*refs):
        ins, results = refs[:n_in], refs[n_in : n_in + len(out_shape)]
        holds = refs[n_in + len(out_shape) :]
        sems = holds[n_hold] if n_sems else None
        big = results[n_out] if uses else None
        given, leaving, late = [], [], n_hold
        for item in plan:
            if item[0] == "here":
                given.append(ins[item[1]])
                if isinstance(item[2], Save):
                    copy = pltpu.make_async_copy(ins[item[1]], item[2].slot.of(big), sems.at[late])
                    copy.start()
                    leaving.append(copy)
                    late += 1
                continue
            to, sem = holds[item[2]], sems.at[item[2]]
            if item[0] == "half":
                h = item[3]
                mine = lax.axis_index("pipe") == h.core
                for k in range(2):

                    @pl.when(mine if k == 0 else jnp.logical_not(mine))
                    def _(src=ins[item[1] + k]):
                        for c in range(h.slot.shape[0] // h.rows):
                            pltpu.make_async_copy(
                                src.at[pl.ds(c * h.block, h.rows), pl.ds(h.at, h.width)],
                                to.at[pl.ds(c * h.rows, h.rows)],
                                sem,
                            ).start()

                whole = pltpu.make_async_copy(to, to, sem)
                out = pltpu.make_async_copy(to, h.slot.of(big), sems.at[late])
                late += 1
                leaving.append(out)

                def arrive(whole=whole, out=out):
                    whole.wait()
                    out.start()

                given.append(Held(to, arrive, h.slot.shape, bf16))
                continue
            if item[0] == "slot":
                copy = pltpu.make_async_copy(item[1].of(big), to, sem)
                shape, dtype = item[1].shape, item[1].dtype
            else:
                copy = pltpu.make_async_copy(ins[item[1]], to, sem)
                shape, dtype = to.shape, to.dtype
            copy.start()
            given.append(Held(to, copy.wait, shape, dtype))
        for slot, at in out_plan:
            if slot is None:
                given.append(results[at])
            else:
                copy = pltpu.make_async_copy(holds[at], slot.of(big), sems.at[at])
                kept = Kept(holds[at], copy, slot.shape, slot.dtype)
                leaving.append(copy)
                given.append(kept)
        kernel(*given)
        ready(*given)
        for g in given:
            if isinstance(g, Kept):
                g.send()
        for copy in leaving:
            copy.wait()

    got = pl.pallas_call(
        wrapped,
        out_shape=tuple(out_shape),
        in_specs=in_specs,
        out_specs=tuple(out_specs),
        scratch_shapes=scratch + ([pltpu.SemaphoreType.DMA((n_sems,))] if n_sems else []),
        input_output_aliases=alias,
        compiler_params=pltpu.CompilerParams(vmem_limit_bytes=24 * 1024 * 1024),
    )(*flat)
    if uses:
        store.array = got[n_out]
    return got[:n_out]


def mm(a, b):
    return lax.dot_general(a, b, (((1,), (0,)), ((), ())), preferred_element_type=f32)


def mm_nt(a, b):
    return lax.dot_general(a, b, (((1,), (1,)), ((), ())), preferred_element_type=f32)


def mm_tn(a, b):
    return lax.dot_general(a, b, (((0,), (0,)), ((), ())), preferred_element_type=f32)


def part(mod, k):
    return jnp.concatenate(
        [jnp.broadcast_to(mod[3 * k + l : 3 * k + l + 1, :], (8, mod.shape[1])) for l in range(LAT)],
        axis=0,
    )


def centred(x):
    c = x - jnp.mean(x, axis=-1, keepdims=True)
    r = lax.rsqrt(jnp.mean(c * c, axis=-1, keepdims=True) + EPS)
    return c * r, r


def norm_back(x, dy, scale):
    xh, r = centred(x)
    g = dy * (1.0 + scale)
    dx = r * (
        g - jnp.mean(g, axis=-1, keepdims=True) - xh * jnp.mean(g * xh, axis=-1, keepdims=True)
    )
    return dx, dy, dy * xh


def row_sums(*vs):
    return jnp.concatenate(
        [jnp.sum(v[8 * l : 8 * l + 8], axis=0, keepdims=True) for v in vs for l in range(LAT)], axis=0
    )


def summed(ref, *at):
    total = ref[(0, *at)].astype(f32)
    for j in range(1, 8):
        total = total + ref[(j, *at)].astype(f32)
    return total


def to_all(ref, v):
    for j in range(8):
        ref[j] = v


def by_latent(v):
    v = v.reshape(8, LAT, 8, v.shape[-1])
    return [v[:, l].reshape(64, v.shape[-1]) for l in range(LAT)]


def rows_of(v):
    return v.reshape(-1, v.shape[-1])


def by_part(vs):
    w = vs[0].shape[-1]
    return jnp.stack([v.reshape(8, 8, w) for v in vs], axis=1).reshape(192, w)


def gelu_parts(x):
    t = jnp.tanh(GELU_C * (x + GELU_A * (x * x * x)))
    return t


def k_halves(p_ref, wq_ref, wo_ref, up_ref, down_ref, keep_ref, send_ref):
    ready(wq_ref, wo_ref, up_ref, down_ref)

    def put(a_ref, b_ref):
        for k in range(2):
            a_ref[:, 128 * k : 128 * k + 128] = wq_ref[k]
        a_ref[:, 256:] = up_ref[...]
        b_ref[:, :128] = wq_ref[2]
        b_ref[:, 128:256] = wo_ref[...].astype(f32).T.astype(bf16)
        b_ref[:, 256:] = down_ref[...].astype(f32).T.astype(bf16)

    @pl.when(p_ref[0] == 0)
    def _():
        put(keep_ref, send_ref)

    @pl.when(p_ref[0] == 1)
    def _():
        put(send_ref, keep_ref)


def k_pack(
    p_ref, t_ref, lab_ref, table_ref, sinus_ref, ada_ref, keep_ref, got_ref,
    o_ref, w0_ref, w1_ref, cond_ref, act_ref,
):
    first = p_ref[0] == 0
    keep, got = keep_ref[...].astype(f32), got_ref[...].astype(f32)
    w0 = jnp.where(first, keep, got).astype(bf16)
    w0_ref[...] = w0[:, 256:]
    w1_ref[...] = jnp.where(first, got, keep).astype(bf16)
    row = lax.broadcasted_iota(jnp.int32, (8, table_ref.shape[0]), 0)
    col = lax.broadcasted_iota(jnp.int32, (8, table_ref.shape[0]), 1)
    label = jnp.where(row == 0, lab_ref[0], jnp.where(row == 1, lab_ref[1], lab_ref[2]))
    cond = mm(jnp.where(col == label, 1.0, 0.0).astype(bf16), table_ref[...])[:LAT] + sinus_ref[...]
    cond_ref[...] = cond
    act = (cond / (1.0 + jnp.exp(-cond))).astype(bf16)
    act_ref[...] = act
    lane = lax.broadcasted_iota(jnp.int32, (16, 256), 1)
    row = lax.broadcasted_iota(jnp.int32, (16, 256), 0)
    place = jnp.where(lane == row + 16 * t_ref[0], 1.0, 0.0).astype(bf16)
    mod = [mm(mm_nt(act, ada_ref[16 * k : 16 * k + 16]).astype(bf16), place) for k in range(6)]
    mod = jnp.concatenate(mod + [jnp.zeros((14, 256), f32)], axis=0).astype(bf16)
    for j in range(8):
        o_ref[j, :128] = w0[:, :256]
        o_ref[j, 128:] = mod


def k_spread(r_ref, o_ref):
    for c in range(8):
        v = r_ref[c, 128:, :128]
        for j in range(8):
            o_ref[j, c] = v


def k_mods(r_ref, o_ref):
    for c in range(8):
        o_ref[:, 128 * c : 128 * c + 128] = summed(r_ref, c).astype(bf16)


def k_two_layers(p_ref, own_ref, other_ref, a_ref, b_ref):
    own, other, first = own_ref[...].astype(f32), other_ref[...].astype(f32), p_ref[0] == 0
    a_ref[...] = jnp.where(first, own, other).astype(bf16)
    b_ref[...] = jnp.where(first, other, own).astype(bf16)


def put_qkv(y, q_ref, kv_ref):
    y = jnp.concatenate(by_latent(y), axis=0).astype(bf16)
    q_ref[...] = y[:, :128]
    to_all(kv_ref, y[:, 128:])


def triple(n, wa_ref, wb_ref):
    a = mm(n, rows_of(wa_ref[...]))
    return jnp.concatenate([a, mm(n, rows_of(wb_ref[...])[:, :128])], axis=1)


def own_blocks(p_ref, t_ref, x_ref, own_ref):
    start = pl.multiple_of(64 * p_ref[0], 64)
    few = pl.multiple_of(64 * p_ref[0] + 8 * t_ref[0], 8)
    own_ref[...] = jnp.concatenate([x_ref[l, pl.ds(few, 8), :] for l in range(LAT)], axis=0)
    blocks = [x_ref[l, pl.ds(start, 64), :] for l in range(LAT)]
    return [
        jnp.concatenate([b[8 * j : 8 * j + 8] for b in blocks], axis=0) for j in range(8)
    ]


def k_first(p_ref, t_ref, x_ref, mod_ref, wa_ref, wb_ref, own_ref, n_ref, q_ref, kv_ref):
    mod = mod_ref[...].astype(f32)
    shift, scale = part(mod, 0), 1.0 + part(mod, 1)
    x_ref.ready()
    rows = [centred(x)[0] * scale + shift for x in own_blocks(p_ref, t_ref, x_ref.ref, own_ref)]
    n = jnp.concatenate(rows, axis=0).astype(bf16)
    n_ref[...] = n
    put_qkv(triple(n, wa_ref, wb_ref), q_ref, kv_ref)


def k_qkv(n_ref, wa_ref, wb_ref, q_ref, kv_ref):
    put_qkv(triple(n_ref[...], wa_ref, wb_ref), q_ref, kv_ref)


def head_rows(v):
    lane = lax.broadcasted_iota(jnp.int32, v.shape, 1)
    zero = jnp.zeros_like(v)
    return jnp.concatenate(
        [jnp.where(lane < HEAD, v, zero), jnp.where(lane < HEAD, zero, v)], axis=0
    )


def head_lanes(v):
    lane = lax.broadcasted_iota(jnp.int32, (64, 128), 1)
    return jnp.where(lane < HEAD, v[:64], v[64:])


def keys_values(a_ref, b_ref, l):
    at = [64 * (LAT * c + l) for c in range(8)]
    kv = jnp.concatenate([r[i : i + 64] for r in (a_ref, b_ref) for i in at], axis=0)
    return kv[:, :128], kv[:, 128:]


def soft(qs, k):
    s = mm_nt(qs, k) * 0.125
    e = jnp.exp(s - jnp.max(s, axis=-1, keepdims=True))
    return e / jnp.sum(e, axis=-1, keepdims=True)


def k_attn(q_ref, a_ref, b_ref, w_ref, att_ref, o_ref):
    outs = []
    for l in range(LAT):
        k, v = keys_values(a_ref, b_ref, l)
        probs = soft(head_rows(q_ref[64 * l : 64 * l + 64].astype(f32)).astype(bf16), k)
        outs.append(head_lanes(mm(probs.astype(bf16), v)))
    att = by_part(outs).astype(bf16)
    att_ref[...] = att
    o_ref[...] = mm_nt(att, rows_of(w_ref[...])[:, 128:]).astype(bf16)


def k_attn_back(q_ref, a_ref, b_ref, w_ref, db_ref, dq_ref, da_ref, dp_ref):
    datt = by_latent(mm(db_ref[...], rows_of(w_ref[...])[:, 128:]))
    for l in range(LAT):
        k, v = keys_values(a_ref, b_ref, l)
        qs = head_rows(q_ref[64 * l : 64 * l + 64].astype(f32)).astype(bf16)
        do = head_rows(datt[l]).astype(bf16)
        probs = soft(qs, k)
        dprobs = mm_nt(do, v)
        dv = mm_tn(probs.astype(bf16), do)
        ds = probs * (dprobs - jnp.sum(probs * dprobs, axis=-1, keepdims=True))
        ds = ds.astype(bf16)
        dk = mm_tn(ds, qs) * 0.125
        dq_ref[64 * l : 64 * l + 64] = (head_lanes(mm(ds, k)) * 0.125).astype(bf16)
        dkv = jnp.concatenate([dk, dv], axis=1).astype(bf16)
        for c in range(8):
            at = 64 * (LAT * c + l)
            da_ref[at : at + 64] = dkv[64 * c : 64 * c + 64]
            dp_ref[at : at + 64] = dkv[512 + 64 * c : 512 + 64 * c + 64]


def k_pair_sum(a_ref, b_ref, o_ref):
    o_ref[...] = (a_ref[...].astype(f32) + b_ref[...].astype(f32)).astype(bf16)


def k_qkv_back(dq_ref, r_ref, wa_ref, wb_ref, dt_ref, o_ref):
    dt = jnp.concatenate([dq_ref[...].astype(f32), summed(r_ref)], axis=1)
    dt = by_part([dt[64 * l : 64 * l + 64] for l in range(LAT)]).astype(bf16)
    dt_ref[...] = dt
    back = mm_nt(dt[:, :256], rows_of(wa_ref[...])) + mm_nt(dt[:, 256:], rows_of(wb_ref[...])[:, :128])
    o_ref[...] = back.astype(bf16)


def k_mid(r_ref, x_ref, mod_ref, br_ref, mid_ref, o_ref):
    mod = mod_ref[...].astype(f32)
    branch = summed(r_ref)
    mid = x_ref[...] + part(mod, 2) * branch
    br_ref[...] = branch
    mid_ref[...] = mid
    xh, _ = centred(mid)
    to_all(o_ref, (xh * (1.0 + part(mod, 4)) + part(mod, 3)).astype(bf16))


def k_mlp(n_ref, up_ref, down_ref, hid_ref, o_ref):
    pre = mm(n_ref[...], rows_of(up_ref[...]))
    hid = (0.5 * pre * (1.0 + gelu_parts(pre))).astype(bf16)
    hid_ref[...] = hid
    o_ref[...] = mm_nt(hid, rows_of(down_ref[...])).astype(bf16)


def gelu_slope(pre, t):
    inner = GELU_C * (1.0 + 3.0 * GELU_A * pre * pre)
    return 0.5 * (1.0 + t) + 0.5 * pre * (1.0 - t * t) * inner


def k_mlp_both(n_ref, up_ref, down_ref, dm_ref, hid_ref, dpre_ref, o_ref):
    pre = mm(n_ref[...], rows_of(up_ref[...]))
    t = gelu_parts(pre)
    hid = (0.5 * pre * (1.0 + t)).astype(bf16)
    hid_ref[...] = hid
    out = mm_nt(hid, rows_of(down_ref[...])).astype(bf16)
    dhid = mm(dm_ref[...], rows_of(down_ref[...]))
    dpre = (dhid * gelu_slope(pre, t)).astype(bf16)
    dpre_ref[...] = dpre
    back = mm_nt(dpre, rows_of(up_ref[...])).astype(bf16)
    for j in range(8):
        o_ref[j, 0] = out[24 * j : 24 * j + 24]
        o_ref[j, 1] = back[24 * j : 24 * j + 24]


def k_mlp_back(n_ref, up_ref, down_ref, dm_ref, dpre_ref, o_ref):
    pre = mm(n_ref[...], rows_of(up_ref[...]))
    dhid = mm(dm_ref[...], rows_of(down_ref[...]))
    dpre = (dhid * gelu_slope(pre, gelu_parts(pre))).astype(bf16)
    dpre_ref[...] = dpre
    o_ref[...] = mm_nt(dpre, rows_of(up_ref[...])).astype(bf16)


def k_gate_rows(p_ref, t_ref, c_ref, mod_ref, own_ref, o_ref):
    gate = part(mod_ref[...].astype(f32), 5)
    c_ref.ready()
    rows = [gate * c for c in own_blocks(p_ref, t_ref, c_ref.ref, own_ref)]
    o_ref[...] = jnp.concatenate(rows, axis=0).astype(bf16)


def k_next(r_ref, mid_ref, mod_ref, mod_next_ref, mlp_ref, x_ref, o_ref):
    mod, mod_next = mod_ref[...].astype(f32), mod_next_ref[...].astype(f32)
    mlp = summed(r_ref)
    mlp_ref[...] = mlp
    x = mid_ref[...] + part(mod, 5) * mlp
    x_ref[...] = x
    xh, _ = centred(x)
    to_all(o_ref, (xh * (1.0 + part(mod_next, 1)) + part(mod_next, 0)).astype(bf16))


def back_two(mod, mid, branch, dy, dn, mlp, dmid_ref, dmod_ref, o_ref):
    dx, ds, dc = norm_back(mid, dn, part(mod, 4))
    dmid = dy + dx
    dmid_ref[...] = dmid
    to_all(o_ref, (part(mod, 2) * dmid).astype(bf16))
    dmod_ref[...] = row_sums(dmid * branch, ds, dc, dy * mlp)


def k_last(r_ref, mid_ref, br_ref, dy_ref, mod_ref, res_ref, dmid_ref, dmod_ref, o_ref):
    mod = mod_ref[...].astype(f32)
    mlp, dn = summed(r_ref, 0), summed(r_ref, 1)
    mid = mid_ref[...]
    res_ref[...] = mid + part(mod, 5) * mlp
    back_two(mod, mid, br_ref[...], dy_ref[...], dn, mlp, dmid_ref, dmod_ref, o_ref)


def k_back_two(r_ref, mid_ref, br_ref, dy_ref, mlp_ref, mod_ref, dmid_ref, dmod_ref, o_ref):
    mod = mod_ref[...].astype(f32)
    back_two(
        mod, mid_ref[...], br_ref[...], dy_ref[...], summed(r_ref), mlp_ref[...],
        dmid_ref, dmod_ref, o_ref,
    )


def k_back_one(r_ref, x_ref, dmid_ref, mod_ref, mod_before_ref, dx_ref, dmod_ref, o_ref):
    dx, ds, dc = norm_back(x_ref[...], summed(r_ref), part(mod_ref[...].astype(f32), 1))
    dx = dmid_ref[...] + dx
    dx_ref[...] = dx
    dmod_ref[...] = row_sums(ds, dc)
    to_all(o_ref, (part(mod_before_ref[...].astype(f32), 5) * dx).astype(bf16))


def k_back_first(
    p_ref, r_ref, x_ref, dmid_ref, mod_ref, d0_ref, d1a_ref, d1b_ref, res_ref, keep_ref, send_ref
):
    first = p_ref[0] == 0
    dx, ds, dc = norm_back(x_ref[...], summed(r_ref), part(mod_ref[...].astype(f32), 1))
    dx = dmid_ref[...] + dx
    res = res_ref[...]
    keep_ref[:24] = jnp.where(first, dx, res)
    send_ref[:24] = jnp.where(first, res, dx)
    none = jnp.zeros((6, dx.shape[1]), f32)
    d0 = jnp.concatenate([row_sums(ds, dc), d0_ref[...], none], axis=0)
    d1 = jnp.concatenate([d1b_ref[...], d1a_ref[...], none], axis=0)
    keep_ref[24:] = jnp.where(first, d0, d1)
    send_ref[24:] = jnp.where(first, d1, d0)


def k_tail_tp(p_ref, keep_ref, got_ref, o_ref):
    first = p_ref[0] == 0
    keep, got = keep_ref[...], got_ref[...]
    v = jnp.concatenate(
        [
            jnp.where(first, keep[:24], got[:24]),
            jnp.where(first, got[:24], keep[:24]),
            keep[24:] + got[24:],
        ],
        axis=0,
    ).astype(bf16)
    to_all(o_ref, v)


def k_tail_ctx(r_ref, a_ref, b_ref, o_ref):
    total = r_ref[0].astype(f32)[48:]
    for j in range(1, 8):
        total = total + r_ref[j].astype(f32)[48:]
    total = jnp.concatenate([total, jnp.zeros((8, total.shape[1]), f32)], axis=0).astype(bf16)
    both = (a_ref[...].astype(f32) + b_ref[...].astype(f32)).astype(bf16)
    none = jnp.zeros((32, 128), bf16)
    for c in range(8):
        o_ref[c, :128, :] = both[128 * c : 128 * c + 128]
        o_ref[c, 128:, :128] = total[:, 128 * c : 128 * c + 128]
        o_ref[c, 128:, 128:] = none


def k_ends(r_ref, o_ref):
    for j in range(8):
        v = r_ref[j].astype(f32)
        for half in range(2):
            for l in range(LAT):
                at = 64 * half + 8 * j
                o_ref[l, at : at + 8, :] = v[24 * half + 8 * l : 24 * half + 8 * l + 8]


def k_cond(t_ref, r_ref, act_ref, ada_ref, g_ref, ada_grad_ref, c_ref):
    total = summed(r_ref)
    g_ref[...] = total[:128].astype(bf16)
    d = total[128:, :128].astype(bf16)
    lane = lax.broadcasted_iota(jnp.int32, (128, 16), 0)
    col = lax.broadcasted_iota(jnp.int32, (128, 16), 1)
    pick = jnp.where(lane == col + 16 * t_ref[0], 1.0, 0.0).astype(bf16)
    d = mm(d, pick)
    act = act_ref[...]
    c = jnp.zeros(c_ref.shape, f32)
    for k in range(6):
        dk = d[3 * k : 3 * k + 3].astype(bf16)
        ada_grad_ref[16 * k : 16 * k + 16, :] = mm_tn(dk, act)
        c = c + mm(dk, ada_ref[16 * k : 16 * k + 16, :])
    c_ref[...] = c


def k_grad_mlp(p_ref, n_ref, dpre_ref, dm_ref, hid_ref, keep_ref, send_ref):
    first = p_ref[0] == 0
    n, dm = n_ref[...], dm_ref[...]
    dpre, hid = dpre_ref[...], hid_ref[...]

    def pick(a, b):
        return jnp.where(first, a.astype(f32), b.astype(f32)).astype(bf16)

    send_ref[...] = mm_tn(pick(dm, n), pick(hid, dpre)).astype(bf16)
    keep_ref[...] = mm_tn(pick(n, dm), pick(dpre, hid)).astype(bf16)


def k_grad_attn(p_ref, n_ref, dt_ref, db_ref, att_ref, keep_ref, send_ref):
    first = p_ref[0] == 0
    n, dt = n_ref[...], dt_ref[...]
    qk = mm_tn(n, dt[:, :256])
    vo = jnp.concatenate([mm_tn(n, dt[:, 256:]), mm_tn(db_ref[...], att_ref[...])], axis=1)
    send_ref[...] = jnp.where(first, vo, qk).astype(bf16)
    keep_ref[...] = jnp.where(first, qk, vo).astype(bf16)


def k_grad_sum(a_ref, b_ref, c_ref, d_ref, e_ref, f_ref, o_ref):
    at = 0
    for keep, got in ((a_ref, b_ref), (c_ref, d_ref), (e_ref, f_ref)):
        v = (keep[...].astype(f32) + got[...].astype(f32)).astype(bf16)
        o_ref[:, at : at + v.shape[1]] = v
        at += v.shape[1]


def exchange(x, axis):
    return lax.all_to_all(x, axis, 0, 0, tiled=True)


def swap(x):
    return lax.ppermute(x, "pipe", [(0, 1), (1, 0)])


def copies(x, n):
    return jnp.broadcast_to(x[None], (n, *x.shape))


def body(latents, cotangent, labels, steps, label_table, w_ada, w_qkv, w_out, w_up, w_down):
    p, t = lax.axis_index("pipe"), lax.axis_index("tp")
    first = p == 0
    who, part_no = p.astype(jnp.int32).reshape(1), t.astype(jnp.int32).reshape(1)
    width = latents.shape[2]

    def of_layer(own, other):
        return jnp.where(first, own, other), jnp.where(first, other, own)

    store = Store()
    slot = store.slot

    def run(kernel, outs, *args):
        return call(store, kernel, outs, *args)

    keep, send = run(
        k_halves, [((128, 768), bf16)] * 2,
        who, Near(w_qkv[0].transpose(1, 0, 2)), Near(w_out[0]), Near(w_up[0]), Near(w_down[0]),
    )
    half = width // 2
    freq = jnp.exp(-math.log(10000.0) * jnp.arange(half, dtype=f32) / half)
    angles = steps.astype(f32)[:, None] * freq[None, :]
    sinus = jnp.concatenate([jnp.cos(angles), jnp.sin(angles)], axis=1)
    ada = w_ada[0].transpose(1, 2, 0).reshape(96, width)
    packed, w0, w1, condition, cond_act = run(
        k_pack,
        [
            ((8, 160, 256), bf16), ((128, 512), bf16), ((128, 768), bf16),
            ((LAT, width), f32), ((LAT, width), bf16),
        ],
        who, part_no, labels, label_table, sinus, ada, keep, swap(send),
    )
    w0 = lax.all_gather(w0, "ctx", axis=0, tiled=True)
    packed = exchange(packed, "ctx")
    (spread,) = run(k_spread, [((8, 8, 32, 128), bf16)], packed)
    packed = packed.reshape(1280, 256)
    packed_other = swap(packed)
    sa = [[slot((1024, 256), bf16) for _ in range(2)] for _ in range(2)]
    sm = [[slot((1024, 512), bf16) for _ in range(2)] for _ in range(2)]
    wa0 = [Half(c, packed, packed_other, 160, 128, 0, 256, sa[0][c]) for c in range(2)]
    (mod_own,) = run(k_mods, [((32, 1024), bf16)], exchange(spread, "tp"))
    mods = run(k_two_layers, [((32, 1024), bf16)] * 2, who, mod_own, swap(mod_own))

    bc = ((8, 24, 1024), bf16)
    wide = ((192, 1024), bf16)
    kv_all = ((1536, 256), bf16)

    def rows24(n=24):
        return slot((n, 1024), f32)

    def rows192(n):
        return slot((192, n), bf16)

    def attn_forward(q, kv, w):
        kv_a = exchange(kv, "ctx").reshape(1536, 256)
        kv_b = swap(kv_a)
        att, sa, sb = rows192(128), slot((1536, 256), bf16), slot((1536, 256), bf16)
        (branch,) = run(k_attn, [att, wide], q, Save(kv_a, sa), Save(kv_b, sb), w[1])
        return (q, sa, sb, att), exchange(branch.reshape(8, 24, 1024), "tp")

    def attn_back(kept, normed, dbranch, w):
        q, kv_a, kv_b, att = kept
        db, dq, dt = rows192(1024), rows192(128), rows192(384)
        da, dp = run(k_attn_back, [dq, kv_all, kv_all], q, kv_a, kv_b, w[1], Save(dbranch, db))
        (both,) = run(k_pair_sum, [kv_all], da, swap(dp))
        arrived = exchange(both.reshape(8, 192, 256), "ctx")
        (dn,) = run(k_qkv_back, [dt, wide], dq, arrived, *w)
        arrived = exchange(dn.reshape(8, 24, 1024), "tp")
        keep = slot((1024, 256), bf16)
        (send,) = run(k_grad_attn, [keep, ((1024, 256), bf16)], who, normed, dt, db, att)
        return arrived, keep, swap(send)

    def grads_mlp(n, dpre, dm, hid):
        keep = slot((1024, 512), bf16)
        (send,) = run(k_grad_mlp, [keep, ((1024, 512), bf16)], who, n, dpre, dm, hid)
        return keep, swap(send)

    def to_rows(x):
        return exchange(x, "tp").reshape(192, 1024)

    x0, normed0, q0 = rows24(), rows192(1024), rows192(128)
    (kv,) = run(
        k_first, [x0, normed0, q0, ((8, 192, 256), bf16)],
        who, part_no, Near(latents), mods[0], *wa0,
    )
    wa0 = sa[0]
    cot, dm1 = rows24(), rows192(1024)
    run(k_gate_rows, [cot, dm1], who, part_no, Near(cotangent), mods[1])
    kept0, arrived = attn_forward(q0, kv, wa0)
    br0, mid0 = rows24(), rows24()
    (n2,) = run(k_mid, [br0, mid0, bc], arrived, x0, mods[0])
    n2 = to_rows(n2)
    w0_other = swap(w0)
    wm0 = [Half(c, w0, w0_other, 1024, 1024, 0, 512, sm[0][c]) for c in range(2)]
    n2_0, hid0 = rows192(1024), rows192(512)
    (out,) = run(k_mlp, [hid0, wide], Save(n2, n2_0), *wm0)
    wm0 = sm[0]
    arrived = exchange(out.reshape(8, 24, 1024), "tp")
    mlp0, x1 = rows24(), rows24()
    (n1,) = run(k_next, [mlp0, x1, bc], arrived, mid0, mods[0], mods[1])

    w1 = lax.all_gather(w1, "ctx", axis=0, tiled=True)
    n1, w1 = lax.optimization_barrier((n1, w1))
    n1 = to_rows(n1)
    w1_other = swap(w1)
    wa1 = [Half(c, w1, w1_other, 1024, 1024, 0, 256, sa[1][c]) for c in range(2)]
    wm1 = [Half(c, w1, w1_other, 1024, 1024, 256, 512, sm[1][c]) for c in range(2)]
    normed1, q1 = rows192(1024), rows192(128)
    (kv,) = run(k_qkv, [q1, ((8, 192, 256), bf16)], Save(n1, normed1), *wa1)
    wa1 = sa[1]
    kept1, arrived = attn_forward(q1, kv, wa1)
    br1, mid1 = rows24(), rows24()
    (n2,) = run(k_mid, [br1, mid1, bc], arrived, x1, mods[1])
    n2 = to_rows(n2)
    n2_1, hid1, dpre1 = rows192(1024), rows192(512), rows192(512)
    (both,) = run(
        k_mlp_both, [hid1, dpre1, ((8, 2, 24, 1024), bf16)], Save(n2, n2_1), *wm1, dm1
    )
    arrived = exchange(both, "tp")
    res1, dmid1, dmod1a = rows24(), rows24(), rows24(12)
    (db,) = run(k_last, [res1, dmid1, dmod1a, bc], arrived, mid1, br1, cot, mods[1])
    gm1 = grads_mlp(n2_1, dpre1, dm1, hid1)

    arrived, *ga1 = attn_back(kept1, normed1, to_rows(db), wa1)
    dx1, dmod1b = rows24(), rows24(6)
    (dm,) = run(k_back_one, [dx1, dmod1b, bc], arrived, x1, dmid1, mods[1], mods[0])
    dm = to_rows(dm)

    dm0, dpre0 = rows192(1024), rows192(512)
    (dn,) = run(k_mlp_back, [dpre0, wide], n2_0, *wm0, Save(dm, dm0))
    arrived = exchange(dn.reshape(8, 24, 1024), "tp")
    gm0 = grads_mlp(n2_0, dpre0, dm0, hid0)
    dmid0, dmod0a = rows24(), rows24(12)
    (db,) = run(k_back_two, [dmid0, dmod0a, bc], arrived, mid0, br0, dx1, mlp0, mods[0])
    (mixed,) = run(k_grad_sum, [((1024, 1280), bf16)], *gm0, *gm1, *ga1)
    mixed = lax.psum_scatter(mixed, "ctx", tiled=True)
    gm0, gm1, ga1 = mixed[:, :512], mixed[:, 512:1024], mixed[:, 1024:]

    arrived, *ga0 = attn_back(kept0, normed0, to_rows(db), wa0)
    keep, send = run(
        k_back_first, [((48, 1024), f32)] * 2,
        who, arrived, x0, dmid0, mods[0], dmod0a, dmod1a, dmod1b, res1,
    )

    (tail,) = run(k_tail_tp, [((8, 72, 1024), bf16)], who, keep, swap(send))
    tail = exchange(tail, "tp")
    (tail_ctx,) = run(k_tail_ctx, [((8, 160, 256), bf16)], tail, *ga0)
    tail_ctx = exchange(tail_ctx, "ctx")
    (ends,) = run(k_ends, [((LAT, 128, 1024), f32)], tail)
    ga0, grad_ada, cond_part = run(
        k_cond, [((128, 256), bf16), ((96, 1024), f32), ((LAT, 1024), f32)],
        part_no, tail_ctx, cond_act, ada,
    )
    cond_part = (cond_part + swap(cond_part)).reshape(24, 128)
    grad_act = exchange(copies(cond_part, 64), ("ctx", "tp"))
    mine = jnp.concatenate([jnp.where(first, gm0, gm1), jnp.where(first, ga0, ga1)], axis=1)
    send = jnp.concatenate([jnp.where(first, gm1, gm0), jnp.where(first, ga1, ga0)], axis=1)
    half0, half1 = of_layer(mine, swap(send))
    grad_up = half0[:, :512].astype(f32)
    grad_down = half1[:, :512].astype(f32).T
    grad_qkv = jnp.concatenate([half0[:, 512:], half1[:, 512:640]], axis=1).astype(f32)
    grad_out = half1[:, 640:].astype(f32).T

    grad_act, grad_up, grad_down, grad_qkv, grad_out = lax.optimization_barrier(
        (grad_act, grad_up, grad_down, grad_qkv, grad_out)
    )
    grad_act = grad_act.sum(axis=0).reshape(LAT, width)
    sig = jax.nn.sigmoid(condition)
    grad_cond = grad_act * (sig * (1.0 + condition * (1.0 - sig)))
    classes = jnp.arange(label_table.shape[0], dtype=jnp.int32)[:, None]
    grad_table = sum(
        jnp.where(classes == labels[l], grad_cond[l : l + 1], 0.0) for l in range(LAT)
    )

    return (
        ends[None],
        grad_table,
        grad_ada.reshape(6, 16, width).transpose(2, 0, 1)[None],
        grad_qkv.reshape(1, 128, 3, 128),
        grad_out[None],
        grad_up[None],
        grad_down[None],
    )


def solution(mesh):
    return jax.shard_map(
        body,
        mesh=mesh,
        in_specs=(
            P(None, "ctx", None),
            P(None, "ctx", None),
            P(),
            P(),
            P(),
            P("pipe", None, None, ("ctx", "tp")),
            P("pipe", "ctx", None, "tp"),
            P("pipe", "tp", "ctx"),
            P("pipe", "ctx", "tp"),
            P("pipe", "tp", "ctx"),
        ),
        out_specs=(
            P("pipe", None, "ctx", None),
            P(),
            P("pipe", None, None, ("ctx", "tp")),
            P("pipe", "ctx", None, "tp"),
            P("pipe", "tp", "ctx"),
            P("pipe", "ctx", "tp"),
            P("pipe", "tp", "ctx"),
        ),
        check_vma=False,
    )
```

time: 489 us -> 463 us (0.947)
  Pallas kernels: 30.3 us -> 76.4 us
  local copies, waits for them, and re-layouts: 49.6 us -> 15.7 us
  starting transfers between devices: 99.3 us -> 74.8 us
  blocking collectives: 157 us -> 175 us
  waiting for transfers between devices: 109 us -> 95.6 us
  other arithmetic: 19.3 us -> 8.08 us
  between operations: 20.5 us -> 14.3 us
    pallas_call x30 -> x35, Pallas kernels: 30.3 us -> 76.4 us  [call(): pl.pallas_call(wrapped, out_shape=tuple(out_shape), in_specs=in_specs, ou...]
    all_to_all x11 -> x9, starting transfers between devices: 63.4 us -> 38.8 us  [exchange(): return lax.all_to_all(x, axis, 0, 0, tiled=True)]
    unnamed x204 -> x35, local copies, waits for them, and re-layouts: 35.5 us -> 14 us
    all_to_all x12 -> x13, blocking collectives: 157 us -> 175 us  [exchange(): return lax.all_to_all(x, axis, 0, 0, tiled=True)]
    reduce_scatter x2 -> x1, waiting for transfers between devices: 9.69 us -> 0.01 us  [body(): mixed = lax.psum_scatter(mixed, 'ctx', tiled=True)]
    select_n x5 -> x1, other arithmetic: 6.93 us -> 0.07 us  [of_layer(): return (jnp.where(first, own, other), jnp.where(first, other, own))]
    all_to_all x11 -> x9, waiting for transfers between devices: 88.4 us -> 84.6 us  [exchange(): return lax.all_to_all(x, axis, 0, 0, tiled=True)]
    ppermute x15 -> x16, waiting for transfers between devices: 7.48 us -> 10.2 us  [swap(): return lax.ppermute(x, 'pipe', [(0, 1), (1, 0)])]
  transfers between devices with their start and end apart: 29 -> 28, of which waited for: 18 -> 17; matrix products, arithmetic and copies ran while one was open for 7% -> 1% of each run, Pallas kernels for 4% -> 10%
where the time goes in v2:
time: 463 us; the launch traced here: 460 us
  blocking collectives  175 us (38%)
  waiting for transfers between devices  95.6 us (21%)
  Pallas kernels  76.4 us (17%)
  starting transfers between devices  74.8 us (16%)
  local copies, waits for them, and re-layouts  15.7 us (3%)
  between operations  14.3 us (3%)
  other arithmetic  8.08 us (2%)
    all_to_all x13, blocking collectives, exchange(): return lax.all_to_all(x, axis, 0, 0, tiled=True)  175 us
    all_to_all x9, waiting for transfers between devices, exchange(): return lax.all_to_all(x, axis, 0, 0, tiled=True)  84.6 us
    pallas_call x35, Pallas kernels, call(): pl.pallas_call(wrapped, out_shape=tuple(out_shape), in_specs=in_specs, ou...  76.4 us
    all_to_all x9, starting transfers between devices, exchange(): return lax.all_to_all(x, axis, 0, 0, tiled=True)  38.8 us
    ppermute x16, starting transfers between devices, swap(): return lax.ppermute(x, 'pipe', [(0, 1), (1, 0)])  35.9 us
    unnamed x35, local copies, waits for them, and re-layouts  14 us
    ppermute x16, waiting for transfers between devices, swap(): return lax.ppermute(x, 'pipe', [(0, 1), (1, 0)])  10.2 us
  transfers between devices with their start and end apart: 28, of which 17 were waited for; matrix products, arithmetic and copies ran while one was open for 1% of the time, Pallas kernels for 10%

profile of v2, /device:TPU:1, one launch (start us, length us, event | category | flops | bytes accessed | tf_op | source)
XLA Modules:
  0.0 460.3 jit_solution(3818590425180551391)
XLA Ops:
  19.6 15.9 %all_to_all.110.refs_0_ = bf16[8,160,256]{2,1,0:T(8,128)(2,1)S(1)} all-to-all(bf16[8,160,256]{2,1,0:T(8,128)(2,1)S(1)} %get-tuple-element.78), channel_id=1, replica_groups=mesh['pipe'=2,'ctx'=8,'tp'=8] {'ctx'}, dimensions={0} | all-to-all | bytes 1310720 | tf_op jit(solution)/shard_map/all_to_all | solution.py:673
  39.5 7.1 %all-to-all-start.1 = ((bf16[8,8,32,128]{3,2,1,0:T(8,128)(2,1)}), bf16[8,8,32,128]{3,2,1,0:T(8,128)(2,1)S(1)}, u32[]{:S(2)}, u32[]{:S(2)}) async-start(bf16[8,8,32,128]{3,2,1,0:T(8,128)(2,1)} %shard_map.155), calls=%async_computation.1 | async-start | bytes 1048576 | tf_op jit(solution)/shard_map/all_to_all | solution.py:673
  47.4 12.6 %all-to-all-done.1.refs_0_ = bf16[8,8,32,128]{3,2,1,0:T(8,128)(2,1)S(1)} async-done(((bf16[8,8,32,128]{3,2,1,0:T(8,128)(2,1)}), bf16[8,8,32,128]{3,2,1,0:T(8,128)(2,1)S(1)}, u32[]{:S(2)}, u32[]{:S(2)}) %all-to-all-start.1) | async-done | bytes 524320 | tf_op jit(solution)/shard_map/all_to_all | solution.py:673
  66.1 14.5 %all_to_all.111 = bf16[8,192,256]{2,1,0:T(8,128)(2,1)S(1)} all-to-all(bf16[8,192,256]{2,1,0:T(8,128)(2,1)S(1)} %get-tuple-element.80), channel_id=1, replica_groups=mesh['pipe'=2,'ctx'=8,'tp'=8] {'ctx'}, dimensions={0} | all-to-all | bytes 1572864 | tf_op jit(solution)/shard_map/all_to_all | solution.py:673
  85.9 4.2 shard_map.160
  90.0 14.7 %all_to_all.112.refs_0_ = bf16[8,24,1024]{2,1,0:T(8,128)(2,1)S(1)} all-to-all(bf16[8,24,1024]{2,1,0:T(8,128)(2,1)S(1)} %bitcast.69), channel_id=1, replica_groups=mesh['pipe'=2,'ctx'=8,'tp'=8] {'tp'}, dimensions={0} | all-to-all | bytes 786432 | tf_op jit(solution)/shard_map/all_to_all | solution.py:673
  107.2 3.9 all-to-all-start.4
  111.1 11.4 %all-to-all-done.4 = bf16[8,24,1024]{2,1,0:T(8,128)(2,1)S(1)} async-done(((bf16[8,24,1024]{2,1,0:T(8,128)(2,1)}), bf16[8,24,1024]{2,1,0:T(8,128)(2,1)S(1)}, u32[]{:S(2)}, u32[]{:S(2)}) %all-to-all-start.4) | async-done | bytes 393248 | tf_op jit(solution)/shard_map/all_to_all | solution.py:673
  124.3 12.4 %all_to_all.113.refs_0_ = bf16[8,24,1024]{2,1,0:T(8,128)(2,1)S(1)} all-to-all(bf16[8,24,1024]{2,1,0:T(8,128)(2,1)S(1)} %bitcast.68), channel_id=1, replica_groups=mesh['pipe'=2,'ctx'=8,'tp'=8] {'tp'}, dimensions={0} | all-to-all | bytes 786432 | tf_op jit(solution)/shard_map/all_to_all | solution.py:673
  140.6 11.9 %all_to_all.114 = bf16[8,24,1024]{2,1,0:T(8,128)(2,1)S(1)} all-to-all(bf16[8,24,1024]{2,1,0:T(8,128)(2,1)S(1)} %get-tuple-element.92), channel_id=1, replica_groups=mesh['pipe'=2,'ctx'=8,'tp'=8] {'tp'}, dimensions={0} | all-to-all | bytes 786432 | tf_op jit(solution)/shard_map/all_to_all | solution.py:673
  155.3 13.4 %all_to_all.115 = bf16[8,192,256]{2,1,0:T(8,128)(2,1)S(1)} all-to-all(bf16[8,192,256]{2,1,0:T(8,128)(2,1)S(1)} %get-tuple-element.95), channel_id=1, replica_groups=mesh['pipe'=2,'ctx'=8,'tp'=8] {'ctx'}, dimensions={0} | all-to-all | bytes 1572864 | tf_op jit(solution)/shard_map/all_to_all | solution.py:673
  176.8 11.6 %all_to_all.116.refs_0_ = bf16[8,24,1024]{2,1,0:T(8,128)(2,1)S(1)} all-to-all(bf16[8,24,1024]{2,1,0:T(8,128)(2,1)S(1)} %bitcast.70), channel_id=1, replica_groups=mesh['pipe'=2,'ctx'=8,'tp'=8] {'tp'}, dimensions={0} | all-to-all | bytes 786432 | tf_op jit(solution)/shard_map/all_to_all | solution.py:673
  190.1 11.4 %all_to_all.117 = bf16[8,24,1024]{2,1,0:T(8,128)(2,1)S(1)} all-to-all(bf16[8,24,1024]{2,1,0:T(8,128)(2,1)S(1)} %get-tuple-element.99), channel_id=1, replica_groups=mesh['pipe'=2,'ctx'=8,'tp'=8] {'tp'}, dimensions={0} | all-to-all | bytes 786432 | tf_op jit(solution)/shard_map/all_to_all | solution.py:673
  204.1 13.5 %all_to_all.118.refs_0_ = bf16[8,2,24,1024]{3,2,1,0:T(8,128)(2,1)S(1)} all-to-all(bf16[8,2,24,1024]{3,2,1,0:T(8,128)(2,1)S(1)} %get-tuple-element.101), channel_id=1, replica_groups=mesh['pipe'=2,'ctx'=8,'tp'=8] {'tp'}, dimensions={0} | all-to-all | bytes 1572864 | tf_op jit(solution)/shard_map/all_to_all | solution.py:673
  227.0 4.6 %all-to-all-done.11 = bf16[8,24,1024]{2,1,0:T(8,128)(2,1)S(1)} async-done(((bf16[8,24,1024]{2,1,0:T(8,128)(2,1)}), bf16[8,24,1024]{2,1,0:T(8,128)(2,1)S(1)}, u32[]{:S(2)}, u32[]{:S(2)}) %all-to-all-start.11) | async-done | bytes 393248 | tf_op jit(solution)/shard_map/all_to_all | solution.py:673
  231.6 5.1 %shard_map.170 = (bf16[1536,256]{1,0:T(8,128)(2,1)S(1)}, bf16[1536,256]{1,0:T(8,128)(2,1)S(1)}, bf16[34048,1024]{1,0:T(8,128)(2,1)}) custom-call(bf16[192,1024]{1,0:T(8,128)(2,1)S(1)} %bitcast.61, bf16[34048,1024]{1,0:T(8,128)(2,1)} %get-tuple-element.105.refs_1_), custom_call_target="tpu_custom_call", output_to_operand_aliasing={{2}: (1, {})} | custom-call | tf_op jit(solution)/shard_map/pallas_call | solution.py:228
  236.8 5.2 %collective-permute-start.7 = (bf16[1536,256]{1,0:T(8,128)(2,1)S(1)}, bf16[1536,256]{1,0:T(8,128)(2,1)S(1)}, u32[]{:S(2)}, u32[]{:S(2)}) collective-permute-start(bf16[1536,256]{1,0:T(8,128)(2,1)S(1)} %get-tuple-element.107), channel_id=1, source_target_pairs={{0,64},{64,0},{1,65},{65,1},{2,66},{66,2},{3,67},{67,3},{4,68},{68... | collective-permute-start | bytes 2359304 | tf_op jit(solution)/shard_map/ppermute | solution.py:677
  244.1 14.0 %all_to_all.119.refs_0_ = bf16[8,192,256]{2,1,0:T(8,128)(2,1)S(1)} all-to-all(bf16[8,192,256]{2,1,0:T(8,128)(2,1)S(1)} %bitcast.57), channel_id=1, replica_groups=mesh['pipe'=2,'ctx'=8,'tp'=8] {'ctx'}, dimensions={0} | all-to-all | bytes 1572864 | tf_op jit(solution)/shard_map/all_to_all | solution.py:673
  267.8 4.0 all-to-all-done.13.refs_0_
  281.5 4.2 all-to-all-done.14
  291.9 4.7 %collective-permute-start.8 = (bf16[1024,512]{1,0:T(8,128)(2,1)S(1)}, bf16[1024,512]{1,0:T(8,128)(2,1)S(1)}, u32[]{:S(2)}, u32[]{:S(2)}) collective-permute-start(bf16[1024,512]{1,0:T(8,128)(2,1)S(1)} %get-tuple-element.118), channel_id=1, source_target_pairs={{0,64},{64,0},{1,65},{65,1},{2,66},{66,2},{3,67},{67,3},{4,68},{68... | collective-permute-start | bytes 3145736 | tf_op jit(solution)/shard_map/ppermute | solution.py:677
  296.7 11.5 %all_to_all.120.refs_0_ = bf16[8,24,1024]{2,1,0:T(8,128)(2,1)S(1)} all-to-all(bf16[8,24,1024]{2,1,0:T(8,128)(2,1)S(1)} %bitcast.67), channel_id=1, replica_groups=mesh['pipe'=2,'ctx'=8,'tp'=8] {'tp'}, dimensions={0} | all-to-all | bytes 786432 | tf_op jit(solution)/shard_map/all_to_all | solution.py:673
  314.0 11.6 %all_to_all.121 = bf16[8,24,1024]{2,1,0:T(8,128)(2,1)S(1)} all-to-all(bf16[8,24,1024]{2,1,0:T(8,128)(2,1)S(1)} %get-tuple-element.117), channel_id=1, replica_groups=mesh['pipe'=2,'ctx'=8,'tp'=8] {'tp'}, dimensions={0} | all-to-all | bytes 786432 | tf_op jit(solution)/shard_map/all_to_all | solution.py:673
  325.6 5.1 %shard_map.179 = (bf16[1536,256]{1,0:T(8,128)(2,1)S(1)}, bf16[1536,256]{1,0:T(8,128)(2,1)S(1)}, bf16[34048,1024]{1,0:T(8,128)(2,1)}) custom-call(bf16[192,1024]{1,0:T(8,128)(2,1)S(1)} %bitcast.64, bf16[34048,1024]{1,0:T(8,128)(2,1)} %get-tuple-element.122.refs_1_), custom_call_target="tpu_custom_call", output_to_operand_aliasing={{2}: (1, {})} | custom-call | tf_op jit(solution)/shard_map/pallas_call | solution.py:228
  330.8 6.2 %collective-permute-start.11 = (bf16[1536,256]{1,0:T(8,128)(2,1)S(1)}, bf16[1536,256]{1,0:T(8,128)(2,1)S(1)}, u32[]{:S(2)}, u32[]{:S(2)}) collective-permute-start(bf16[1536,256]{1,0:T(8,128)(2,1)S(1)} %get-tuple-element.124), channel_id=1, source_target_pairs={{0,64},{64,0},{1,65},{65,1},{2,66},{66,2},{3,67},{67,3},{4,68},{68... | collective-permute-start | bytes 2359304 | tf_op jit(solution)/shard_map/ppermute | solution.py:677
  339.0 19.1 %all_to_all.122.refs_0_ = bf16[8,192,256]{2,1,0:T(8,128)(2,1)S(1)} all-to-all(bf16[8,192,256]{2,1,0:T(8,128)(2,1)S(1)} %bitcast.58), channel_id=1, replica_groups=mesh['pipe'=2,'ctx'=8,'tp'=8] {'ctx'}, dimensions={0} | all-to-all | bytes 1572864 | tf_op jit(solution)/shard_map/all_to_all | solution.py:673
  360.5 4.6 all-to-all-start.18
  368.1 8.2 %all-to-all-done.18.refs_1_ = bf16[8,24,1024]{2,1,0:T(8,128)(2,1)S(1)} async-done(((bf16[8,24,1024]{2,1,0:T(8,128)(2,1)}), bf16[8,24,1024]{2,1,0:T(8,128)(2,1)S(1)}, u32[]{:S(2)}, u32[]{:S(2)}) %all-to-all-start.18) | async-done | bytes 393248 | tf_op jit(solution)/shard_map/all_to_all | solution.py:673
  386.8 16.3 %all-to-all-done.19.refs_0_ = bf16[8,72,1024]{2,1,0:T(8,128)(2,1)S(1)} async-done(((bf16[8,72,1024]{2,1,0:T(8,128)(2,1)}), bf16[8,72,1024]{2,1,0:T(8,128)(2,1)S(1)}, u32[]{:S(2)}, u32[]{:S(2)}) %all-to-all-start.19) | async-done | bytes 1179680 | tf_op jit(solution)/shard_map/all_to_all | solution.py:673
  409.3 9.4 %all-to-all-done.20.refs_1_ = bf16[8,160,256]{2,1,0:T(8,128)(2,1)S(1)} async-done(((bf16[8,160,256]{2,1,0:T(8,128)(2,1)}), bf16[8,160,256]{2,1,0:T(8,128)(2,1)S(1)}, u32[]{:S(2)}, u32[]{:S(2)}) %all-to-all-start.20) | async-done | bytes 655392 | tf_op jit(solution)/shard_map/all_to_all | solution.py:673
  427.9 5.7 %all-to-all-start.21 = ((f32[64,24,128]{2,1,0:T(8,128)}), f32[64,24,128]{2,1,0:T(8,128)S(1)}, u32[]{:S(2)}, u32[]{:S(2)}) async-start(f32[64,24,128]{2,1,0:T(8,128)} %broadcast_in_dim.76), calls=%async_computation.21 | async-start | bytes 1572864 | tf_op jit(solution)/shard_map/all_to_all | solution.py:673
  434.6 14.0 %all-to-all-done.21 = f32[64,24,128]{2,1,0:T(8,128)S(1)} async-done(((f32[64,24,128]{2,1,0:T(8,128)}), f32[64,24,128]{2,1,0:T(8,128)S(1)}, u32[]{:S(2)}, u32[]{:S(2)}) %all-to-all-start.21) | async-done | bytes 786464 | tf_op jit(solution)/shard_map/all_to_all | solution.py:673
  (134 shorter events, 134.2 us)
Async XLA Ops:
  7.2 75.6 %all-gather.3.cloned.1.call-start = ((), (), s32[]{:S(2)}) async-start(), calls=%async_computation.23 | async-start | bytes 1179648 | tf_op jit(solution)/shard_map/all_gather | solution.py:716
  11.3 2.6 collective-permute-start
  35.6 25.9 %collective-permute-start.2 = (bf16[1280,256]{1,0:T(8,128)(2,1)S(1)}, bf16[1280,256]{1,0:T(8,128)(2,1)S(1)}, u32[]{:S(2)}, u32[]{:S(2)}) collective-permute-start(bf16[1280,256]{1,0:T(8,128)(2,1)S(1)} %bitcast.50), channel_id=1, source_target_pairs={{0,64},{64,0},{1,65},{65,1},{2,66},{66,2},{3,67},{67,3},{4,68},{68... | collective-permute-start | bytes 1966088 | tf_op jit(solution)/shard_map/ppermute | solution.py:677
  39.5 20.4 %all-to-all-start.1 = ((bf16[8,8,32,128]{3,2,1,0:T(8,128)(2,1)}), bf16[8,8,32,128]{3,2,1,0:T(8,128)(2,1)S(1)}, u32[]{:S(2)}, u32[]{:S(2)}) async-start(bf16[8,8,32,128]{3,2,1,0:T(8,128)(2,1)} %shard_map.155), calls=%async_computation.1 | async-start | bytes 1048576 | tf_op jit(solution)/shard_map/all_to_all | solution.py:673
  46.6 91.7 %all-gather.5.cloned.1.call-start = ((), (), s32[]{:S(2)}) async-start(), calls=%async_computation.24 | async-start | bytes 1769472 | tf_op jit(solution)/shard_map/all_gather | solution.py:785
  60.0 1.4 collective-permute-start.1
  80.7 5.2 %collective-permute-start.3 = (bf16[1536,256]{1,0:T(8,128)(2,1)S(1)}, bf16[1536,256]{1,0:T(8,128)(2,1)}, u32[]{:S(2)}, u32[]{:S(2)}) collective-permute-start(bf16[1536,256]{1,0:T(8,128)(2,1)S(1)} %bitcast.53), channel_id=1, source_target_pairs={{0,64},{64,0},{1,65},{65,1},{2,66},{66,2},{3,67},{67,3},{4,68},{68... | collective-permute-start | bytes 2359304 | tf_op jit(solution)/shard_map/ppermute | solution.py:677
  82.8 28.3 %collective-permute-start.4 = (bf16[1024,512]{1,0:T(8,128)(2,1)}, bf16[1024,512]{1,0:T(8,128)(2,1)S(1)}, u32[]{:S(2)}, u32[]{:S(2)}) collective-permute-start(bf16[1024,512]{1,0:T(8,128)(2,1)} %all-gather.3.cloned.1.call-done.refs_1_.refs_3_), channel_id=1, source_target_pairs={{0,64},{64,0},{1,65},{65,1},{2,66},{66,2},{3,67},{67,3},{4,68},{68... | collective-permute-start | bytes 3145736 | tf_op jit(solution)/shard_map/ppermute | solution.py:677
  85.2 37.3 %copy-start.2 = (bf16[1024,512]{1,0:T(8,128)(2,1)S(1)}, bf16[1024,512]{1,0:T(8,128)(2,1)}, u32[]{:S(2)}) copy-start(bf16[1024,512]{1,0:T(8,128)(2,1)} %all-gather.3.cloned.1.call-done.refs_1_.refs_3_) | copy-start | bytes 3145732
  107.2 15.3 %all-to-all-start.4 = ((bf16[8,24,1024]{2,1,0:T(8,128)(2,1)}), bf16[8,24,1024]{2,1,0:T(8,128)(2,1)S(1)}, u32[]{:S(2)}, u32[]{:S(2)}) async-start(bf16[8,24,1024]{2,1,0:T(8,128)(2,1)} %get-tuple-element.85), calls=%async_computation.4 | async-start | bytes 786432 | tf_op jit(solution)/shard_map/all_to_all | solution.py:673
  138.3 14.2 %collective-permute-start.5 = (bf16[1024,768]{1,0:T(8,128)(2,1)}, bf16[1024,768]{1,0:T(8,128)(2,1)S(1)}, u32[]{:S(2)}, u32[]{:S(2)}) collective-permute-start(bf16[1024,768]{1,0:T(8,128)(2,1)} %all-gather.5.cloned.1.call-done.refs_1_.refs_3_), channel_id=1, source_target_pairs={{0,64},{64,0},{1,65},{65,1},{2,66},{66,2},{3,67},{67,3},{4,68},{68... | collective-permute-start | bytes 4718600 | tf_op jit(solution)/shard_map/ppermute | solution.py:677
  168.7 4.9 %collective-permute-start.6 = (bf16[1536,256]{1,0:T(8,128)(2,1)S(1)}, bf16[1536,256]{1,0:T(8,128)(2,1)S(1)}, u32[]{:S(2)}, u32[]{:S(2)}) collective-permute-start(bf16[1536,256]{1,0:T(8,128)(2,1)S(1)} %bitcast.55), channel_id=1, source_target_pairs={{0,64},{64,0},{1,65},{65,1},{2,66},{66,2},{3,67},{67,3},{4,68},{68... | collective-permute-start | bytes 2359304 | tf_op jit(solution)/shard_map/ppermute | solution.py:677
  173.6 28.0 %copy-start.1 = (bf16[1024,768]{1,0:T(8,128)(2,1)S(1)}, bf16[1024,768]{1,0:T(8,128)(2,1)}, u32[]{:S(2)}) copy-start(bf16[1024,768]{1,0:T(8,128)(2,1)} %all-gather.5.cloned.1.call-done.refs_1_.refs_3_) | copy-start | bytes 4718596
  220.4 11.2 %all-to-all-start.11 = ((bf16[8,24,1024]{2,1,0:T(8,128)(2,1)}), bf16[8,24,1024]{2,1,0:T(8,128)(2,1)S(1)}, u32[]{:S(2)}, u32[]{:S(2)}) async-start(bf16[8,24,1024]{2,1,0:T(8,128)(2,1)} %get-tuple-element.103), calls=%async_computation.11 | async-start | bytes 786432 | tf_op jit(solution)/shard_map/all_to_all | solution.py:673
  236.8 7.2 %collective-permute-start.7 = (bf16[1536,256]{1,0:T(8,128)(2,1)S(1)}, bf16[1536,256]{1,0:T(8,128)(2,1)S(1)}, u32[]{:S(2)}, u32[]{:S(2)}) collective-permute-start(bf16[1536,256]{1,0:T(8,128)(2,1)S(1)} %get-tuple-element.107), channel_id=1, source_target_pairs={{0,64},{64,0},{1,65},{65,1},{2,66},{66,2},{3,67},{67,3},{4,68},{68... | collective-permute-start | bytes 2359304 | tf_op jit(solution)/shard_map/ppermute | solution.py:677
  260.5 11.2 %all-to-all-start.13 = ((bf16[8,24,1024]{2,1,0:T(8,128)(2,1)}), bf16[8,24,1024]{2,1,0:T(8,128)(2,1)S(1)}, u32[]{:S(2)}, u32[]{:S(2)}) async-start(bf16[8,24,1024]{2,1,0:T(8,128)(2,1)} %bitcast.21), calls=%async_computation.13 | async-start | bytes 786432 | tf_op jit(solution)/shard_map/all_to_all | solution.py:673
  274.5 11.2 %all-to-all-start.14 = ((bf16[8,24,1024]{2,1,0:T(8,128)(2,1)}), bf16[8,24,1024]{2,1,0:T(8,128)(2,1)S(1)}, u32[]{:S(2)}, u32[]{:S(2)}) async-start(bf16[8,24,1024]{2,1,0:T(8,128)(2,1)} %get-tuple-element.112), calls=%async_computation.14 | async-start | bytes 786432 | tf_op jit(solution)/shard_map/all_to_all | solution.py:673
  277.9 142.0 %reduce-scatter.2.cloned.1.call-start = ((), (), s32[]{:S(2)}) async-start(), calls=%async_computation.25 | async-start | bytes 2949120 | tf_op jit(solution)/shard_map/reduce_scatter | solution.py:819
  278.0 32.4 %collective-permute-start.9 = (bf16[1024,512]{1,0:T(8,128)(2,1)S(1)}, bf16[1024,512]{1,0:T(8,128)(2,1)S(1)}, u32[]{:S(2)}, u32[]{:S(2)}) collective-permute-start(bf16[1024,512]{1,0:T(8,128)(2,1)S(1)} %get-tuple-element.119), channel_id=1, source_target_pairs={{0,64},{64,0},{1,65},{65,1},{2,66},{66,2},{3,67},{67,3},{4,68},{68... | collective-permute-start | bytes 3145736 | tf_op jit(solution)/shard_map/ppermute | solution.py:677
  291.9 18.4 %collective-permute-start.8 = (bf16[1024,512]{1,0:T(8,128)(2,1)S(1)}, bf16[1024,512]{1,0:T(8,128)(2,1)S(1)}, u32[]{:S(2)}, u32[]{:S(2)}) collective-permute-start(bf16[1024,512]{1,0:T(8,128)(2,1)S(1)} %get-tuple-element.118), channel_id=1, source_target_pairs={{0,64},{64,0},{1,65},{65,1},{2,66},{66,2},{3,67},{67,3},{4,68},{68... | collective-permute-start | bytes 3145736 | tf_op jit(solution)/shard_map/ppermute | solution.py:677
  296.6 13.7 %collective-permute-start.10 = (bf16[1024,256]{1,0:T(8,128)(2,1)S(1)}, bf16[1024,256]{1,0:T(8,128)(2,1)S(1)}, u32[]{:S(2)}, u32[]{:S(2)}) collective-permute-start(bf16[1024,256]{1,0:T(8,128)(2,1)S(1)} %copy-done.15), channel_id=1, source_target_pairs={{0,64},{64,0},{1,65},{65,1},{2,66},{66,2},{3,67},{67,3},{4,68},{68... | collective-permute-start | bytes 1572872 | tf_op jit(solution)/shard_map/ppermute | solution.py:677
  330.8 8.1 %collective-permute-start.11 = (bf16[1536,256]{1,0:T(8,128)(2,1)S(1)}, bf16[1536,256]{1,0:T(8,128)(2,1)S(1)}, u32[]{:S(2)}, u32[]{:S(2)}) collective-permute-start(bf16[1536,256]{1,0:T(8,128)(2,1)S(1)} %get-tuple-element.124), channel_id=1, source_target_pairs={{0,64},{64,0},{1,65},{65,1},{2,66},{66,2},{3,67},{67,3},{4,68},{68... | collective-permute-start | bytes 2359304 | tf_op jit(solution)/shard_map/ppermute | solution.py:677
  360.5 15.8 %all-to-all-start.18 = ((bf16[8,24,1024]{2,1,0:T(8,128)(2,1)}), bf16[8,24,1024]{2,1,0:T(8,128)(2,1)S(1)}, u32[]{:S(2)}, u32[]{:S(2)}) async-start(bf16[8,24,1024]{2,1,0:T(8,128)(2,1)} %bitcast.26), calls=%async_computation.18 | async-start | bytes 786432 | tf_op jit(solution)/shard_map/all_to_all | solution.py:673
  376.3 32.4 %copy-start.13 = (s32[3]{0:T(128)S(1)}, s32[3]{0:T(128)}, u32[]{:S(2)}) copy-start(s32[3]{0:T(128)} %refs_2_.3) | copy-start | bytes 40
  376.3 42.4 %copy-start.7 = (bf16[1,1024,6,16]{1,3,2,0:T(8,128)(2,1)S(1)}, bf16[1,1024,6,16]{1,3,2,0:T(8,128)(2,1)}, u32[]{:S(2)}) copy-start(bf16[1,1024,6,16]{1,3,2,0:T(8,128)(2,1)} %param.15) | copy-start | bytes 589828
  377.7 2.5 collective-permute-start.12
  381.3 21.8 %all-to-all-start.19 = ((bf16[8,72,1024]{2,1,0:T(8,128)(2,1)}), bf16[8,72,1024]{2,1,0:T(8,128)(2,1)S(1)}, u32[]{:S(2)}, u32[]{:S(2)}) async-start(bf16[8,72,1024]{2,1,0:T(8,128)(2,1)} %shard_map.184), calls=%async_computation.19 | async-start | bytes 2359296 | tf_op jit(solution)/shard_map/all_to_all | solution.py:673
  384.9 2.0 collective-permute-start.13
  405.1 13.5 %all-to-all-start.20 = ((bf16[8,160,256]{2,1,0:T(8,128)(2,1)}), bf16[8,160,256]{2,1,0:T(8,128)(2,1)S(1)}, u32[]{:S(2)}, u32[]{:S(2)}) async-start(bf16[8,160,256]{2,1,0:T(8,128)(2,1)} %get-tuple-element.133), calls=%async_computation.20 | async-start | bytes 1310720 | tf_op jit(solution)/shard_map/all_to_all | solution.py:673
  421.8 11.9 %collective-permute-start.15 = (bf16[128,768]{1,0:T(8,128)(2,1)S(1)}, bf16[128,768]{1,0:T(8,128)(2,1)S(1)}, u32[]{:S(2)}, u32[]{:S(2)}) collective-permute-start(bf16[128,768]{1,0:T(8,128)(2,1)S(1)} %pad_maximum_fusion.1), channel_id=1, source_target_pairs={{0,64},{64,0},{1,65},{65,1},{2,66},{66,2},{3,67},{67,3},{4,68},{68... | collective-permute-start | bytes 589832 | tf_op jit(solution)/shard_map/ppermute | solution.py:677
  425.0 2.0 collective-permute-start.14
  427.9 20.7 %all-to-all-start.21 = ((f32[64,24,128]{2,1,0:T(8,128)}), f32[64,24,128]{2,1,0:T(8,128)S(1)}, u32[]{:S(2)}, u32[]{:S(2)}) async-start(f32[64,24,128]{2,1,0:T(8,128)} %broadcast_in_dim.76), calls=%async_computation.21 | async-start | bytes 1572864 | tf_op jit(solution)/shard_map/all_to_all | solution.py:673
  (12 other events, 22.6 us)
Sparse Core Ops, SparseCore 0:
  19.7 43.6 all-gather.2
  65.7 55.5 all-gather.4
  314.1 73.5 reduce-scatter.1

commit v3 on v2

--- a/solution.py
+++ b/solution.py
@@ -110,7 +110,7 @@
             r.ready()
 
 
-def call(store, kernel, outs, *args):
+def call(store, kernel, outs, *args, alone=False):
     vmem = pl.BlockSpec(memory_space=pltpu.VMEM)
     smem = pl.BlockSpec(memory_space=pltpu.SMEM)
     far = pl.BlockSpec(memory_space=pltpu.HBM)
@@ -143,6 +143,10 @@
     for o in outs:
         if isinstance(o, Slot):
             out_plan.append((o, hold((o.rows, o.shape[1]), bf16)))
+        elif alone:
+            out_plan.append((len(out_shape), hold(*o)))
+            out_shape.append(sds(*o))
+            out_specs.append(far)
         else:
             out_plan.append((None, len(out_shape)))
             out_shape.append(sds(*o))
@@ -213,8 +217,12 @@
             if slot is None:
                 given.append(results[at])
             else:
-                copy = pltpu.make_async_copy(holds[at], slot.of(big), sems.at[at])
-                kept = Kept(holds[at], copy, slot.shape, slot.dtype)
+                if isinstance(slot, Slot):
+                    copy = pltpu.make_async_copy(holds[at], slot.of(big), sems.at[at])
+                    kept = Kept(holds[at], copy, slot.shape, slot.dtype)
+                else:
+                    copy = pltpu.make_async_copy(holds[at], results[slot], sems.at[at])
+                    kept = Kept(holds[at], copy, None, None)
                 leaving.append(copy)
                 given.append(kept)
         kernel(*given)
@@ -232,7 +240,7 @@
         out_specs=tuple(out_specs),
         scratch_shapes=scratch + ([pltpu.SemaphoreType.DMA((n_sems,))] if n_sems else []),
         input_output_aliases=alias,
-        compiler_params=pltpu.CompilerParams(vmem_limit_bytes=24 * 1024 * 1024),
+        compiler_params=pltpu.CompilerParams(vmem_limit_bytes=(60 if alone else 24) * 1024 * 1024),
     )(*flat)
     if uses:
         store.array = got[n_out]
@@ -313,21 +321,12 @@
 def k_halves(p_ref, wq_ref, wo_ref, up_ref, down_ref, keep_ref, send_ref):
     ready(wq_ref, wo_ref, up_ref, down_ref)
 
-    def put(a_ref, b_ref):
-        for k in range(2):
-            a_ref[:, 128 * k : 128 * k + 128] = wq_ref[k]
-        a_ref[:, 256:] = up_ref[...]
-        b_ref[:, :128] = wq_ref[2]
-        b_ref[:, 128:256] = wo_ref[...].astype(f32).T.astype(bf16)
-        b_ref[:, 256:] = down_ref[...].astype(f32).T.astype(bf16)
-
-    @pl.when(p_ref[0] == 0)
-    def _():
-        put(keep_ref, send_ref)
-
-    @pl.when(p_ref[0] == 1)
-    def _():
-        put(send_ref, keep_ref)
+    a = jnp.concatenate([wq_ref[0], wq_ref[1], up_ref[...]], axis=1).astype(f32)
+    wo, down = wo_ref[...].astype(f32).T, down_ref[...].astype(f32).T
+    b = jnp.concatenate([wq_ref[2].astype(f32), wo, down], axis=1)
+    first = p_ref[0] == 0
+    send_ref[...] = jnp.where(first, b, a).astype(bf16)
+    keep_ref[...] = jnp.where(first, a, b).astype(bf16)
 
 
 def k_pack(
@@ -346,11 +345,14 @@
     cond_ref[...] = cond
     act = (cond / (1.0 + jnp.exp(-cond))).astype(bf16)
     act_ref[...] = act
-    lane = lax.broadcasted_iota(jnp.int32, (16, 256), 1)
-    row = lax.broadcasted_iota(jnp.int32, (16, 256), 0)
-    place = jnp.where(lane == row + 16 * t_ref[0], 1.0, 0.0).astype(bf16)
-    mod = [mm(mm_nt(act, ada_ref[16 * k : 16 * k + 16]).astype(bf16), place) for k in range(6)]
-    mod = jnp.concatenate(mod + [jnp.zeros((14, 256), f32)], axis=0).astype(bf16)
+    row = lax.broadcasted_iota(jnp.int32, (96, 768), 0)
+    lane = lax.broadcasted_iota(jnp.int32, (96, 768), 1)
+    to = 128 * (row // 16) + row % 16 + 16 * t_ref[0]
+    place = jnp.where(lane == to, 1.0, 0.0).astype(bf16)
+    mod = mm(mm_nt(act, ada_ref[...]).astype(bf16), place)
+    mod = jnp.concatenate([mod[:, 128 * k : 128 * k + 128] for k in range(6)], axis=0)
+    mod = jnp.concatenate([mod, jnp.zeros((14, 128), f32)], axis=0)
+    mod = jnp.concatenate([mod, jnp.zeros((32, 128), f32)], axis=1).astype(bf16)
     for j in range(8):
         o_ref[j, :128] = w0[:, :256]
         o_ref[j, 128:] = mod
@@ -358,7 +360,7 @@
 
 def k_spread(r_ref, o_ref):
     for c in range(8):
-        v = r_ref[c, 128:, :128]
+        v = r_ref[c, 128:, :128][:24]
         for j in range(8):
             o_ref[j, c] = v
 
@@ -385,21 +387,23 @@
     return jnp.concatenate([a, mm(n, rows_of(wb_ref[...])[:, :128])], axis=1)
 
 
-def own_blocks(p_ref, t_ref, x_ref, own_ref):
+def k_rows(p_ref, t_ref, x_ref, c_ref, x_all_ref, x_own_ref, c_all_ref, c_own_ref):
     start = pl.multiple_of(64 * p_ref[0], 64)
     few = pl.multiple_of(64 * p_ref[0] + 8 * t_ref[0], 8)
-    own_ref[...] = jnp.concatenate([x_ref[l, pl.ds(few, 8), :] for l in range(LAT)], axis=0)
-    blocks = [x_ref[l, pl.ds(start, 64), :] for l in range(LAT)]
-    return [
-        jnp.concatenate([b[8 * j : 8 * j + 8] for b in blocks], axis=0) for j in range(8)
-    ]
-
-
-def k_first(p_ref, t_ref, x_ref, mod_ref, wa_ref, wb_ref, own_ref, n_ref, q_ref, kv_ref):
+    ready(x_ref, c_ref)
+    for ref, all_ref, own_ref in ((x_ref.ref, x_all_ref, x_own_ref), (c_ref.ref, c_all_ref, c_own_ref)):
+        blocks = [ref[l, pl.ds(start, 64), :] for l in range(LAT)]
+        all_ref[...] = jnp.concatenate(
+            [b[8 * j : 8 * j + 8] for j in range(8) for b in blocks], axis=0
+        )
+        own_ref[...] = jnp.concatenate([ref[l, pl.ds(few, 8), :] for l in range(LAT)], axis=0)
+
+
+def k_first(x_ref, mod_ref, wa_ref, wb_ref, n_ref, q_ref, kv_ref):
     mod = mod_ref[...].astype(f32)
     shift, scale = part(mod, 0), 1.0 + part(mod, 1)
-    x_ref.ready()
-    rows = [centred(x)[0] * scale + shift for x in own_blocks(p_ref, t_ref, x_ref.ref, own_ref)]
+    x = x_ref[...]
+    rows = [centred(x[24 * j : 24 * j + 24])[0] * scale + shift for j in range(8)]
     n = jnp.concatenate(rows, axis=0).astype(bf16)
     n_ref[...] = n
     put_qkv(triple(n, wa_ref, wb_ref), q_ref, kv_ref)
@@ -429,9 +433,9 @@
 
 
 def soft(qs, k):
-    s = mm_nt(qs, k) * 0.125
-    e = jnp.exp(s - jnp.max(s, axis=-1, keepdims=True))
-    return e / jnp.sum(e, axis=-1, keepdims=True)
+    s = mm_nt(k, qs) * 0.125
+    e = jnp.exp(s - jnp.max(s, axis=0, keepdims=True))
+    return e * (1.0 / jnp.sum(e, axis=0, keepdims=True))
 
 
 def k_attn(q_ref, a_ref, b_ref, w_ref, att_ref, o_ref):
@@ -439,7 +443,7 @@
     for l in range(LAT):
         k, v = keys_values(a_ref, b_ref, l)
         probs = soft(head_rows(q_ref[64 * l : 64 * l + 64].astype(f32)).astype(bf16), k)
-        outs.append(head_lanes(mm(probs.astype(bf16), v)))
+        outs.append(head_lanes(mm_tn(probs.astype(bf16), v)))
     att = by_part(outs).astype(bf16)
     att_ref[...] = att
     o_ref[...] = mm_nt(att, rows_of(w_ref[...])[:, 128:]).astype(bf16)
@@ -452,12 +456,12 @@
         qs = head_rows(q_ref[64 * l : 64 * l + 64].astype(f32)).astype(bf16)
         do = head_rows(datt[l]).astype(bf16)
         probs = soft(qs, k)
-        dprobs = mm_nt(do, v)
-        dv = mm_tn(probs.astype(bf16), do)
-        ds = probs * (dprobs - jnp.sum(probs * dprobs, axis=-1, keepdims=True))
+        dprobs = mm_nt(v, do)
+        dv = mm(probs.astype(bf16), do)
+        ds = probs * (dprobs - jnp.sum(probs * dprobs, axis=0, keepdims=True))
         ds = ds.astype(bf16)
-        dk = mm_tn(ds, qs) * 0.125
-        dq_ref[64 * l : 64 * l + 64] = (head_lanes(mm(ds, k)) * 0.125).astype(bf16)
+        dk = mm(ds, qs) * 0.125
+        dq_ref[64 * l : 64 * l + 64] = (head_lanes(mm_tn(ds, k)) * 0.125).astype(bf16)
         dkv = jnp.concatenate([dk, dv], axis=1).astype(bf16)
         for c in range(8):
             at = 64 * (LAT * c + l)
@@ -522,10 +526,10 @@
     o_ref[...] = mm_nt(dpre, rows_of(up_ref[...])).astype(bf16)
 
 
-def k_gate_rows(p_ref, t_ref, c_ref, mod_ref, own_ref, o_ref):
+def k_gate_rows(c_ref, mod_ref, o_ref):
     gate = part(mod_ref[...].astype(f32), 5)
-    c_ref.ready()
-    rows = [gate * c for c in own_blocks(p_ref, t_ref, c_ref.ref, own_ref)]
+    c = c_ref[...]
+    rows = [gate * c[24 * j : 24 * j + 24] for j in range(8)]
     o_ref[...] = jnp.concatenate(rows, axis=0).astype(bf16)
 
 
@@ -606,12 +610,12 @@
     for j in range(1, 8):
         total = total + r_ref[j].astype(f32)[48:]
     total = jnp.concatenate([total, jnp.zeros((8, total.shape[1]), f32)], axis=0).astype(bf16)
-    both = (a_ref[...].astype(f32) + b_ref[...].astype(f32)).astype(bf16)
     none = jnp.zeros((32, 128), bf16)
     for c in range(8):
-        o_ref[c, :128, :] = both[128 * c : 128 * c + 128]
-        o_ref[c, 128:, :128] = total[:, 128 * c : 128 * c + 128]
-        o_ref[c, 128:, 128:] = none
+        at = slice(128 * c, 128 * c + 128)
+        o_ref[c, :128, :] = (a_ref[at].astype(f32) + b_ref[at].astype(f32)).astype(bf16)
+        o_ref[c, 128:160, :128] = total[:, at]
+        o_ref[c, 128:160, 128:] = none
 
 
 def k_ends(r_ref, o_ref):
@@ -623,21 +627,42 @@
                 o_ref[l, at : at + 8, :] = v[24 * half + 8 * l : 24 * half + 8 * l + 8]
 
 
-def k_cond(t_ref, r_ref, act_ref, ada_ref, g_ref, ada_grad_ref, c_ref):
+def k_cond(t_ref, r_ref, act_ref, ada_ref, g_ref, ada_grad_ref, o_ref):
     total = summed(r_ref)
-    g_ref[...] = total[:128].astype(bf16)
     d = total[128:, :128].astype(bf16)
     lane = lax.broadcasted_iota(jnp.int32, (128, 16), 0)
     col = lax.broadcasted_iota(jnp.int32, (128, 16), 1)
     pick = jnp.where(lane == col + 16 * t_ref[0], 1.0, 0.0).astype(bf16)
     d = mm(d, pick)
     act = act_ref[...]
-    c = jnp.zeros(c_ref.shape, f32)
+    c = jnp.zeros(act.shape, f32)
     for k in range(6):
         dk = d[3 * k : 3 * k + 3].astype(bf16)
         ada_grad_ref[16 * k : 16 * k + 16, :] = mm_tn(dk, act)
         c = c + mm(dk, ada_ref[16 * k : 16 * k + 16, :])
-    c_ref[...] = c
+    v = [c[l : l + 1, 128 * k : 128 * k + 128] for l in range(LAT) for k in range(8)]
+    v = jnp.concatenate(v, axis=0).astype(bf16)
+    for j in range(64):
+        o_ref[j] = v
+    g_ref[...] = total[:128].astype(bf16)
+
+
+def k_final_send(p_ref, m0_ref, m1_ref, o_ref):
+    m0, m1 = m0_ref[...].astype(f32), m1_ref[...].astype(f32)
+    o_ref[:, :512] = jnp.where(p_ref[0] == 0, m1[:, :512], m0).astype(bf16)
+    o_ref[:, 512:] = m1[:, 512:].astype(bf16)
+
+
+def k_final(p_ref, m0_ref, m1_ref, a_ref, g_ref, b_ref, up_ref, down_ref, qkv_ref, out_ref):
+    first = p_ref[0] == 0
+    m0, m1, a = (r[...].astype(f32) for r in (m0_ref, m1_ref, a_ref))
+    g, b = g_ref[...].astype(f32), b_ref[...].astype(f32)
+    up_ref[...] = jnp.where(first, m0, a[:, :512])
+    down_ref[...] = jnp.where(first, a[:, :512], m1[:, :512]).T
+    qk = jnp.where(first, g, a[:, 512:])
+    vo = jnp.where(first, b, m1[:, 512:])
+    qkv_ref[0], qkv_ref[1], qkv_ref[2] = qk[:, :128], qk[:, 128:], vo[:, :128]
+    out_ref[...] = vo[:, 128:].T
 
 
 def k_grad_mlp(p_ref, n_ref, dpre_ref, dm_ref, hid_ref, keep_ref, send_ref):
@@ -661,9 +686,9 @@
     keep_ref[...] = jnp.where(first, qk, vo).astype(bf16)
 
 
-def k_grad_sum(a_ref, b_ref, c_ref, d_ref, e_ref, f_ref, o_ref):
-    at = 0
-    for keep, got in ((a_ref, b_ref), (c_ref, d_ref), (e_ref, f_ref)):
+def k_grad_sum(*refs):
+    o_ref, at = refs[-1], 0
+    for keep, got in zip(refs[0:-1:2], refs[1:-1:2]):
         v = (keep[...].astype(f32) + got[...].astype(f32)).astype(bf16)
         o_ref[:, at : at + v.shape[1]] = v
         at += v.shape[1]
@@ -677,28 +702,21 @@
     return lax.ppermute(x, "pipe", [(0, 1), (1, 0)])
 
 
-def copies(x, n):
-    return jnp.broadcast_to(x[None], (n, *x.shape))
-
-
 def body(latents, cotangent, labels, steps, label_table, w_ada, w_qkv, w_out, w_up, w_down):
     p, t = lax.axis_index("pipe"), lax.axis_index("tp")
-    first = p == 0
     who, part_no = p.astype(jnp.int32).reshape(1), t.astype(jnp.int32).reshape(1)
     width = latents.shape[2]
 
-    def of_layer(own, other):
-        return jnp.where(first, own, other), jnp.where(first, other, own)
-
     store = Store()
     slot = store.slot
 
-    def run(kernel, outs, *args):
-        return call(store, kernel, outs, *args)
+    def run(kernel, outs, *args, alone=False):
+        return call(store, kernel, outs, *args, alone=alone)
 
     keep, send = run(
         k_halves, [((128, 768), bf16)] * 2,
         who, Near(w_qkv[0].transpose(1, 0, 2)), Near(w_out[0]), Near(w_up[0]), Near(w_down[0]),
+        alone=True,
     )
     half = width // 2
     freq = jnp.exp(-math.log(10000.0) * jnp.arange(half, dtype=f32) / half)
@@ -711,18 +729,24 @@
             ((8, 160, 256), bf16), ((128, 512), bf16), ((128, 768), bf16),
             ((LAT, width), f32), ((LAT, width), bf16),
         ],
-        who, part_no, labels, label_table, sinus, ada, keep, swap(send),
+        who, part_no, labels, Near(label_table), Near(sinus), Near(ada), Near(keep), Near(swap(send)),
+        alone=True,
     )
     w0 = lax.all_gather(w0, "ctx", axis=0, tiled=True)
     packed = exchange(packed, "ctx")
-    (spread,) = run(k_spread, [((8, 8, 32, 128), bf16)], packed)
+    packed, latents, cotangent = lax.optimization_barrier((packed, latents, cotangent))
+    (spread,) = run(k_spread, [((8, 8, 24, 128), bf16)], packed)
     packed = packed.reshape(1280, 256)
     packed_other = swap(packed)
     sa = [[slot((1024, 256), bf16) for _ in range(2)] for _ in range(2)]
     sm = [[slot((1024, 512), bf16) for _ in range(2)] for _ in range(2)]
     wa0 = [Half(c, packed, packed_other, 160, 128, 0, 256, sa[0][c]) for c in range(2)]
-    (mod_own,) = run(k_mods, [((32, 1024), bf16)], exchange(spread, "tp"))
-    mods = run(k_two_layers, [((32, 1024), bf16)] * 2, who, mod_own, swap(mod_own))
+    x_all, x0 = slot((192, 1024), f32), slot((24, 1024), f32)
+    cot_all, cot = slot((192, 1024), f32), slot((24, 1024), f32)
+    run(k_rows, [x_all, x0, cot_all, cot], who, part_no, Near(latents), Near(cotangent), alone=True)
+    spread, store.array = lax.optimization_barrier((exchange(spread, "tp"), store.array))
+    (mod_own,) = run(k_mods, [((24, 1024), bf16)], spread)
+    mods = run(k_two_layers, [((24, 1024), bf16)] * 2, who, mod_own, swap(mod_own))
 
     bc = ((8, 24, 1024), bf16)
     wide = ((192, 1024), bf16)
@@ -751,24 +775,20 @@
         arrived = exchange(dn.reshape(8, 24, 1024), "tp")
         keep = slot((1024, 256), bf16)
         (send,) = run(k_grad_attn, [keep, ((1024, 256), bf16)], who, normed, dt, db, att)
-        return arrived, keep, swap(send)
+        return arrived, (keep, swap(send))
 
     def grads_mlp(n, dpre, dm, hid):
         keep = slot((1024, 512), bf16)
         (send,) = run(k_grad_mlp, [keep, ((1024, 512), bf16)], who, n, dpre, dm, hid)
-        return keep, swap(send)
+        return keep, send
 
     def to_rows(x):
         return exchange(x, "tp").reshape(192, 1024)
 
-    x0, normed0, q0 = rows24(), rows192(1024), rows192(128)
-    (kv,) = run(
-        k_first, [x0, normed0, q0, ((8, 192, 256), bf16)],
-        who, part_no, Near(latents), mods[0], *wa0,
-    )
+    normed0, q0, dm1 = rows192(1024), rows192(128), rows192(1024)
+    (kv,) = run(k_first, [normed0, q0, ((8, 192, 256), bf16)], x_all, mods[0], *wa0)
     wa0 = sa[0]
-    cot, dm1 = rows24(), rows192(1024)
-    run(k_gate_rows, [cot, dm1], who, part_no, Near(cotangent), mods[1])
+    run(k_gate_rows, [dm1], cot_all, mods[1])
     kept0, arrived = attn_forward(q0, kv, wa0)
     br0, mid0 = rows24(), rows24()
     (n2,) = run(k_mid, [br0, mid0, bc], arrived, x0, mods[0])
@@ -802,24 +822,27 @@
     arrived = exchange(both, "tp")
     res1, dmid1, dmod1a = rows24(), rows24(), rows24(12)
     (db,) = run(k_last, [res1, dmid1, dmod1a, bc], arrived, mid1, br1, cot, mods[1])
-    gm1 = grads_mlp(n2_1, dpre1, dm1, hid1)
-
-    arrived, *ga1 = attn_back(kept1, normed1, to_rows(db), wa1)
+    gm1, send = grads_mlp(n2_1, dpre1, dm1, hid1)
+    gm1 = gm1, swap(send)
+
+    arrived, ga1 = attn_back(kept1, normed1, to_rows(db), wa1)
     dx1, dmod1b = rows24(), rows24(6)
     (dm,) = run(k_back_one, [dx1, dmod1b, bc], arrived, x1, dmid1, mods[1], mods[0])
+    (mixed,) = run(k_grad_sum, [((1024, 768), bf16)], *gm1, *ga1)
+    mixed = lax.psum_scatter(mixed, "ctx", tiled=True)
     dm = to_rows(dm)
 
     dm0, dpre0 = rows192(1024), rows192(512)
     (dn,) = run(k_mlp_back, [dpre0, wide], n2_0, *wm0, Save(dm, dm0))
     arrived = exchange(dn.reshape(8, 24, 1024), "tp")
-    gm0 = grads_mlp(n2_0, dpre0, dm0, hid0)
+    gm0, send = grads_mlp(n2_0, dpre0, dm0, hid0)
     dmid0, dmod0a = rows24(), rows24(12)
     (db,) = run(k_back_two, [dmid0, dmod0a, bc], arrived, mid0, br0, dx1, mlp0, mods[0])
-    (mixed,) = run(k_grad_sum, [((1024, 1280), bf16)], *gm0, *gm1, *ga1)
-    mixed = lax.psum_scatter(mixed, "ctx", tiled=True)
-    gm0, gm1, ga1 = mixed[:, :512], mixed[:, 512:1024], mixed[:, 1024:]
-
-    arrived, *ga0 = attn_back(kept0, normed0, to_rows(db), wa0)
+    db, send = lax.optimization_barrier((db, send))
+    (mixed0,) = run(k_grad_sum, [((1024, 512), bf16)], gm0, swap(send))
+    mixed0 = lax.psum_scatter(mixed0, "ctx", tiled=True)
+    arrived, ga0 = attn_back(kept0, normed0, to_rows(db), wa0)
+    arrived, mixed = lax.optimization_barrier((arrived, mixed))
     keep, send = run(
         k_back_first, [((48, 1024), f32)] * 2,
         who, arrived, x0, dmid0, mods[0], dmod0a, dmod1a, dmod1b, res1,
@@ -827,39 +850,39 @@
 
     (tail,) = run(k_tail_tp, [((8, 72, 1024), bf16)], who, keep, swap(send))
     tail = exchange(tail, "tp")
+    tail, gm0 = lax.optimization_barrier((tail, mixed0))
     (tail_ctx,) = run(k_tail_ctx, [((8, 160, 256), bf16)], tail, *ga0)
     tail_ctx = exchange(tail_ctx, "ctx")
+    ga0, grad_ada, spread = run(
+        k_cond, [((128, 256), bf16), ((96, 1024), f32), ((64, 24, 128), bf16)],
+        part_no, tail_ctx, cond_act, ada,
+    )
+    grad_act = exchange(spread, ("ctx", "tp"))
+    tail, ga0, gm0 = lax.optimization_barrier((tail, ga0, gm0))
     (ends,) = run(k_ends, [((LAT, 128, 1024), f32)], tail)
-    ga0, grad_ada, cond_part = run(
-        k_cond, [((128, 256), bf16), ((96, 1024), f32), ((LAT, 1024), f32)],
-        part_no, tail_ctx, cond_act, ada,
-    )
-    cond_part = (cond_part + swap(cond_part)).reshape(24, 128)
-    grad_act = exchange(copies(cond_part, 64), ("ctx", "tp"))
-    mine = jnp.concatenate([jnp.where(first, gm0, gm1), jnp.where(first, ga0, ga1)], axis=1)
-    send = jnp.concatenate([jnp.where(first, gm1, gm0), jnp.where(first, ga1, ga0)], axis=1)
-    half0, half1 = of_layer(mine, swap(send))
-    grad_up = half0[:, :512].astype(f32)
-    grad_down = half1[:, :512].astype(f32).T
-    grad_qkv = jnp.concatenate([half0[:, 512:], half1[:, 512:640]], axis=1).astype(f32)
-    grad_out = half1[:, 640:].astype(f32).T
-
-    grad_act, grad_up, grad_down, grad_qkv, grad_out = lax.optimization_barrier(
-        (grad_act, grad_up, grad_down, grad_qkv, grad_out)
-    )
-    grad_act = grad_act.sum(axis=0).reshape(LAT, width)
-    sig = jax.nn.sigmoid(condition)
-    grad_cond = grad_act * (sig * (1.0 + condition * (1.0 - sig)))
+
+    (send,) = run(k_final_send, [((128, 768), bf16)], who, gm0, mixed)
+    grad_up, grad_down, grad_qkv, grad_out = run(
+        k_final,
+        [((128, 512), f32), ((512, 128), f32), ((3, 128, 128), f32), ((128, 128), f32)],
+        who, gm0, mixed, swap(send), ga0, swap(ga0),
+    )
     classes = jnp.arange(label_table.shape[0], dtype=jnp.int32)[:, None]
-    grad_table = sum(
-        jnp.where(classes == labels[l], grad_cond[l : l + 1], 0.0) for l in range(LAT)
-    )
+    match = [classes == labels[l] for l in range(LAT)]
+    slope = jax.nn.sigmoid(condition)
+    slope = slope * (1.0 + condition * (1.0 - slope))
+    grad_act, ends, grad_up, grad_down, grad_qkv, grad_out, match, slope = lax.optimization_barrier(
+        (grad_act, ends, grad_up, grad_down, grad_qkv, grad_out, match, slope)
+    )
+    grad_act = grad_act.astype(f32).sum(axis=0)
+    grad_cond = (grad_act + swap(grad_act)).reshape(LAT, width) * slope
+    grad_table = sum(jnp.where(match[l], grad_cond[l : l + 1], 0.0) for l in range(LAT))
 
     return (
         ends[None],
         grad_table,
         grad_ada.reshape(6, 16, width).transpose(2, 0, 1)[None],
-        grad_qkv.reshape(1, 128, 3, 128),
+        grad_qkv.transpose(1, 0, 2)[None],
         grad_out[None],
         grad_up[None],
         grad_down[None],

time: 463 us -> 448 us (0.968)
  blocking collectives: 175 us -> 144 us
  waiting for transfers between devices: 95.6 us -> 109 us
  local copies, waits for them, and re-layouts: 15.7 us -> 2.73 us
  Pallas kernels: 76.4 us -> 88 us
  starting transfers between devices: 74.8 us -> 80.8 us
    all_to_all x13 -> x11, blocking collectives: 175 us -> 144 us  [exchange(): return lax.all_to_all(x, axis, 0, 0, tiled=True)]
    unnamed x35 -> x20, local copies, waits for them, and re-layouts: 14 us -> 2.12 us
    pallas_call x35 -> x39, Pallas kernels: 76.4 us -> 88 us  [call(): pl.pallas_call(wrapped, out_shape=tuple(out_shape), in_specs=in_specs, ou...]
    all_to_all x9 -> x11, waiting for transfers between devices: 84.6 us -> 94.5 us  [exchange(): return lax.all_to_all(x, axis, 0, 0, tiled=True)]
    all_to_all x9 -> x11, starting transfers between devices: 38.8 us -> 48.4 us  [exchange(): return lax.all_to_all(x, axis, 0, 0, tiled=True)]
    ppermute x16 -> x17, starting transfers between devices: 35.9 us -> 32.2 us  [swap(): return lax.ppermute(x, 'pipe', [(0, 1), (1, 0)])]
    ppermute x16 -> x17, waiting for transfers between devices: 10.2 us -> 9.55 us  [swap(): return lax.ppermute(x, 'pipe', [(0, 1), (1, 0)])]
  transfers between devices with their start and end apart: 28 -> 32, of which waited for: 17 -> 19; matrix products, arithmetic and copies ran while one was open for 1% -> 1% of each run, Pallas kernels for 10% -> 13%
where the time goes in v3:
time: 448 us; the launch traced here: 446 us
  blocking collectives  144 us (32%)
  waiting for transfers between devices  109 us (24%)
  Pallas kernels  88 us (20%)
  starting transfers between devices  80.8 us (18%)
  between operations  14.2 us (3%)
  other arithmetic  6.09 us (1%)
    all_to_all x11, blocking collectives, exchange(): return lax.all_to_all(x, axis, 0, 0, tiled=True)  144 us
    all_to_all x11, waiting for transfers between devices, exchange(): return lax.all_to_all(x, axis, 0, 0, tiled=True)  94.5 us
    pallas_call x39, Pallas kernels, call(): pl.pallas_call(wrapped, out_shape=tuple(out_shape), in_specs=in_specs, ou...  88 us
    all_to_all x11, starting transfers between devices, exchange(): return lax.all_to_all(x, axis, 0, 0, tiled=True)  48.4 us
    ppermute x17, starting transfers between devices, swap(): return lax.ppermute(x, 'pipe', [(0, 1), (1, 0)])  32.2 us
    ppermute x17, waiting for transfers between devices, swap(): return lax.ppermute(x, 'pipe', [(0, 1), (1, 0)])  9.55 us
  transfers between devices with their start and end apart: 32, of which 19 were waited for; matrix products, arithmetic and copies ran while one was open for 1% of the time, Pallas kernels for 13%

profile of v3, /device:TPU:1, one launch (start us, length us, event | category | flops | bytes accessed | tf_op | source)
XLA Modules:
  0.0 445.7 jit_solution(17146657018591670322)
XLA Ops:
  12.8 4.2 shard_map.154
  17.0 16.5 %all_to_all.110.refs_0_ = bf16[8,160,256]{2,1,0:T(8,128)(2,1)S(1)} all-to-all(bf16[8,160,256]{2,1,0:T(8,128)(2,1)} %get-tuple-element.103), channel_id=1, replica_groups=mesh['pipe'=2,'ctx'=8,'tp'=8] {'ctx'}, dimensions={0} | all-to-all | bytes 1310720 | tf_op jit(solution)/shard_map/all_to_all | solution.py:698
  37.0 7.3 %all-to-all-start.1 = ((bf16[8,8,24,128]{3,2,1,0:T(8,128)(2,1)}), bf16[8,8,24,128]{3,2,1,0:T(8,128)(2,1)S(1)}, u32[]{:S(2)}, u32[]{:S(2)}) async-start(bf16[8,8,24,128]{3,2,1,0:T(8,128)(2,1)} %shard_map.155), calls=%async_computation.1 | async-start | bytes 786432 | tf_op jit(solution)/shard_map/all_to_all | solution.py:698
  48.4 6.7 %all-to-all-done.1.refs_0_ = bf16[8,8,24,128]{3,2,1,0:T(8,128)(2,1)S(1)} async-done(((bf16[8,8,24,128]{3,2,1,0:T(8,128)(2,1)}), bf16[8,8,24,128]{3,2,1,0:T(8,128)(2,1)S(1)}, u32[]{:S(2)}, u32[]{:S(2)}) %all-to-all-start.1) | async-done | bytes 393248 | tf_op jit(solution)/shard_map/all_to_all | solution.py:698
  60.2 14.7 %all_to_all.111 = bf16[8,192,256]{2,1,0:T(8,128)(2,1)S(1)} all-to-all(bf16[8,192,256]{2,1,0:T(8,128)(2,1)S(1)} %get-tuple-element.110), channel_id=1, replica_groups=mesh['pipe'=2,'ctx'=8,'tp'=8] {'ctx'}, dimensions={0} | all-to-all | bytes 1572864 | tf_op jit(solution)/shard_map/all_to_all | solution.py:698
  80.0 4.2 shard_map.161
  84.2 14.9 %all_to_all.112.refs_0_ = bf16[8,24,1024]{2,1,0:T(8,128)(2,1)S(1)} all-to-all(bf16[8,24,1024]{2,1,0:T(8,128)(2,1)S(1)} %bitcast.65), channel_id=1, replica_groups=mesh['pipe'=2,'ctx'=8,'tp'=8] {'tp'}, dimensions={0} | all-to-all | bytes 786432 | tf_op jit(solution)/shard_map/all_to_all | solution.py:698
  105.3 11.5 %all-to-all-done.4 = bf16[8,24,1024]{2,1,0:T(8,128)(2,1)S(1)} async-done(((bf16[8,24,1024]{2,1,0:T(8,128)(2,1)}), bf16[8,24,1024]{2,1,0:T(8,128)(2,1)S(1)}, u32[]{:S(2)}, u32[]{:S(2)}) %all-to-all-start.4) | async-done | bytes 393248 | tf_op jit(solution)/shard_map/all_to_all | solution.py:698
  118.7 12.1 %all_to_all.113.refs_0_ = bf16[8,24,1024]{2,1,0:T(8,128)(2,1)S(1)} all-to-all(bf16[8,24,1024]{2,1,0:T(8,128)(2,1)S(1)} %bitcast.64), channel_id=1, replica_groups=mesh['pipe'=2,'ctx'=8,'tp'=8] {'tp'}, dimensions={0} | all-to-all | bytes 786432 | tf_op jit(solution)/shard_map/all_to_all | solution.py:698
  134.9 11.9 %all_to_all.114 = bf16[8,24,1024]{2,1,0:T(8,128)(2,1)S(1)} all-to-all(bf16[8,24,1024]{2,1,0:T(8,128)(2,1)S(1)} %get-tuple-element.122), channel_id=1, replica_groups=mesh['pipe'=2,'ctx'=8,'tp'=8] {'tp'}, dimensions={0} | all-to-all | bytes 786432 | tf_op jit(solution)/shard_map/all_to_all | solution.py:698
  149.6 13.6 %all_to_all.115 = bf16[8,192,256]{2,1,0:T(8,128)(2,1)S(1)} all-to-all(bf16[8,192,256]{2,1,0:T(8,128)(2,1)S(1)} %get-tuple-element.125), channel_id=1, replica_groups=mesh['pipe'=2,'ctx'=8,'tp'=8] {'ctx'}, dimensions={0} | all-to-all | bytes 1572864 | tf_op jit(solution)/shard_map/all_to_all | solution.py:698
  171.3 11.6 %all_to_all.116.refs_0_ = bf16[8,24,1024]{2,1,0:T(8,128)(2,1)S(1)} all-to-all(bf16[8,24,1024]{2,1,0:T(8,128)(2,1)S(1)} %bitcast.66), channel_id=1, replica_groups=mesh['pipe'=2,'ctx'=8,'tp'=8] {'tp'}, dimensions={0} | all-to-all | bytes 786432 | tf_op jit(solution)/shard_map/all_to_all | solution.py:698
  184.7 11.4 %all_to_all.117 = bf16[8,24,1024]{2,1,0:T(8,128)(2,1)S(1)} all-to-all(bf16[8,24,1024]{2,1,0:T(8,128)(2,1)S(1)} %get-tuple-element.129), channel_id=1, replica_groups=mesh['pipe'=2,'ctx'=8,'tp'=8] {'tp'}, dimensions={0} | all-to-all | bytes 786432 | tf_op jit(solution)/shard_map/all_to_all | solution.py:698
  198.9 13.4 %all_to_all.118.refs_0_ = bf16[8,2,24,1024]{3,2,1,0:T(8,128)(2,1)S(1)} all-to-all(bf16[8,2,24,1024]{3,2,1,0:T(8,128)(2,1)S(1)} %get-tuple-element.131), channel_id=1, replica_groups=mesh['pipe'=2,'ctx'=8,'tp'=8] {'tp'}, dimensions={0} | all-to-all | bytes 1572864 | tf_op jit(solution)/shard_map/all_to_all | solution.py:698
  221.7 4.6 %all-to-all-done.11 = bf16[8,24,1024]{2,1,0:T(8,128)(2,1)S(1)} async-done(((bf16[8,24,1024]{2,1,0:T(8,128)(2,1)}), bf16[8,24,1024]{2,1,0:T(8,128)(2,1)S(1)}, u32[]{:S(2)}, u32[]{:S(2)}) %all-to-all-start.11) | async-done | bytes 393248 | tf_op jit(solution)/shard_map/all_to_all | solution.py:698
  226.3 5.1 %shard_map.171 = (bf16[1536,256]{1,0:T(8,128)(2,1)S(1)}, bf16[1536,256]{1,0:T(8,128)(2,1)S(1)}, bf16[34048,1024]{1,0:T(8,128)(2,1)}) custom-call(bf16[192,1024]{1,0:T(8,128)(2,1)S(1)} %bitcast.57, bf16[34048,1024]{1,0:T(8,128)(2,1)} %get-tuple-element.135.refs_1_), custom_call_target="tpu_custom_call", output_to_operand_aliasing={{2}: (1, {})} | custom-call | tf_op jit(solution)/shard_map/pallas_call | solution.py:236
  231.4 5.2 %collective-permute-start.7 = (bf16[1536,256]{1,0:T(8,128)(2,1)S(1)}, bf16[1536,256]{1,0:T(8,128)(2,1)S(1)}, u32[]{:S(2)}, u32[]{:S(2)}) collective-permute-start(bf16[1536,256]{1,0:T(8,128)(2,1)S(1)} %get-tuple-element.137), channel_id=1, source_target_pairs={{0,64},{64,0},{1,65},{65,1},{2,66},{66,2},{3,67},{67,3},{4,68},{68... | collective-permute-start | bytes 2359304 | tf_op jit(solution)/shard_map/ppermute | solution.py:702
  243.7 11.9 %all-to-all-done.12.refs_0_ = bf16[8,192,256]{2,1,0:T(8,128)(2,1)S(1)} async-done(((bf16[8,192,256]{2,1,0:T(8,128)(2,1)}), bf16[8,192,256]{2,1,0:T(8,128)(2,1)S(1)}, u32[]{:S(2)}, u32[]{:S(2)}) %all-to-all-start.12) | async-done | bytes 786464 | tf_op jit(solution)/shard_map/all_to_all | solution.py:698
  261.6 12.2 %all_to_all.119.refs_0_ = bf16[8,24,1024]{2,1,0:T(8,128)(2,1)S(1)} all-to-all(bf16[8,24,1024]{2,1,0:T(8,128)(2,1)S(1)} %bitcast.63), channel_id=1, replica_groups=mesh['pipe'=2,'ctx'=8,'tp'=8] {'tp'}, dimensions={0} | all-to-all | bytes 786432 | tf_op jit(solution)/shard_map/all_to_all | solution.py:698
  278.6 12.1 %all_to_all.120 = bf16[8,24,1024]{2,1,0:T(8,128)(2,1)S(1)} all-to-all(bf16[8,24,1024]{2,1,0:T(8,128)(2,1)S(1)} %get-tuple-element.142), channel_id=1, replica_groups=mesh['pipe'=2,'ctx'=8,'tp'=8] {'tp'}, dimensions={0} | all-to-all | bytes 786432 | tf_op jit(solution)/shard_map/all_to_all | solution.py:698
  294.6 5.3 %all-to-all-start.15 = ((bf16[8,24,1024]{2,1,0:T(8,128)(2,1)}), bf16[8,24,1024]{2,1,0:T(8,128)(2,1)S(1)}, u32[]{:S(2)}, u32[]{:S(2)}) async-start(bf16[8,24,1024]{2,1,0:T(8,128)(2,1)} %bitcast.23), calls=%async_computation.15 | async-start | bytes 786432 | tf_op jit(solution)/shard_map/all_to_all | solution.py:698
  303.0 5.9 %all-to-all-done.15.refs_0_ = bf16[8,24,1024]{2,1,0:T(8,128)(2,1)S(1)} async-done(((bf16[8,24,1024]{2,1,0:T(8,128)(2,1)}), bf16[8,24,1024]{2,1,0:T(8,128)(2,1)S(1)}, u32[]{:S(2)}, u32[]{:S(2)}) %all-to-all-start.15) | async-done | bytes 393248 | tf_op jit(solution)/shard_map/all_to_all | solution.py:698
  311.8 4.0 collective-permute-start.10
  321.9 7.2 %all-to-all-done.16 = bf16[8,24,1024]{2,1,0:T(8,128)(2,1)S(1)} async-done(((bf16[8,24,1024]{2,1,0:T(8,128)(2,1)}), bf16[8,24,1024]{2,1,0:T(8,128)(2,1)S(1)}, u32[]{:S(2)}, u32[]{:S(2)}) %all-to-all-start.16) | async-done | bytes 393248 | tf_op jit(solution)/shard_map/all_to_all | solution.py:698
  329.1 5.1 %shard_map.181 = (bf16[1536,256]{1,0:T(8,128)(2,1)S(1)}, bf16[1536,256]{1,0:T(8,128)(2,1)S(1)}, bf16[34048,1024]{1,0:T(8,128)(2,1)}) custom-call(bf16[192,1024]{1,0:T(8,128)(2,1)S(1)} %bitcast.55, bf16[34048,1024]{1,0:T(8,128)(2,1)} %get-tuple-element.155.refs_1_), custom_call_target="tpu_custom_call", output_to_operand_aliasing={{2}: (1, {})} | custom-call | tf_op jit(solution)/shard_map/pallas_call | solution.py:236
  342.5 11.8 %all-to-all-done.17.refs_0_ = bf16[8,192,256]{2,1,0:T(8,128)(2,1)S(1)} async-done(((bf16[8,192,256]{2,1,0:T(8,128)(2,1)}), bf16[8,192,256]{2,1,0:T(8,128)(2,1)S(1)}, u32[]{:S(2)}, u32[]{:S(2)}) %all-to-all-start.17) | async-done | bytes 786464 | tf_op jit(solution)/shard_map/all_to_all | solution.py:698
  363.2 6.7 %all-to-all-done.18.refs_1_ = bf16[8,24,1024]{2,1,0:T(8,128)(2,1)S(1)} async-done(((bf16[8,24,1024]{2,1,0:T(8,128)(2,1)}), bf16[8,24,1024]{2,1,0:T(8,128)(2,1)S(1)}, u32[]{:S(2)}, u32[]{:S(2)}) %all-to-all-start.18) | async-done | bytes 393248 | tf_op jit(solution)/shard_map/all_to_all | solution.py:698
  380.3 4.0 reduce-scatter.5.cloned.1.call-done.refs_1_
  384.3 14.6 %all-to-all-done.19.refs_0_ = bf16[8,72,1024]{2,1,0:T(8,128)(2,1)S(1)} async-done(((bf16[8,72,1024]{2,1,0:T(8,128)(2,1)}), bf16[8,72,1024]{2,1,0:T(8,128)(2,1)S(1)}, u32[]{:S(2)}, u32[]{:S(2)}) %all-to-all-start.19) | async-done | bytes 1179680 | tf_op jit(solution)/shard_map/all_to_all | solution.py:698
  405.1 9.0 %all-to-all-done.20.refs_1_ = bf16[8,160,256]{2,1,0:T(8,128)(2,1)S(1)} async-done(((bf16[8,160,256]{2,1,0:T(8,128)(2,1)}), bf16[8,160,256]{2,1,0:T(8,128)(2,1)S(1)}, u32[]{:S(2)}, u32[]{:S(2)}) %all-to-all-start.20) | async-done | bytes 655392 | tf_op jit(solution)/shard_map/all_to_all | solution.py:698
  415.4 7.3 %all-to-all-start.21 = ((bf16[64,24,128]{2,1,0:T(8,128)(2,1)}), bf16[64,24,128]{2,1,0:T(8,128)(2,1)S(1)}, u32[]{:S(2)}, u32[]{:S(2)}) async-start(bf16[64,24,128]{2,1,0:T(8,128)(2,1)} %get-tuple-element.172), calls=%async_computation.23 | async-start | bytes 786432 | tf_op jit(solution)/shard_map/all_to_all | solution.py:698
  428.5 4.5 %all-to-all-done.21 = bf16[64,24,128]{2,1,0:T(8,128)(2,1)S(1)} async-done(((bf16[64,24,128]{2,1,0:T(8,128)(2,1)}), bf16[64,24,128]{2,1,0:T(8,128)(2,1)S(1)}, u32[]{:S(2)}, u32[]{:S(2)}) %all-to-all-start.21) | async-done | bytes 393248 | tf_op jit(solution)/shard_map/all_to_all | solution.py:698
  (123 shorter events, 140.8 us)
Async XLA Ops:
  7.2 69.7 %all-gather.3.cloned.1.call-start = ((), (), s32[]{:S(2)}) async-start(), calls=%async_computation.24 | async-start | bytes 1179648 | tf_op jit(solution)/shard_map/all_gather | solution.py:735
  9.2 2.9 collective-permute-start
  33.5 23.6 %collective-permute-start.2 = (bf16[1280,256]{1,0:T(8,128)(2,1)S(1)}, bf16[1280,256]{1,0:T(8,128)(2,1)S(1)}, u32[]{:S(2)}, u32[]{:S(2)}) collective-permute-start(bf16[1280,256]{1,0:T(8,128)(2,1)S(1)} %bitcast.48), channel_id=1, source_target_pairs={{0,64},{64,0},{1,65},{65,1},{2,66},{66,2},{3,67},{67,3},{4,68},{68... | collective-permute-start | bytes 1966088 | tf_op jit(solution)/shard_map/ppermute | solution.py:702
  37.0 18.1 %all-to-all-start.1 = ((bf16[8,8,24,128]{3,2,1,0:T(8,128)(2,1)}), bf16[8,8,24,128]{3,2,1,0:T(8,128)(2,1)S(1)}, u32[]{:S(2)}, u32[]{:S(2)}) async-start(bf16[8,8,24,128]{3,2,1,0:T(8,128)(2,1)} %shard_map.155), calls=%async_computation.1 | async-start | bytes 786432 | tf_op jit(solution)/shard_map/all_to_all | solution.py:698
  44.3 88.2 %all-gather.5.cloned.1.call-start = ((), (), s32[]{:S(2)}) async-start(), calls=%async_computation.25 | async-start | bytes 1769472 | tf_op jit(solution)/shard_map/all_gather | solution.py:805
  55.1 2.0 collective-permute-start.1
  74.8 5.2 %collective-permute-start.3 = (bf16[1536,256]{1,0:T(8,128)(2,1)S(1)}, bf16[1536,256]{1,0:T(8,128)(2,1)}, u32[]{:S(2)}, u32[]{:S(2)}) collective-permute-start(bf16[1536,256]{1,0:T(8,128)(2,1)S(1)} %bitcast.51), channel_id=1, source_target_pairs={{0,64},{64,0},{1,65},{65,1},{2,66},{66,2},{3,67},{67,3},{4,68},{68... | collective-permute-start | bytes 2359304 | tf_op jit(solution)/shard_map/ppermute | solution.py:702
  76.9 28.4 %collective-permute-start.4 = (bf16[1024,512]{1,0:T(8,128)(2,1)}, bf16[1024,512]{1,0:T(8,128)(2,1)S(1)}, u32[]{:S(2)}, u32[]{:S(2)}) collective-permute-start(bf16[1024,512]{1,0:T(8,128)(2,1)} %all-gather.3.cloned.1.call-done.refs_1_.refs_3_), channel_id=1, source_target_pairs={{0,64},{64,0},{1,65},{65,1},{2,66},{66,2},{3,67},{67,3},{4,68},{68... | collective-permute-start | bytes 3145736 | tf_op jit(solution)/shard_map/ppermute | solution.py:702
  101.6 15.2 %all-to-all-start.4 = ((bf16[8,24,1024]{2,1,0:T(8,128)(2,1)}), bf16[8,24,1024]{2,1,0:T(8,128)(2,1)S(1)}, u32[]{:S(2)}, u32[]{:S(2)}) async-start(bf16[8,24,1024]{2,1,0:T(8,128)(2,1)} %get-tuple-element.115), calls=%async_computation.4 | async-start | bytes 786432 | tf_op jit(solution)/shard_map/all_to_all | solution.py:698
  132.4 14.4 %collective-permute-start.5 = (bf16[1024,768]{1,0:T(8,128)(2,1)}, bf16[1024,768]{1,0:T(8,128)(2,1)S(1)}, u32[]{:S(2)}, u32[]{:S(2)}) collective-permute-start(bf16[1024,768]{1,0:T(8,128)(2,1)} %all-gather.5.cloned.1.call-done.refs_1_.refs_3_), channel_id=1, source_target_pairs={{0,64},{64,0},{1,65},{65,1},{2,66},{66,2},{3,67},{67,3},{4,68},{68... | collective-permute-start | bytes 4718600 | tf_op jit(solution)/shard_map/ppermute | solution.py:702
  163.2 4.9 %collective-permute-start.6 = (bf16[1536,256]{1,0:T(8,128)(2,1)S(1)}, bf16[1536,256]{1,0:T(8,128)(2,1)S(1)}, u32[]{:S(2)}, u32[]{:S(2)}) collective-permute-start(bf16[1536,256]{1,0:T(8,128)(2,1)S(1)} %bitcast.53), channel_id=1, source_target_pairs={{0,64},{64,0},{1,65},{65,1},{2,66},{66,2},{3,67},{67,3},{4,68},{68... | collective-permute-start | bytes 2359304 | tf_op jit(solution)/shard_map/ppermute | solution.py:702
  215.1 11.2 %all-to-all-start.11 = ((bf16[8,24,1024]{2,1,0:T(8,128)(2,1)}), bf16[8,24,1024]{2,1,0:T(8,128)(2,1)S(1)}, u32[]{:S(2)}, u32[]{:S(2)}) async-start(bf16[8,24,1024]{2,1,0:T(8,128)(2,1)} %get-tuple-element.133), calls=%async_computation.11 | async-start | bytes 786432 | tf_op jit(solution)/shard_map/all_to_all | solution.py:698
  231.4 7.2 %collective-permute-start.7 = (bf16[1536,256]{1,0:T(8,128)(2,1)S(1)}, bf16[1536,256]{1,0:T(8,128)(2,1)S(1)}, u32[]{:S(2)}, u32[]{:S(2)}) collective-permute-start(bf16[1536,256]{1,0:T(8,128)(2,1)S(1)} %get-tuple-element.137), channel_id=1, source_target_pairs={{0,64},{64,0},{1,65},{65,1},{2,66},{66,2},{3,67},{67,3},{4,68},{68... | collective-permute-start | bytes 2359304 | tf_op jit(solution)/shard_map/ppermute | solution.py:702
  239.7 16.0 %all-to-all-start.12 = ((bf16[8,192,256]{2,1,0:T(8,128)(2,1)}), bf16[8,192,256]{2,1,0:T(8,128)(2,1)S(1)}, u32[]{:S(2)}, u32[]{:S(2)}) async-start(bf16[8,192,256]{2,1,0:T(8,128)(2,1)} %bitcast.20), calls=%async_computation.12 | async-start | bytes 1572864 | tf_op jit(solution)/shard_map/all_to_all | solution.py:698
  243.2 120.0 %reduce-scatter.3.cloned.1.call-start = ((), (), s32[]{:S(2)}) async-start(), calls=%async_computation.26 | async-start | bytes 1769472 | tf_op jit(solution)/shard_map/reduce_scatter | solution.py:832
  243.3 32.5 %collective-permute-start.8 = (bf16[1024,512]{1,0:T(8,128)(2,1)S(1)}, bf16[1024,512]{1,0:T(8,128)(2,1)S(1)}, u32[]{:S(2)}, u32[]{:S(2)}) collective-permute-start(bf16[1024,512]{1,0:T(8,128)(2,1)S(1)} %get-tuple-element.143), channel_id=1, source_target_pairs={{0,64},{64,0},{1,65},{65,1},{2,66},{66,2},{3,67},{67,3},{4,68},{68... | collective-permute-start | bytes 3145736 | tf_op jit(solution)/shard_map/ppermute | solution.py:702
  260.3 15.5 %collective-permute-start.9 = (bf16[1024,256]{1,0:T(8,128)(2,1)S(1)}, bf16[1024,256]{1,0:T(8,128)(2,1)S(1)}, u32[]{:S(2)}, u32[]{:S(2)}) collective-permute-start(bf16[1024,256]{1,0:T(8,128)(2,1)S(1)} %get-tuple-element.144), channel_id=1, source_target_pairs={{0,64},{64,0},{1,65},{65,1},{2,66},{66,2},{3,67},{67,3},{4,68},{68... | collective-permute-start | bytes 1572872 | tf_op jit(solution)/shard_map/ppermute | solution.py:702
  294.6 14.3 %all-to-all-start.15 = ((bf16[8,24,1024]{2,1,0:T(8,128)(2,1)}), bf16[8,24,1024]{2,1,0:T(8,128)(2,1)S(1)}, u32[]{:S(2)}, u32[]{:S(2)}) async-start(bf16[8,24,1024]{2,1,0:T(8,128)(2,1)} %bitcast.23), calls=%async_computation.15 | async-start | bytes 786432 | tf_op jit(solution)/shard_map/all_to_all | solution.py:698
  311.8 7.7 %collective-permute-start.10 = (bf16[1024,512]{1,0:T(8,128)(2,1)S(1)}, bf16[1024,512]{1,0:T(8,128)(2,1)S(1)}, u32[]{:S(2)}, u32[]{:S(2)}) collective-permute-start(bf16[1024,512]{1,0:T(8,128)(2,1)S(1)} %get-tuple-element.153), channel_id=1, source_target_pairs={{0,64},{64,0},{1,65},{65,1},{2,66},{66,2},{3,67},{67,3},{4,68},{68... | collective-permute-start | bytes 3145736 | tf_op jit(solution)/shard_map/ppermute | solution.py:702
  315.8 13.3 %all-to-all-start.16 = ((bf16[8,24,1024]{2,1,0:T(8,128)(2,1)}), bf16[8,24,1024]{2,1,0:T(8,128)(2,1)S(1)}, u32[]{:S(2)}, u32[]{:S(2)}) async-start(bf16[8,24,1024]{2,1,0:T(8,128)(2,1)} %get-tuple-element.152), calls=%async_computation.16 | async-start | bytes 786432 | tf_op jit(solution)/shard_map/all_to_all | solution.py:698
  334.2 3.0 collective-permute-start.11
  338.3 16.0 %all-to-all-start.17 = ((bf16[8,192,256]{2,1,0:T(8,128)(2,1)}), bf16[8,192,256]{2,1,0:T(8,128)(2,1)S(1)}, u32[]{:S(2)}, u32[]{:S(2)}) async-start(bf16[8,192,256]{2,1,0:T(8,128)(2,1)} %bitcast.25), calls=%async_computation.17 | async-start | bytes 1572864 | tf_op jit(solution)/shard_map/all_to_all | solution.py:698
  341.9 42.4 %reduce-scatter.5.cloned.1.call-start = ((), (), s32[]{:S(2)}) async-start(), calls=%async_computation.27 | async-start | bytes 1179648 | tf_op jit(solution)/shard_map/reduce_scatter | solution.py:843
  356.7 13.1 %all-to-all-start.18 = ((bf16[8,24,1024]{2,1,0:T(8,128)(2,1)}), bf16[8,24,1024]{2,1,0:T(8,128)(2,1)S(1)}, u32[]{:S(2)}, u32[]{:S(2)}) async-start(bf16[8,24,1024]{2,1,0:T(8,128)(2,1)} %bitcast.26), calls=%async_computation.18 | async-start | bytes 786432 | tf_op jit(solution)/shard_map/all_to_all | solution.py:698
  371.3 3.8 collective-permute-start.12
  376.3 22.7 %all-to-all-start.19 = ((bf16[8,72,1024]{2,1,0:T(8,128)(2,1)}), bf16[8,72,1024]{2,1,0:T(8,128)(2,1)S(1)}, u32[]{:S(2)}, u32[]{:S(2)}) async-start(bf16[8,72,1024]{2,1,0:T(8,128)(2,1)} %shard_map.186), calls=%async_computation.20 | async-start | bytes 2359296 | tf_op jit(solution)/shard_map/all_to_all | solution.py:698
  379.8 19.1 %collective-permute-start.13 = (bf16[1024,256]{1,0:T(8,128)(2,1)S(1)}, bf16[1024,256]{1,0:T(8,128)(2,1)S(1)}, u32[]{:S(2)}, u32[]{:S(2)}) collective-permute-start(bf16[1024,256]{1,0:T(8,128)(2,1)S(1)} %get-tuple-element.168), channel_id=1, source_target_pairs={{0,64},{64,0},{1,65},{65,1},{2,66},{66,2},{3,67},{67,3},{4,68},{68... | collective-permute-start | bytes 1572872 | tf_op jit(solution)/shard_map/ppermute | solution.py:702
  401.0 13.1 %all-to-all-start.20 = ((bf16[8,160,256]{2,1,0:T(8,128)(2,1)}), bf16[8,160,256]{2,1,0:T(8,128)(2,1)S(1)}, u32[]{:S(2)}, u32[]{:S(2)}) async-start(bf16[8,160,256]{2,1,0:T(8,128)(2,1)} %get-tuple-element.170), calls=%async_computation.22 | async-start | bytes 1310720 | tf_op jit(solution)/shard_map/all_to_all | solution.py:698
  415.4 17.6 %all-to-all-start.21 = ((bf16[64,24,128]{2,1,0:T(8,128)(2,1)}), bf16[64,24,128]{2,1,0:T(8,128)(2,1)S(1)}, u32[]{:S(2)}, u32[]{:S(2)}) async-start(bf16[64,24,128]{2,1,0:T(8,128)(2,1)} %get-tuple-element.172), calls=%async_computation.23 | async-start | bytes 786432 | tf_op jit(solution)/shard_map/all_to_all | solution.py:698
  424.8 2.8 collective-permute-start.14
  426.2 1.4 collective-permute-start.15
  433.1 3.5 collective-permute-start.16
  (10 other events, 342.8 us)
Sparse Core Ops, SparseCore 0:
  17.1 43.4 all-gather.2
  62.8 56.8 all-gather.4
  278.7 48.9 reduce-scatter.2
  345.4 38.9 reduce-scatter.4

commit v4 on v3

--- a/solution.py
+++ b/solution.py
@@ -575,47 +575,58 @@
     to_all(o_ref, (part(mod_before_ref[...].astype(f32), 5) * dx).astype(bf16))
 
 
-def k_back_first(
-    p_ref, r_ref, x_ref, dmid_ref, mod_ref, d0_ref, d1a_ref, d1b_ref, res_ref, keep_ref, send_ref
-):
+def k_early(p_ref, d0_ref, d1a_ref, d1b_ref, keep_ref, send_ref):
     first = p_ref[0] == 0
-    dx, ds, dc = norm_back(x_ref[...], summed(r_ref), part(mod_ref[...].astype(f32), 1))
+    none = jnp.zeros((6, keep_ref.shape[1]), f32)
+    d0 = jnp.concatenate([none, d0_ref[...]], axis=0)
+    d1 = jnp.concatenate([d1b_ref[...], d1a_ref[...]], axis=0)
+    keep_ref[...] = jnp.where(first, d0, d1)
+    send_ref[...] = jnp.where(first, d1, d0)
+
+
+def k_qkv_back_first(dq_ref, r_ref, wa_ref, wb_ref, x_ref, keep_ref, got_ref, dt_ref, o_ref):
+    dt = jnp.concatenate([dq_ref[...].astype(f32), summed(r_ref)], axis=1)
+    dt = by_part([dt[64 * l : 64 * l + 64] for l in range(LAT)]).astype(bf16)
+    dt_ref[...] = dt
+    back = mm_nt(dt[:, :256], rows_of(wa_ref[...])) + mm_nt(dt[:, 256:], rows_of(wb_ref[...])[:, :128])
+    x = x_ref[...]
+    ds = jnp.zeros((24, x.shape[1]), f32)
+    dc = jnp.zeros((24, x.shape[1]), f32)
+    for j in range(8):
+        dn = back[24 * j : 24 * j + 24]
+        ds = ds + dn
+        dc = dc + dn * centred(x[24 * j : 24 * j + 24])[0]
+    sums = jnp.concatenate([row_sums(ds, dc), keep_ref[...] + got_ref[...]], axis=0)
+    for j in range(8):
+        o_ref[j] = jnp.concatenate([back[24 * j : 24 * j + 24], sums], axis=0).astype(bf16)
+
+
+def rows_sum(r_ref, at, n):
+    total = r_ref[0].astype(f32)[at : at + n]
+    for j in range(1, 8):
+        total = total + r_ref[j].astype(f32)[at : at + n]
+    return total
+
+
+def k_back_first(p_ref, r_ref, x_ref, dmid_ref, mod_ref, res_ref, keep_ref, send_ref):
+    first = p_ref[0] == 0
+    dn = rows_sum(r_ref, 0, 24)
+    dx, _, _ = norm_back(x_ref[...], dn, part(mod_ref[...].astype(f32), 1))
     dx = dmid_ref[...] + dx
     res = res_ref[...]
-    keep_ref[:24] = jnp.where(first, dx, res)
-    send_ref[:24] = jnp.where(first, res, dx)
-    none = jnp.zeros((6, dx.shape[1]), f32)
-    d0 = jnp.concatenate([row_sums(ds, dc), d0_ref[...], none], axis=0)
-    d1 = jnp.concatenate([d1b_ref[...], d1a_ref[...], none], axis=0)
-    keep_ref[24:] = jnp.where(first, d0, d1)
-    send_ref[24:] = jnp.where(first, d1, d0)
-
-
-def k_tail_tp(p_ref, keep_ref, got_ref, o_ref):
-    first = p_ref[0] == 0
-    keep, got = keep_ref[...], got_ref[...]
-    v = jnp.concatenate(
-        [
-            jnp.where(first, keep[:24], got[:24]),
-            jnp.where(first, got[:24], keep[:24]),
-            keep[24:] + got[24:],
-        ],
-        axis=0,
-    ).astype(bf16)
-    to_all(o_ref, v)
+    keep_ref[...] = jnp.where(first, dx, res)
+    send_ref[...] = jnp.where(first, res, dx)
 
 
 def k_tail_ctx(r_ref, a_ref, b_ref, o_ref):
-    total = r_ref[0].astype(f32)[48:]
-    for j in range(1, 8):
-        total = total + r_ref[j].astype(f32)[48:]
+    total = rows_sum(r_ref, 24, 24)
     total = jnp.concatenate([total, jnp.zeros((8, total.shape[1]), f32)], axis=0).astype(bf16)
     none = jnp.zeros((32, 128), bf16)
     for c in range(8):
         at = slice(128 * c, 128 * c + 128)
         o_ref[c, :128, :] = (a_ref[at].astype(f32) + b_ref[at].astype(f32)).astype(bf16)
-        o_ref[c, 128:160, :128] = total[:, at]
-        o_ref[c, 128:160, 128:] = none
+        o_ref[c, 128:, :128] = total[:, at]
+        o_ref[c, 128:, 128:] = none
 
 
 def k_ends(r_ref, o_ref):
@@ -627,24 +638,32 @@
                 o_ref[l, at : at + 8, :] = v[24 * half + 8 * l : 24 * half + 8 * l + 8]
 
 
-def k_cond(t_ref, r_ref, act_ref, ada_ref, g_ref, ada_grad_ref, o_ref):
+def k_cond(
+    p_ref, t_ref, r_ref, other_ref, act_ref, ada_ref, keep_ref, got_ref, g_ref, ada_grad_ref, o_ref
+):
+    first = p_ref[0] == 0
     total = summed(r_ref)
-    d = total[128:, :128].astype(bf16)
+    d = total[128:, :128]
+    late = jnp.where(first, d[:6] + summed(other_ref)[:6], 0.0)
+    d = jnp.concatenate([d[6:12] + late, d[12:24], jnp.zeros((14, 128), f32)], axis=0)
     lane = lax.broadcasted_iota(jnp.int32, (128, 16), 0)
     col = lax.broadcasted_iota(jnp.int32, (128, 16), 1)
     pick = jnp.where(lane == col + 16 * t_ref[0], 1.0, 0.0).astype(bf16)
-    d = mm(d, pick)
+    d = mm(d.astype(bf16), pick)
     act = act_ref[...]
     c = jnp.zeros(act.shape, f32)
     for k in range(6):
         dk = d[3 * k : 3 * k + 3].astype(bf16)
         ada_grad_ref[16 * k : 16 * k + 16, :] = mm_tn(dk, act)
         c = c + mm(dk, ada_ref[16 * k : 16 * k + 16, :])
-    v = [c[l : l + 1, 128 * k : 128 * k + 128] for l in range(LAT) for k in range(8)]
-    v = jnp.concatenate(v, axis=0).astype(bf16)
-    for j in range(64):
-        o_ref[j] = v
+    keep, got = keep_ref[...], got_ref[...]
+    v = [jnp.where(first, keep, got), jnp.where(first, got, keep), c, jnp.zeros((13, c.shape[1]), f32)]
+    to_all(o_ref, jnp.concatenate(v, axis=0).astype(bf16))
     g_ref[...] = total[:128].astype(bf16)
+
+
+def k_cond_tp(r_ref, o_ref):
+    to_all(o_ref, rows_sum(r_ref, 48, 8))
 
 
 def k_final_send(p_ref, m0_ref, m1_ref, o_ref):
@@ -765,14 +784,18 @@
         (branch,) = run(k_attn, [att, wide], q, Save(kv_a, sa), Save(kv_b, sb), w[1])
         return (q, sa, sb, att), exchange(branch.reshape(8, 24, 1024), "tp")
 
-    def attn_back(kept, normed, dbranch, w):
+    def attn_back(kept, normed, dbranch, w, last=None):
         q, kv_a, kv_b, att = kept
         db, dq, dt = rows192(1024), rows192(128), rows192(384)
         da, dp = run(k_attn_back, [dq, kv_all, kv_all], q, kv_a, kv_b, w[1], Save(dbranch, db))
         (both,) = run(k_pair_sum, [kv_all], da, swap(dp))
         arrived = exchange(both.reshape(8, 192, 256), "ctx")
-        (dn,) = run(k_qkv_back, [dt, wide], dq, arrived, *w)
-        arrived = exchange(dn.reshape(8, 24, 1024), "tp")
+        if last is None:
+            (dn,) = run(k_qkv_back, [dt, wide], dq, arrived, *w)
+            dn = dn.reshape(8, 24, 1024)
+        else:
+            (dn,) = run(k_qkv_back_first, [dt, ((8, 48, 1024), bf16)], dq, arrived, *w, *last)
+        arrived = exchange(dn, "tp")
         keep = slot((1024, 256), bf16)
         (send,) = run(k_grad_attn, [keep, ((1024, 256), bf16)], who, normed, dt, db, att)
         return arrived, (keep, swap(send))
@@ -841,24 +864,22 @@
     db, send = lax.optimization_barrier((db, send))
     (mixed0,) = run(k_grad_sum, [((1024, 512), bf16)], gm0, swap(send))
     mixed0 = lax.psum_scatter(mixed0, "ctx", tiled=True)
-    arrived, ga0 = attn_back(kept0, normed0, to_rows(db), wa0)
+    keep, send = run(k_early, [((18, 1024), f32)] * 2, who, dmod0a, dmod1a, dmod1b)
+    arrived, ga0 = attn_back(kept0, normed0, to_rows(db), wa0, (x_all, keep, swap(send)))
     arrived, mixed = lax.optimization_barrier((arrived, mixed))
+
+    (tail_ctx,) = run(k_tail_ctx, [((8, 160, 256), bf16)], arrived, *ga0)
     keep, send = run(
-        k_back_first, [((48, 1024), f32)] * 2,
-        who, arrived, x0, dmid0, mods[0], dmod0a, dmod1a, dmod1b, res1,
-    )
-
-    (tail,) = run(k_tail_tp, [((8, 72, 1024), bf16)], who, keep, swap(send))
-    tail = exchange(tail, "tp")
-    tail, gm0 = lax.optimization_barrier((tail, mixed0))
-    (tail_ctx,) = run(k_tail_ctx, [((8, 160, 256), bf16)], tail, *ga0)
+        k_back_first, [((24, 1024), f32)] * 2, who, arrived, x0, dmid0, mods[0], res1
+    )
     tail_ctx = exchange(tail_ctx, "ctx")
-    ga0, grad_ada, spread = run(
-        k_cond, [((128, 256), bf16), ((96, 1024), f32), ((64, 24, 128), bf16)],
-        part_no, tail_ctx, cond_act, ada,
-    )
-    grad_act = exchange(spread, ("ctx", "tp"))
-    tail, ga0, gm0 = lax.optimization_barrier((tail, ga0, gm0))
+    ga0, grad_ada, tail = run(
+        k_cond, [((128, 256), bf16), ((96, 1024), f32), ((8, 64, 1024), bf16)],
+        who, part_no, tail_ctx, swap(tail_ctx[:, 128:, :128]), cond_act, ada, keep, swap(send),
+    )
+    tail, gm0 = lax.optimization_barrier((exchange(tail, "tp"), mixed0))
+    (grad_act,) = run(k_cond_tp, [((8, 8, 1024), f32)], tail)
+    grad_act = exchange(grad_act, "ctx")
     (ends,) = run(k_ends, [((LAT, 128, 1024), f32)], tail)
 
     (send,) = run(k_final_send, [((128, 768), bf16)], who, gm0, mixed)
@@ -874,8 +895,8 @@
     grad_act, ends, grad_up, grad_down, grad_qkv, grad_out, match, slope = lax.optimization_barrier(
         (grad_act, ends, grad_up, grad_down, grad_qkv, grad_out, match, slope)
     )
-    grad_act = grad_act.astype(f32).sum(axis=0)
-    grad_cond = (grad_act + swap(grad_act)).reshape(LAT, width) * slope
+    grad_act = grad_act.sum(axis=0)
+    grad_cond = (grad_act + swap(grad_act))[:LAT] * slope
     grad_table = sum(jnp.where(match[l], grad_cond[l : l + 1], 0.0) for l in range(LAT))
 
     return (

time: 448 us -> 437 us (0.975)
  blocking collectives: 144 us -> 121 us
  starting transfers between devices: 80.8 us -> 87.6 us
    all_to_all x11 -> x9, blocking collectives: 144 us -> 121 us  [exchange(): return lax.all_to_all(x, axis, 0, 0, tiled=True)]
    all_to_all x11 -> x13, waiting for transfers between devices: 94.5 us -> 87 us  [exchange(): return lax.all_to_all(x, axis, 0, 0, tiled=True)]
    reduce_scatter x1, waiting for transfers between devices: 4.02 us -> 11.2 us  [body(): mixed0 = lax.psum_scatter(mixed0, 'ctx', tiled=True)]
    all_to_all x11 -> x13, starting transfers between devices: 48.4 us -> 54.6 us  [exchange(): return lax.all_to_all(x, axis, 0, 0, tiled=True)]
    pallas_call x39 -> x40, Pallas kernels: 88 us -> 91.8 us  [call(): pl.pallas_call(wrapped, out_shape=tuple(out_shape), in_specs=in_specs, ou...]
    ppermute x17 -> x19, waiting for transfers between devices: 9.55 us -> 10.5 us  [swap(): return lax.ppermute(x, 'pipe', [(0, 1), (1, 0)])]
    ppermute x17 -> x19, starting transfers between devices: 32.2 us -> 32.9 us  [swap(): return lax.ppermute(x, 'pipe', [(0, 1), (1, 0)])]
  transfers between devices with their start and end apart: 32 -> 36, of which waited for: 19 -> 23; matrix products, arithmetic and copies ran while one was open for 1% -> 1% of each run, Pallas kernels for 13% -> 15%
where the time goes in v4:
time: 437 us; the launch traced here: 434 us
  blocking collectives  121 us (28%)
  waiting for transfers between devices  110 us (25%)
  Pallas kernels  91.8 us (21%)
  starting transfers between devices  87.6 us (20%)
  between operations  14.2 us (3%)
  other arithmetic  6.02 us (1%)
    all_to_all x9, blocking collectives, exchange(): return lax.all_to_all(x, axis, 0, 0, tiled=True)  121 us
    pallas_call x40, Pallas kernels, call(): pl.pallas_call(wrapped, out_shape=tuple(out_shape), in_specs=in_specs, ou...  91.8 us
    all_to_all x13, waiting for transfers between devices, exchange(): return lax.all_to_all(x, axis, 0, 0, tiled=True)  87 us
    all_to_all x13, starting transfers between devices, exchange(): return lax.all_to_all(x, axis, 0, 0, tiled=True)  54.6 us
    ppermute x19, starting transfers between devices, swap(): return lax.ppermute(x, 'pipe', [(0, 1), (1, 0)])  32.9 us
    reduce_scatter x1, waiting for transfers between devices, body(): mixed0 = lax.psum_scatter(mixed0, 'ctx', tiled=True)  11.2 us
    ppermute x19, waiting for transfers between devices, swap(): return lax.ppermute(x, 'pipe', [(0, 1), (1, 0)])  10.5 us
  transfers between devices with their start and end apart: 36, of which 23 were waited for; matrix products, arithmetic and copies ran while one was open for 1% of the time, Pallas kernels for 15%

profile of v4, /device:TPU:1, one launch (start us, length us, event | category | flops | bytes accessed | tf_op | source)
XLA Modules:
  0.0 434.4 jit_solution(8940177204180453825)
XLA Ops:
  12.8 4.2 shard_map.154
  17.0 16.5 %all_to_all.110.refs_0_ = bf16[8,160,256]{2,1,0:T(8,128)(2,1)S(1)} all-to-all(bf16[8,160,256]{2,1,0:T(8,128)(2,1)} %get-tuple-element.103), channel_id=1, replica_groups=mesh['pipe'=2,'ctx'=8,'tp'=8] {'ctx'}, dimensions={0} | all-to-all | bytes 1310720 | tf_op jit(solution)/shard_map/all_to_all | solution.py:717
  37.0 7.3 %all-to-all-start.1 = ((bf16[8,8,24,128]{3,2,1,0:T(8,128)(2,1)}), bf16[8,8,24,128]{3,2,1,0:T(8,128)(2,1)S(1)}, u32[]{:S(2)}, u32[]{:S(2)}) async-start(bf16[8,8,24,128]{3,2,1,0:T(8,128)(2,1)} %shard_map.155), calls=%async_computation.1 | async-start | bytes 786432 | tf_op jit(solution)/shard_map/all_to_all | solution.py:717
  48.3 6.7 %all-to-all-done.1.refs_0_ = bf16[8,8,24,128]{3,2,1,0:T(8,128)(2,1)S(1)} async-done(((bf16[8,8,24,128]{3,2,1,0:T(8,128)(2,1)}), bf16[8,8,24,128]{3,2,1,0:T(8,128)(2,1)S(1)}, u32[]{:S(2)}, u32[]{:S(2)}) %all-to-all-start.1) | async-done | bytes 393248 | tf_op jit(solution)/shard_map/all_to_all | solution.py:717
  60.2 14.7 %all_to_all.111 = bf16[8,192,256]{2,1,0:T(8,128)(2,1)S(1)} all-to-all(bf16[8,192,256]{2,1,0:T(8,128)(2,1)S(1)} %get-tuple-element.110), channel_id=1, replica_groups=mesh['pipe'=2,'ctx'=8,'tp'=8] {'ctx'}, dimensions={0} | all-to-all | bytes 1572864 | tf_op jit(solution)/shard_map/all_to_all | solution.py:717
  80.0 4.2 shard_map.161
  84.2 15.1 %all_to_all.112.refs_0_ = bf16[8,24,1024]{2,1,0:T(8,128)(2,1)S(1)} all-to-all(bf16[8,24,1024]{2,1,0:T(8,128)(2,1)S(1)} %bitcast.63), channel_id=1, replica_groups=mesh['pipe'=2,'ctx'=8,'tp'=8] {'tp'}, dimensions={0} | all-to-all | bytes 786432 | tf_op jit(solution)/shard_map/all_to_all | solution.py:717
  105.4 10.4 %all-to-all-done.4 = bf16[8,24,1024]{2,1,0:T(8,128)(2,1)S(1)} async-done(((bf16[8,24,1024]{2,1,0:T(8,128)(2,1)}), bf16[8,24,1024]{2,1,0:T(8,128)(2,1)S(1)}, u32[]{:S(2)}, u32[]{:S(2)}) %all-to-all-start.4) | async-done | bytes 393248 | tf_op jit(solution)/shard_map/all_to_all | solution.py:717
  117.5 12.7 %all_to_all.113.refs_0_ = bf16[8,24,1024]{2,1,0:T(8,128)(2,1)S(1)} all-to-all(bf16[8,24,1024]{2,1,0:T(8,128)(2,1)S(1)} %bitcast.62), channel_id=1, replica_groups=mesh['pipe'=2,'ctx'=8,'tp'=8] {'tp'}, dimensions={0} | all-to-all | bytes 786432 | tf_op jit(solution)/shard_map/all_to_all | solution.py:717
  134.5 11.9 %all_to_all.114 = bf16[8,24,1024]{2,1,0:T(8,128)(2,1)S(1)} all-to-all(bf16[8,24,1024]{2,1,0:T(8,128)(2,1)S(1)} %get-tuple-element.122), channel_id=1, replica_groups=mesh['pipe'=2,'ctx'=8,'tp'=8] {'tp'}, dimensions={0} | all-to-all | bytes 786432 | tf_op jit(solution)/shard_map/all_to_all | solution.py:717
  149.2 13.8 %all_to_all.115 = bf16[8,192,256]{2,1,0:T(8,128)(2,1)S(1)} all-to-all(bf16[8,192,256]{2,1,0:T(8,128)(2,1)S(1)} %get-tuple-element.125), channel_id=1, replica_groups=mesh['pipe'=2,'ctx'=8,'tp'=8] {'ctx'}, dimensions={0} | all-to-all | bytes 1572864 | tf_op jit(solution)/shard_map/all_to_all | solution.py:717
  171.1 11.6 %all_to_all.116.refs_0_ = bf16[8,24,1024]{2,1,0:T(8,128)(2,1)S(1)} all-to-all(bf16[8,24,1024]{2,1,0:T(8,128)(2,1)S(1)} %bitcast.64), channel_id=1, replica_groups=mesh['pipe'=2,'ctx'=8,'tp'=8] {'tp'}, dimensions={0} | all-to-all | bytes 786432 | tf_op jit(solution)/shard_map/all_to_all | solution.py:717
  184.4 11.4 %all_to_all.117 = bf16[8,24,1024]{2,1,0:T(8,128)(2,1)S(1)} all-to-all(bf16[8,24,1024]{2,1,0:T(8,128)(2,1)S(1)} %get-tuple-element.129), channel_id=1, replica_groups=mesh['pipe'=2,'ctx'=8,'tp'=8] {'tp'}, dimensions={0} | all-to-all | bytes 786432 | tf_op jit(solution)/shard_map/all_to_all | solution.py:717
  198.6 13.4 %all_to_all.118.refs_0_ = bf16[8,2,24,1024]{3,2,1,0:T(8,128)(2,1)S(1)} all-to-all(bf16[8,2,24,1024]{3,2,1,0:T(8,128)(2,1)S(1)} %get-tuple-element.131), channel_id=1, replica_groups=mesh['pipe'=2,'ctx'=8,'tp'=8] {'tp'}, dimensions={0} | all-to-all | bytes 1572864 | tf_op jit(solution)/shard_map/all_to_all | solution.py:717
  218.3 4.1 shard_map.170
  226.1 5.1 %shard_map.171 = (bf16[1536,256]{1,0:T(8,128)(2,1)S(1)}, bf16[1536,256]{1,0:T(8,128)(2,1)S(1)}, bf16[34048,1024]{1,0:T(8,128)(2,1)}) custom-call(bf16[192,1024]{1,0:T(8,128)(2,1)S(1)} %bitcast.57, bf16[34048,1024]{1,0:T(8,128)(2,1)} %get-tuple-element.135.refs_1_), custom_call_target="tpu_custom_call", output_to_operand_aliasing={{2}: (1, {})} | custom-call | tf_op jit(solution)/shard_map/pallas_call | solution.py:236
  231.2 5.3 %collective-permute-start.7 = (bf16[1536,256]{1,0:T(8,128)(2,1)S(1)}, bf16[1536,256]{1,0:T(8,128)(2,1)S(1)}, u32[]{:S(2)}, u32[]{:S(2)}) collective-permute-start(bf16[1536,256]{1,0:T(8,128)(2,1)S(1)} %get-tuple-element.137), channel_id=1, source_target_pairs={{0,64},{64,0},{1,65},{65,1},{2,66},{66,2},{3,67},{67,3},{4,68},{68... | collective-permute-start | bytes 2359304 | tf_op jit(solution)/shard_map/ppermute | solution.py:721
  243.4 12.0 %all-to-all-done.12.refs_0_ = bf16[8,192,256]{2,1,0:T(8,128)(2,1)S(1)} async-done(((bf16[8,192,256]{2,1,0:T(8,128)(2,1)}), bf16[8,192,256]{2,1,0:T(8,128)(2,1)S(1)}, u32[]{:S(2)}, u32[]{:S(2)}) %all-to-all-start.12) | async-done | bytes 786464 | tf_op jit(solution)/shard_map/all_to_all | solution.py:717
  271.8 4.6 %all-to-all-start.14 = ((bf16[8,24,1024]{2,1,0:T(8,128)(2,1)}), bf16[8,24,1024]{2,1,0:T(8,128)(2,1)S(1)}, u32[]{:S(2)}, u32[]{:S(2)}) async-start(bf16[8,24,1024]{2,1,0:T(8,128)(2,1)} %get-tuple-element.142), calls=%async_computation.14 | async-start | bytes 786432 | tf_op jit(solution)/shard_map/all_to_all | solution.py:717
  279.3 5.0 %all-to-all-done.14 = bf16[8,24,1024]{2,1,0:T(8,128)(2,1)S(1)} async-done(((bf16[8,24,1024]{2,1,0:T(8,128)(2,1)}), bf16[8,24,1024]{2,1,0:T(8,128)(2,1)S(1)}, u32[]{:S(2)}, u32[]{:S(2)}) %all-to-all-start.14) | async-done | bytes 393248 | tf_op jit(solution)/shard_map/all_to_all | solution.py:717
  284.2 3.9 shard_map.177
  294.7 5.6 %all-to-all-done.15.refs_0_ = bf16[8,24,1024]{2,1,0:T(8,128)(2,1)S(1)} async-done(((bf16[8,24,1024]{2,1,0:T(8,128)(2,1)}), bf16[8,24,1024]{2,1,0:T(8,128)(2,1)S(1)}, u32[]{:S(2)}, u32[]{:S(2)}) %all-to-all-start.15) | async-done | bytes 393248 | tf_op jit(solution)/shard_map/all_to_all | solution.py:717
  314.1 8.1 %all-to-all-done.16 = bf16[8,24,1024]{2,1,0:T(8,128)(2,1)S(1)} async-done(((bf16[8,24,1024]{2,1,0:T(8,128)(2,1)}), bf16[8,24,1024]{2,1,0:T(8,128)(2,1)S(1)}, u32[]{:S(2)}, u32[]{:S(2)}) %all-to-all-start.16) | async-done | bytes 393248 | tf_op jit(solution)/shard_map/all_to_all | solution.py:717
  322.1 5.2 %shard_map.182 = (bf16[1536,256]{1,0:T(8,128)(2,1)S(1)}, bf16[1536,256]{1,0:T(8,128)(2,1)S(1)}, bf16[34048,1024]{1,0:T(8,128)(2,1)}) custom-call(bf16[192,1024]{1,0:T(8,128)(2,1)S(1)} %bitcast.55, bf16[34048,1024]{1,0:T(8,128)(2,1)} %get-tuple-element.156.refs_1_), custom_call_target="tpu_custom_call", output_to_operand_aliasing={{2}: (1, {})} | custom-call | tf_op jit(solution)/shard_map/pallas_call | solution.py:236
  336.6 10.3 %all-to-all-done.17.refs_0_ = bf16[8,192,256]{2,1,0:T(8,128)(2,1)S(1)} async-done(((bf16[8,192,256]{2,1,0:T(8,128)(2,1)}), bf16[8,192,256]{2,1,0:T(8,128)(2,1)S(1)}, u32[]{:S(2)}, u32[]{:S(2)}) %all-to-all-start.17) | async-done | bytes 786464 | tf_op jit(solution)/shard_map/all_to_all | solution.py:717
  349.9 4.3 all-to-all-start.18
  359.6 6.8 %all-to-all-done.18.refs_0_.refs_1_ = bf16[8,48,1024]{2,1,0:T(8,128)(2,1)S(1)} async-done(((bf16[8,48,1024]{2,1,0:T(8,128)(2,1)}), bf16[8,48,1024]{2,1,0:T(8,128)(2,1)S(1)}, u32[]{:S(2)}, u32[]{:S(2)}) %all-to-all-start.18) | async-done | bytes 786464 | tf_op jit(solution)/shard_map/all_to_all | solution.py:717
  368.5 4.1 all-to-all-start.19
  375.6 9.4 %all-to-all-done.19.refs_2_ = bf16[8,160,256]{2,1,0:T(8,128)(2,1)S(1)} async-done(((bf16[8,160,256]{2,1,0:T(8,128)(2,1)}), bf16[8,160,256]{2,1,0:T(8,128)(2,1)S(1)}, u32[]{:S(2)}, u32[]{:S(2)}) %all-to-all-start.19) | async-done | bytes 655392 | tf_op jit(solution)/shard_map/all_to_all | solution.py:717
  388.4 5.4 %all-to-all-start.20 = ((bf16[8,64,1024]{2,1,0:T(8,128)(2,1)}), bf16[8,64,1024]{2,1,0:T(8,128)(2,1)S(1)}, u32[]{:S(2)}, u32[]{:S(2)}) async-start(bf16[8,64,1024]{2,1,0:T(8,128)(2,1)} %get-tuple-element.173), calls=%async_computation.21 | async-start | bytes 2097152 | tf_op jit(solution)/shard_map/all_to_all | solution.py:717
  395.7 11.2 %reduce-scatter.5.cloned.1.call-done.refs_1_ = bf16[128,512]{1,0:T(8,128)(2,1)} async-done(((bf16[1024,512]{1,0:T(8,128)(2,1)}), bf16[128,512]{1,0:T(8,128)(2,1)}) %reduce-scatter.5.cloned.1.call-update) | async-done | bytes 131088 | tf_op jit(solution)/shard_map/reduce_scatter | solution.py:866
  406.8 4.8 %all-to-all-done.20.refs_0_ = bf16[8,64,1024]{2,1,0:T(8,128)(2,1)S(1)} async-done(((bf16[8,64,1024]{2,1,0:T(8,128)(2,1)}), bf16[8,64,1024]{2,1,0:T(8,128)(2,1)S(1)}, u32[]{:S(2)}, u32[]{:S(2)}) %all-to-all-start.20) | async-done | bytes 1048608 | tf_op jit(solution)/shard_map/all_to_all | solution.py:717
  (129 shorter events, 151.2 us)
Async XLA Ops:
  7.2 69.7 %all-gather.3.cloned.1.call-start = ((), (), s32[]{:S(2)}) async-start(), calls=%async_computation.24 | async-start | bytes 1179648 | tf_op jit(solution)/shard_map/all_gather | solution.py:754
  9.2 2.9 collective-permute-start
  33.5 23.6 %collective-permute-start.2 = (bf16[1280,256]{1,0:T(8,128)(2,1)S(1)}, bf16[1280,256]{1,0:T(8,128)(2,1)S(1)}, u32[]{:S(2)}, u32[]{:S(2)}) collective-permute-start(bf16[1280,256]{1,0:T(8,128)(2,1)S(1)} %bitcast.47), channel_id=1, source_target_pairs={{0,64},{64,0},{1,65},{65,1},{2,66},{66,2},{3,67},{67,3},{4,68},{68... | collective-permute-start | bytes 1966088 | tf_op jit(solution)/shard_map/ppermute | solution.py:721
  37.0 18.1 %all-to-all-start.1 = ((bf16[8,8,24,128]{3,2,1,0:T(8,128)(2,1)}), bf16[8,8,24,128]{3,2,1,0:T(8,128)(2,1)S(1)}, u32[]{:S(2)}, u32[]{:S(2)}) async-start(bf16[8,8,24,128]{3,2,1,0:T(8,128)(2,1)} %shard_map.155), calls=%async_computation.1 | async-start | bytes 786432 | tf_op jit(solution)/shard_map/all_to_all | solution.py:717
  44.3 87.7 %all-gather.5.cloned.1.call-start = ((), (), s32[]{:S(2)}) async-start(), calls=%async_computation.25 | async-start | bytes 1769472 | tf_op jit(solution)/shard_map/all_gather | solution.py:828
  74.9 5.2 %collective-permute-start.3 = (bf16[1536,256]{1,0:T(8,128)(2,1)S(1)}, bf16[1536,256]{1,0:T(8,128)(2,1)}, u32[]{:S(2)}, u32[]{:S(2)}) collective-permute-start(bf16[1536,256]{1,0:T(8,128)(2,1)S(1)} %bitcast.50), channel_id=1, source_target_pairs={{0,64},{64,0},{1,65},{65,1},{2,66},{66,2},{3,67},{67,3},{4,68},{68... | collective-permute-start | bytes 2359304 | tf_op jit(solution)/shard_map/ppermute | solution.py:721
  76.9 28.5 %collective-permute-start.4 = (bf16[1024,512]{1,0:T(8,128)(2,1)}, bf16[1024,512]{1,0:T(8,128)(2,1)S(1)}, u32[]{:S(2)}, u32[]{:S(2)}) collective-permute-start(bf16[1024,512]{1,0:T(8,128)(2,1)} %all-gather.3.cloned.1.call-done.refs_1_.refs_3_), channel_id=1, source_target_pairs={{0,64},{64,0},{1,65},{65,1},{2,66},{66,2},{3,67},{67,3},{4,68},{68... | collective-permute-start | bytes 3145736 | tf_op jit(solution)/shard_map/ppermute | solution.py:721
  101.8 13.9 %all-to-all-start.4 = ((bf16[8,24,1024]{2,1,0:T(8,128)(2,1)}), bf16[8,24,1024]{2,1,0:T(8,128)(2,1)S(1)}, u32[]{:S(2)}, u32[]{:S(2)}) async-start(bf16[8,24,1024]{2,1,0:T(8,128)(2,1)} %get-tuple-element.115), calls=%async_computation.4 | async-start | bytes 786432 | tf_op jit(solution)/shard_map/all_to_all | solution.py:717
  132.0 14.4 %collective-permute-start.5 = (bf16[1024,768]{1,0:T(8,128)(2,1)}, bf16[1024,768]{1,0:T(8,128)(2,1)S(1)}, u32[]{:S(2)}, u32[]{:S(2)}) collective-permute-start(bf16[1024,768]{1,0:T(8,128)(2,1)} %all-gather.5.cloned.1.call-done.refs_1_.refs_3_), channel_id=1, source_target_pairs={{0,64},{64,0},{1,65},{65,1},{2,66},{66,2},{3,67},{67,3},{4,68},{68... | collective-permute-start | bytes 4718600 | tf_op jit(solution)/shard_map/ppermute | solution.py:721
  163.0 4.9 %collective-permute-start.6 = (bf16[1536,256]{1,0:T(8,128)(2,1)S(1)}, bf16[1536,256]{1,0:T(8,128)(2,1)S(1)}, u32[]{:S(2)}, u32[]{:S(2)}) collective-permute-start(bf16[1536,256]{1,0:T(8,128)(2,1)S(1)} %bitcast.52), channel_id=1, source_target_pairs={{0,64},{64,0},{1,65},{65,1},{2,66},{66,2},{3,67},{67,3},{4,68},{68... | collective-permute-start | bytes 2359304 | tf_op jit(solution)/shard_map/ppermute | solution.py:721
  214.9 11.2 %all-to-all-start.11 = ((bf16[8,24,1024]{2,1,0:T(8,128)(2,1)}), bf16[8,24,1024]{2,1,0:T(8,128)(2,1)S(1)}, u32[]{:S(2)}, u32[]{:S(2)}) async-start(bf16[8,24,1024]{2,1,0:T(8,128)(2,1)} %get-tuple-element.133), calls=%async_computation.11 | async-start | bytes 786432 | tf_op jit(solution)/shard_map/all_to_all | solution.py:717
  231.2 7.2 %collective-permute-start.7 = (bf16[1536,256]{1,0:T(8,128)(2,1)S(1)}, bf16[1536,256]{1,0:T(8,128)(2,1)S(1)}, u32[]{:S(2)}, u32[]{:S(2)}) collective-permute-start(bf16[1536,256]{1,0:T(8,128)(2,1)S(1)} %get-tuple-element.137), channel_id=1, source_target_pairs={{0,64},{64,0},{1,65},{65,1},{2,66},{66,2},{3,67},{67,3},{4,68},{68... | collective-permute-start | bytes 2359304 | tf_op jit(solution)/shard_map/ppermute | solution.py:721
  239.4 16.0 %all-to-all-start.12 = ((bf16[8,192,256]{2,1,0:T(8,128)(2,1)}), bf16[8,192,256]{2,1,0:T(8,128)(2,1)S(1)}, u32[]{:S(2)}, u32[]{:S(2)}) async-start(bf16[8,192,256]{2,1,0:T(8,128)(2,1)} %bitcast.20), calls=%async_computation.12 | async-start | bytes 1572864 | tf_op jit(solution)/shard_map/all_to_all | solution.py:717
  243.0 33.5 %collective-permute-start.8 = (bf16[1024,512]{1,0:T(8,128)(2,1)}, bf16[1024,512]{1,0:T(8,128)(2,1)S(1)}, u32[]{:S(2)}, u32[]{:S(2)}) collective-permute-start(bf16[1024,512]{1,0:T(8,128)(2,1)} %get-tuple-element.143), channel_id=1, source_target_pairs={{0,64},{64,0},{1,65},{65,1},{2,66},{66,2},{3,67},{67,3},{4,68},{68... | collective-permute-start | bytes 3145736 | tf_op jit(solution)/shard_map/ppermute | solution.py:721
  257.9 11.2 %all-to-all-start.13 = ((bf16[8,24,1024]{2,1,0:T(8,128)(2,1)}), bf16[8,24,1024]{2,1,0:T(8,128)(2,1)S(1)}, u32[]{:S(2)}, u32[]{:S(2)}) async-start(bf16[8,24,1024]{2,1,0:T(8,128)(2,1)} %bitcast.21), calls=%async_computation.13 | async-start | bytes 786432 | tf_op jit(solution)/shard_map/all_to_all | solution.py:717
  264.3 12.2 %collective-permute-start.9 = (bf16[1024,256]{1,0:T(8,128)(2,1)S(1)}, bf16[1024,256]{1,0:T(8,128)(2,1)S(1)}, u32[]{:S(2)}, u32[]{:S(2)}) collective-permute-start(bf16[1024,256]{1,0:T(8,128)(2,1)S(1)} %get-tuple-element.144), channel_id=1, source_target_pairs={{0,64},{64,0},{1,65},{65,1},{2,66},{66,2},{3,67},{67,3},{4,68},{68... | collective-permute-start | bytes 1572872 | tf_op jit(solution)/shard_map/ppermute | solution.py:721
  271.8 12.5 %all-to-all-start.14 = ((bf16[8,24,1024]{2,1,0:T(8,128)(2,1)}), bf16[8,24,1024]{2,1,0:T(8,128)(2,1)S(1)}, u32[]{:S(2)}, u32[]{:S(2)}) async-start(bf16[8,24,1024]{2,1,0:T(8,128)(2,1)} %get-tuple-element.142), calls=%async_computation.14 | async-start | bytes 786432 | tf_op jit(solution)/shard_map/all_to_all | solution.py:717
  276.4 83.2 %reduce-scatter.3.cloned.1.call-start = ((), (), s32[]{:S(2)}) async-start(), calls=%async_computation.26 | async-start | bytes 1769472 | tf_op jit(solution)/shard_map/reduce_scatter | solution.py:855
  288.1 12.2 %all-to-all-start.15 = ((bf16[8,24,1024]{2,1,0:T(8,128)(2,1)}), bf16[8,24,1024]{2,1,0:T(8,128)(2,1)S(1)}, u32[]{:S(2)}, u32[]{:S(2)}) async-start(bf16[8,24,1024]{2,1,0:T(8,128)(2,1)} %bitcast.23), calls=%async_computation.15 | async-start | bytes 786432 | tf_op jit(solution)/shard_map/all_to_all | solution.py:717
  303.2 7.4 %collective-permute-start.10 = (bf16[1024,512]{1,0:T(8,128)(2,1)S(1)}, bf16[1024,512]{1,0:T(8,128)(2,1)S(1)}, u32[]{:S(2)}, u32[]{:S(2)}) collective-permute-start(bf16[1024,512]{1,0:T(8,128)(2,1)S(1)} %get-tuple-element.153), channel_id=1, source_target_pairs={{0,64},{64,0},{1,65},{65,1},{2,66},{66,2},{3,67},{67,3},{4,68},{68... | collective-permute-start | bytes 3145736 | tf_op jit(solution)/shard_map/ppermute | solution.py:721
  306.8 15.4 %all-to-all-start.16 = ((bf16[8,24,1024]{2,1,0:T(8,128)(2,1)}), bf16[8,24,1024]{2,1,0:T(8,128)(2,1)S(1)}, u32[]{:S(2)}, u32[]{:S(2)}) async-start(bf16[8,24,1024]{2,1,0:T(8,128)(2,1)} %get-tuple-element.152), calls=%async_computation.16 | async-start | bytes 786432 | tf_op jit(solution)/shard_map/all_to_all | solution.py:717
  327.3 2.9 collective-permute-start.11
  331.2 15.7 %all-to-all-start.17 = ((bf16[8,192,256]{2,1,0:T(8,128)(2,1)}), bf16[8,192,256]{2,1,0:T(8,128)(2,1)S(1)}, u32[]{:S(2)}, u32[]{:S(2)}) async-start(bf16[8,192,256]{2,1,0:T(8,128)(2,1)} %bitcast.25), calls=%async_computation.17 | async-start | bytes 1572864 | tf_op jit(solution)/shard_map/all_to_all | solution.py:717
  349.9 16.5 %all-to-all-start.18 = ((bf16[8,48,1024]{2,1,0:T(8,128)(2,1)}), bf16[8,48,1024]{2,1,0:T(8,128)(2,1)S(1)}, u32[]{:S(2)}, u32[]{:S(2)}) async-start(bf16[8,48,1024]{2,1,0:T(8,128)(2,1)} %get-tuple-element.162), calls=%async_computation.18 | async-start | bytes 1572864 | tf_op jit(solution)/shard_map/all_to_all | solution.py:717
  354.2 52.6 %reduce-scatter.5.cloned.1.call-start = ((), (), s32[]{:S(2)}) async-start(), calls=%async_computation.27 | async-start | bytes 1179648 | tf_op jit(solution)/shard_map/reduce_scatter | solution.py:866
  357.8 8.6 %collective-permute-start.13 = (bf16[1024,256]{1,0:T(8,128)(2,1)S(1)}, bf16[1024,256]{1,0:T(8,128)(2,1)S(1)}, u32[]{:S(2)}, u32[]{:S(2)}) collective-permute-start(bf16[1024,256]{1,0:T(8,128)(2,1)S(1)} %get-tuple-element.166), channel_id=1, source_target_pairs={{0,64},{64,0},{1,65},{65,1},{2,66},{66,2},{3,67},{67,3},{4,68},{68... | collective-permute-start | bytes 1572872 | tf_op jit(solution)/shard_map/ppermute | solution.py:721
  368.5 16.5 %all-to-all-start.19 = ((bf16[8,160,256]{2,1,0:T(8,128)(2,1)}), bf16[8,160,256]{2,1,0:T(8,128)(2,1)S(1)}, u32[]{:S(2)}, u32[]{:S(2)}) async-start(bf16[8,160,256]{2,1,0:T(8,128)(2,1)} %get-tuple-element.168), calls=%async_computation.20 | async-start | bytes 1310720 | tf_op jit(solution)/shard_map/all_to_all | solution.py:717
  373.9 12.0 %collective-permute-start.15 = (f32[24,1024]{1,0:T(8,128)S(1)}, f32[24,1024]{1,0:T(8,128)S(1)}, u32[]{:S(2)}, u32[]{:S(2)}) collective-permute-start(f32[24,1024]{1,0:T(8,128)S(1)} %get-tuple-element.172), channel_id=1, source_target_pairs={{0,64},{64,0},{1,65},{65,1},{2,66},{66,2},{3,67},{67,3},{4,68},{68... | collective-permute-start | bytes 294920 | tf_op jit(solution)/shard_map/ppermute | solution.py:721
  388.4 23.3 %all-to-all-start.20 = ((bf16[8,64,1024]{2,1,0:T(8,128)(2,1)}), bf16[8,64,1024]{2,1,0:T(8,128)(2,1)S(1)}, u32[]{:S(2)}, u32[]{:S(2)}) async-start(bf16[8,64,1024]{2,1,0:T(8,128)(2,1)} %get-tuple-element.173), calls=%async_computation.21 | async-start | bytes 2097152 | tf_op jit(solution)/shard_map/all_to_all | solution.py:717
  412.4 9.7 %all-to-all-start.21 = ((f32[8,8,1024]{2,1,0:T(8,128)}), f32[8,8,1024]{2,1,0:T(8,128)S(1)}, u32[]{:S(2)}, u32[]{:S(2)}) async-start(f32[8,8,1024]{2,1,0:T(8,128)} %shard_map.189), calls=%async_computation.23 | async-start | bytes 524288 | tf_op jit(solution)/shard_map/all_to_all | solution.py:717
  416.8 3.4 collective-permute-start.17
  422.1 3.2 collective-permute-start.18
  (14 other events, 246.8 us)
Sparse Core Ops, SparseCore 0:
  17.1 43.4 all-gather.2
  62.8 57.1 all-gather.4
  280.2 52.6 reduce-scatter.2
  357.7 49.0 reduce-scatter.4

commit v5 on v4

--- a/solution.py
+++ b/solution.py
@@ -657,7 +657,7 @@
         ada_grad_ref[16 * k : 16 * k + 16, :] = mm_tn(dk, act)
         c = c + mm(dk, ada_ref[16 * k : 16 * k + 16, :])
     keep, got = keep_ref[...], got_ref[...]
-    v = [jnp.where(first, keep, got), jnp.where(first, got, keep), c, jnp.zeros((13, c.shape[1]), f32)]
+    v = [jnp.where(first, keep, got), jnp.where(first, got, keep), c, jnp.zeros((5, c.shape[1]), f32)]
     to_all(o_ref, jnp.concatenate(v, axis=0).astype(bf16))
     g_ref[...] = total[:128].astype(bf16)
 
@@ -874,10 +874,10 @@
     )
     tail_ctx = exchange(tail_ctx, "ctx")
     ga0, grad_ada, tail = run(
-        k_cond, [((128, 256), bf16), ((96, 1024), f32), ((8, 64, 1024), bf16)],
+        k_cond, [((128, 256), bf16), ((96, 1024), f32), ((8, 56, 1024), bf16)],
         who, part_no, tail_ctx, swap(tail_ctx[:, 128:, :128]), cond_act, ada, keep, swap(send),
     )
-    tail, gm0 = lax.optimization_barrier((exchange(tail, "tp"), mixed0))
+    tail, gm0 = exchange(tail, "tp"), mixed0
     (grad_act,) = run(k_cond_tp, [((8, 8, 1024), f32)], tail)
     grad_act = exchange(grad_act, "ctx")
     (ends,) = run(k_ends, [((LAT, 128, 1024), f32)], tail)

time: 437 us -> 435 us (level)
    reduce_scatter x1, waiting for transfers between devices: 11.2 us -> 0.02 us  [body(): mixed0 = lax.psum_scatter(mixed0, 'ctx', tiled=True)]
    all_to_all x13, waiting for transfers between devices: 87 us -> 96 us  [exchange(): return lax.all_to_all(x, axis, 0, 0, tiled=True)]
  transfers between devices with their start and end apart: 36 -> 36, of which waited for: 23 -> 22; matrix products, arithmetic and copies ran while one was open for 1% -> 1% of each run, Pallas kernels for 15% -> 16%
where the time goes in v5:
time: 435 us; the launch traced here: 433 us
  blocking collectives  121 us (28%)
  waiting for transfers between devices  109 us (25%)
  Pallas kernels  91.8 us (21%)
  starting transfers between devices  87.5 us (20%)
  between operations  14.2 us (3%)
  other arithmetic  6.02 us (1%)
    all_to_all x9, blocking collectives, exchange(): return lax.all_to_all(x, axis, 0, 0, tiled=True)  121 us
    all_to_all x13, waiting for transfers between devices, exchange(): return lax.all_to_all(x, axis, 0, 0, tiled=True)  96 us
    pallas_call x40, Pallas kernels, call(): pl.pallas_call(wrapped, out_shape=tuple(out_shape), in_specs=in_specs, ou...  91.8 us
    all_to_all x13, starting transfers between devices, exchange(): return lax.all_to_all(x, axis, 0, 0, tiled=True)  54.8 us
    ppermute x19, starting transfers between devices, swap(): return lax.ppermute(x, 'pipe', [(0, 1), (1, 0)])  32.6 us
    ppermute x19, waiting for transfers between devices, swap(): return lax.ppermute(x, 'pipe', [(0, 1), (1, 0)])  11.5 us
  transfers between devices with their start and end apart: 36, of which 22 were waited for; matrix products, arithmetic and copies ran while one was open for 1% of the time, Pallas kernels for 16%

profile of v5, /device:TPU:1, one launch (start us, length us, event | category | flops | bytes accessed | tf_op | source)
XLA Modules:
  0.0 433.0 jit_solution(5184483572549674224)
XLA Ops:
  12.8 4.2 shard_map.154
  17.0 16.5 %all_to_all.110.refs_0_ = bf16[8,160,256]{2,1,0:T(8,128)(2,1)S(1)} all-to-all(bf16[8,160,256]{2,1,0:T(8,128)(2,1)} %get-tuple-element.101), channel_id=1, replica_groups=mesh['pipe'=2,'ctx'=8,'tp'=8] {'ctx'}, dimensions={0} | all-to-all | bytes 1310720 | tf_op jit(solution)/shard_map/all_to_all | solution.py:717
  37.0 7.3 %all-to-all-start.1 = ((bf16[8,8,24,128]{3,2,1,0:T(8,128)(2,1)}), bf16[8,8,24,128]{3,2,1,0:T(8,128)(2,1)S(1)}, u32[]{:S(2)}, u32[]{:S(2)}) async-start(bf16[8,8,24,128]{3,2,1,0:T(8,128)(2,1)} %shard_map.155), calls=%async_computation.1 | async-start | bytes 786432 | tf_op jit(solution)/shard_map/all_to_all | solution.py:717
  48.3 6.7 %all-to-all-done.1.refs_0_ = bf16[8,8,24,128]{3,2,1,0:T(8,128)(2,1)S(1)} async-done(((bf16[8,8,24,128]{3,2,1,0:T(8,128)(2,1)}), bf16[8,8,24,128]{3,2,1,0:T(8,128)(2,1)S(1)}, u32[]{:S(2)}, u32[]{:S(2)}) %all-to-all-start.1) | async-done | bytes 393248 | tf_op jit(solution)/shard_map/all_to_all | solution.py:717
  60.2 14.7 %all_to_all.111 = bf16[8,192,256]{2,1,0:T(8,128)(2,1)S(1)} all-to-all(bf16[8,192,256]{2,1,0:T(8,128)(2,1)S(1)} %get-tuple-element.108), channel_id=1, replica_groups=mesh['pipe'=2,'ctx'=8,'tp'=8] {'ctx'}, dimensions={0} | all-to-all | bytes 1572864 | tf_op jit(solution)/shard_map/all_to_all | solution.py:717
  80.0 4.2 shard_map.161
  84.2 15.1 %all_to_all.112.refs_0_ = bf16[8,24,1024]{2,1,0:T(8,128)(2,1)S(1)} all-to-all(bf16[8,24,1024]{2,1,0:T(8,128)(2,1)S(1)} %bitcast.63), channel_id=1, replica_groups=mesh['pipe'=2,'ctx'=8,'tp'=8] {'tp'}, dimensions={0} | all-to-all | bytes 786432 | tf_op jit(solution)/shard_map/all_to_all | solution.py:717
  105.4 10.4 %all-to-all-done.4 = bf16[8,24,1024]{2,1,0:T(8,128)(2,1)S(1)} async-done(((bf16[8,24,1024]{2,1,0:T(8,128)(2,1)}), bf16[8,24,1024]{2,1,0:T(8,128)(2,1)S(1)}, u32[]{:S(2)}, u32[]{:S(2)}) %all-to-all-start.4) | async-done | bytes 393248 | tf_op jit(solution)/shard_map/all_to_all | solution.py:717
  117.5 12.7 %all_to_all.113.refs_0_ = bf16[8,24,1024]{2,1,0:T(8,128)(2,1)S(1)} all-to-all(bf16[8,24,1024]{2,1,0:T(8,128)(2,1)S(1)} %bitcast.62), channel_id=1, replica_groups=mesh['pipe'=2,'ctx'=8,'tp'=8] {'tp'}, dimensions={0} | all-to-all | bytes 786432 | tf_op jit(solution)/shard_map/all_to_all | solution.py:717
  134.5 11.9 %all_to_all.114 = bf16[8,24,1024]{2,1,0:T(8,128)(2,1)S(1)} all-to-all(bf16[8,24,1024]{2,1,0:T(8,128)(2,1)S(1)} %get-tuple-element.120), channel_id=1, replica_groups=mesh['pipe'=2,'ctx'=8,'tp'=8] {'tp'}, dimensions={0} | all-to-all | bytes 786432 | tf_op jit(solution)/shard_map/all_to_all | solution.py:717
  149.2 13.8 %all_to_all.115 = bf16[8,192,256]{2,1,0:T(8,128)(2,1)S(1)} all-to-all(bf16[8,192,256]{2,1,0:T(8,128)(2,1)S(1)} %get-tuple-element.123), channel_id=1, replica_groups=mesh['pipe'=2,'ctx'=8,'tp'=8] {'ctx'}, dimensions={0} | all-to-all | bytes 1572864 | tf_op jit(solution)/shard_map/all_to_all | solution.py:717
  171.1 11.6 %all_to_all.116.refs_0_ = bf16[8,24,1024]{2,1,0:T(8,128)(2,1)S(1)} all-to-all(bf16[8,24,1024]{2,1,0:T(8,128)(2,1)S(1)} %bitcast.64), channel_id=1, replica_groups=mesh['pipe'=2,'ctx'=8,'tp'=8] {'tp'}, dimensions={0} | all-to-all | bytes 786432 | tf_op jit(solution)/shard_map/all_to_all | solution.py:717
  184.4 11.4 %all_to_all.117 = bf16[8,24,1024]{2,1,0:T(8,128)(2,1)S(1)} all-to-all(bf16[8,24,1024]{2,1,0:T(8,128)(2,1)S(1)} %get-tuple-element.127), channel_id=1, replica_groups=mesh['pipe'=2,'ctx'=8,'tp'=8] {'tp'}, dimensions={0} | all-to-all | bytes 786432 | tf_op jit(solution)/shard_map/all_to_all | solution.py:717
  198.6 13.4 %all_to_all.118.refs_0_ = bf16[8,2,24,1024]{3,2,1,0:T(8,128)(2,1)S(1)} all-to-all(bf16[8,2,24,1024]{3,2,1,0:T(8,128)(2,1)S(1)} %get-tuple-element.129), channel_id=1, replica_groups=mesh['pipe'=2,'ctx'=8,'tp'=8] {'tp'}, dimensions={0} | all-to-all | bytes 1572864 | tf_op jit(solution)/shard_map/all_to_all | solution.py:717
  218.3 4.1 shard_map.170
  226.1 5.1 %shard_map.171 = (bf16[1536,256]{1,0:T(8,128)(2,1)S(1)}, bf16[1536,256]{1,0:T(8,128)(2,1)S(1)}, bf16[34048,1024]{1,0:T(8,128)(2,1)}) custom-call(bf16[192,1024]{1,0:T(8,128)(2,1)S(1)} %bitcast.57, bf16[34048,1024]{1,0:T(8,128)(2,1)} %get-tuple-element.133.refs_1_), custom_call_target="tpu_custom_call", output_to_operand_aliasing={{2}: (1, {})} | custom-call | tf_op jit(solution)/shard_map/pallas_call | solution.py:236
  231.2 5.3 %collective-permute-start.7 = (bf16[1536,256]{1,0:T(8,128)(2,1)S(1)}, bf16[1536,256]{1,0:T(8,128)(2,1)S(1)}, u32[]{:S(2)}, u32[]{:S(2)}) collective-permute-start(bf16[1536,256]{1,0:T(8,128)(2,1)S(1)} %get-tuple-element.135), channel_id=1, source_target_pairs={{0,64},{64,0},{1,65},{65,1},{2,66},{66,2},{3,67},{67,3},{4,68},{68... | collective-permute-start | bytes 2359304 | tf_op jit(solution)/shard_map/ppermute | solution.py:721
  243.4 12.0 %all-to-all-done.12.refs_0_ = bf16[8,192,256]{2,1,0:T(8,128)(2,1)S(1)} async-done(((bf16[8,192,256]{2,1,0:T(8,128)(2,1)}), bf16[8,192,256]{2,1,0:T(8,128)(2,1)S(1)}, u32[]{:S(2)}, u32[]{:S(2)}) %all-to-all-start.12) | async-done | bytes 786464 | tf_op jit(solution)/shard_map/all_to_all | solution.py:717
  271.8 4.6 %all-to-all-start.14 = ((bf16[8,24,1024]{2,1,0:T(8,128)(2,1)}), bf16[8,24,1024]{2,1,0:T(8,128)(2,1)S(1)}, u32[]{:S(2)}, u32[]{:S(2)}) async-start(bf16[8,24,1024]{2,1,0:T(8,128)(2,1)} %get-tuple-element.140), calls=%async_computation.14 | async-start | bytes 786432 | tf_op jit(solution)/shard_map/all_to_all | solution.py:717
  279.3 5.0 %all-to-all-done.14 = bf16[8,24,1024]{2,1,0:T(8,128)(2,1)S(1)} async-done(((bf16[8,24,1024]{2,1,0:T(8,128)(2,1)}), bf16[8,24,1024]{2,1,0:T(8,128)(2,1)S(1)}, u32[]{:S(2)}, u32[]{:S(2)}) %all-to-all-start.14) | async-done | bytes 393248 | tf_op jit(solution)/shard_map/all_to_all | solution.py:717
  284.2 3.9 shard_map.177
  294.7 5.6 %all-to-all-done.15.refs_0_ = bf16[8,24,1024]{2,1,0:T(8,128)(2,1)S(1)} async-done(((bf16[8,24,1024]{2,1,0:T(8,128)(2,1)}), bf16[8,24,1024]{2,1,0:T(8,128)(2,1)S(1)}, u32[]{:S(2)}, u32[]{:S(2)}) %all-to-all-start.15) | async-done | bytes 393248 | tf_op jit(solution)/shard_map/all_to_all | solution.py:717
  314.1 8.1 %all-to-all-done.16 = bf16[8,24,1024]{2,1,0:T(8,128)(2,1)S(1)} async-done(((bf16[8,24,1024]{2,1,0:T(8,128)(2,1)}), bf16[8,24,1024]{2,1,0:T(8,128)(2,1)S(1)}, u32[]{:S(2)}, u32[]{:S(2)}) %all-to-all-start.16) | async-done | bytes 393248 | tf_op jit(solution)/shard_map/all_to_all | solution.py:717
  322.1 5.2 %shard_map.182 = (bf16[1536,256]{1,0:T(8,128)(2,1)S(1)}, bf16[1536,256]{1,0:T(8,128)(2,1)S(1)}, bf16[34048,1024]{1,0:T(8,128)(2,1)}) custom-call(bf16[192,1024]{1,0:T(8,128)(2,1)S(1)} %bitcast.55, bf16[34048,1024]{1,0:T(8,128)(2,1)} %get-tuple-element.154.refs_1_), custom_call_target="tpu_custom_call", output_to_operand_aliasing={{2}: (1, {})} | custom-call | tf_op jit(solution)/shard_map/pallas_call | solution.py:236
  336.6 10.3 %all-to-all-done.17.refs_0_ = bf16[8,192,256]{2,1,0:T(8,128)(2,1)S(1)} async-done(((bf16[8,192,256]{2,1,0:T(8,128)(2,1)}), bf16[8,192,256]{2,1,0:T(8,128)(2,1)S(1)}, u32[]{:S(2)}, u32[]{:S(2)}) %all-to-all-start.17) | async-done | bytes 786464 | tf_op jit(solution)/shard_map/all_to_all | solution.py:717
  349.9 4.3 all-to-all-start.18
  359.6 6.8 %all-to-all-done.18.refs_0_.refs_1_ = bf16[8,48,1024]{2,1,0:T(8,128)(2,1)S(1)} async-done(((bf16[8,48,1024]{2,1,0:T(8,128)(2,1)}), bf16[8,48,1024]{2,1,0:T(8,128)(2,1)S(1)}, u32[]{:S(2)}, u32[]{:S(2)}) %all-to-all-start.18) | async-done | bytes 786464 | tf_op jit(solution)/shard_map/all_to_all | solution.py:717
  368.5 4.1 all-to-all-start.19
  375.6 9.4 %all-to-all-done.19.refs_2_ = bf16[8,160,256]{2,1,0:T(8,128)(2,1)S(1)} async-done(((bf16[8,160,256]{2,1,0:T(8,128)(2,1)}), bf16[8,160,256]{2,1,0:T(8,128)(2,1)S(1)}, u32[]{:S(2)}, u32[]{:S(2)}) %all-to-all-start.19) | async-done | bytes 655392 | tf_op jit(solution)/shard_map/all_to_all | solution.py:717
  388.3 5.4 %all-to-all-start.20 = ((bf16[8,56,1024]{2,1,0:T(8,128)(2,1)}), bf16[8,56,1024]{2,1,0:T(8,128)(2,1)S(1)}, u32[]{:S(2)}, u32[]{:S(2)}) async-start(bf16[8,56,1024]{2,1,0:T(8,128)(2,1)} %get-tuple-element.171), calls=%async_computation.21 | async-start | bytes 1835008 | tf_op jit(solution)/shard_map/all_to_all | solution.py:717
  395.6 14.5 %all-to-all-done.20.refs_0_ = bf16[8,56,1024]{2,1,0:T(8,128)(2,1)S(1)} async-done(((bf16[8,56,1024]{2,1,0:T(8,128)(2,1)}), bf16[8,56,1024]{2,1,0:T(8,128)(2,1)S(1)}, u32[]{:S(2)}, u32[]{:S(2)}) %all-to-all-start.20) | async-done | bytes 917536 | tf_op jit(solution)/shard_map/all_to_all | solution.py:717
  410.9 4.0 all-to-all-start.21
  (129 shorter events, 147.3 us)
Async XLA Ops:
  7.2 69.7 %all-gather.3.cloned.1.call-start = ((), (), s32[]{:S(2)}) async-start(), calls=%async_computation.24 | async-start | bytes 1179648 | tf_op jit(solution)/shard_map/all_gather | solution.py:754
  9.2 2.9 collective-permute-start
  33.5 23.6 %collective-permute-start.2 = (bf16[1280,256]{1,0:T(8,128)(2,1)S(1)}, bf16[1280,256]{1,0:T(8,128)(2,1)S(1)}, u32[]{:S(2)}, u32[]{:S(2)}) collective-permute-start(bf16[1280,256]{1,0:T(8,128)(2,1)S(1)} %bitcast.47), channel_id=1, source_target_pairs={{0,64},{64,0},{1,65},{65,1},{2,66},{66,2},{3,67},{67,3},{4,68},{68... | collective-permute-start | bytes 1966088 | tf_op jit(solution)/shard_map/ppermute | solution.py:721
  37.0 18.1 %all-to-all-start.1 = ((bf16[8,8,24,128]{3,2,1,0:T(8,128)(2,1)}), bf16[8,8,24,128]{3,2,1,0:T(8,128)(2,1)S(1)}, u32[]{:S(2)}, u32[]{:S(2)}) async-start(bf16[8,8,24,128]{3,2,1,0:T(8,128)(2,1)} %shard_map.155), calls=%async_computation.1 | async-start | bytes 786432 | tf_op jit(solution)/shard_map/all_to_all | solution.py:717
  44.3 87.7 %all-gather.5.cloned.1.call-start = ((), (), s32[]{:S(2)}) async-start(), calls=%async_computation.25 | async-start | bytes 1769472 | tf_op jit(solution)/shard_map/all_gather | solution.py:828
  74.9 5.2 %collective-permute-start.3 = (bf16[1536,256]{1,0:T(8,128)(2,1)S(1)}, bf16[1536,256]{1,0:T(8,128)(2,1)}, u32[]{:S(2)}, u32[]{:S(2)}) collective-permute-start(bf16[1536,256]{1,0:T(8,128)(2,1)S(1)} %bitcast.50), channel_id=1, source_target_pairs={{0,64},{64,0},{1,65},{65,1},{2,66},{66,2},{3,67},{67,3},{4,68},{68... | collective-permute-start | bytes 2359304 | tf_op jit(solution)/shard_map/ppermute | solution.py:721
  76.9 28.5 %collective-permute-start.4 = (bf16[1024,512]{1,0:T(8,128)(2,1)}, bf16[1024,512]{1,0:T(8,128)(2,1)S(1)}, u32[]{:S(2)}, u32[]{:S(2)}) collective-permute-start(bf16[1024,512]{1,0:T(8,128)(2,1)} %all-gather.3.cloned.1.call-done.refs_1_.refs_3_), channel_id=1, source_target_pairs={{0,64},{64,0},{1,65},{65,1},{2,66},{66,2},{3,67},{67,3},{4,68},{68... | collective-permute-start | bytes 3145736 | tf_op jit(solution)/shard_map/ppermute | solution.py:721
  101.8 13.9 %all-to-all-start.4 = ((bf16[8,24,1024]{2,1,0:T(8,128)(2,1)}), bf16[8,24,1024]{2,1,0:T(8,128)(2,1)S(1)}, u32[]{:S(2)}, u32[]{:S(2)}) async-start(bf16[8,24,1024]{2,1,0:T(8,128)(2,1)} %get-tuple-element.113), calls=%async_computation.4 | async-start | bytes 786432 | tf_op jit(solution)/shard_map/all_to_all | solution.py:717
  132.0 14.4 %collective-permute-start.5 = (bf16[1024,768]{1,0:T(8,128)(2,1)}, bf16[1024,768]{1,0:T(8,128)(2,1)S(1)}, u32[]{:S(2)}, u32[]{:S(2)}) collective-permute-start(bf16[1024,768]{1,0:T(8,128)(2,1)} %all-gather.5.cloned.1.call-done.refs_1_.refs_3_), channel_id=1, source_target_pairs={{0,64},{64,0},{1,65},{65,1},{2,66},{66,2},{3,67},{67,3},{4,68},{68... | collective-permute-start | bytes 4718600 | tf_op jit(solution)/shard_map/ppermute | solution.py:721
  163.0 4.9 %collective-permute-start.6 = (bf16[1536,256]{1,0:T(8,128)(2,1)S(1)}, bf16[1536,256]{1,0:T(8,128)(2,1)S(1)}, u32[]{:S(2)}, u32[]{:S(2)}) collective-permute-start(bf16[1536,256]{1,0:T(8,128)(2,1)S(1)} %bitcast.52), channel_id=1, source_target_pairs={{0,64},{64,0},{1,65},{65,1},{2,66},{66,2},{3,67},{67,3},{4,68},{68... | collective-permute-start | bytes 2359304 | tf_op jit(solution)/shard_map/ppermute | solution.py:721
  214.9 11.2 %all-to-all-start.11 = ((bf16[8,24,1024]{2,1,0:T(8,128)(2,1)}), bf16[8,24,1024]{2,1,0:T(8,128)(2,1)S(1)}, u32[]{:S(2)}, u32[]{:S(2)}) async-start(bf16[8,24,1024]{2,1,0:T(8,128)(2,1)} %get-tuple-element.131), calls=%async_computation.11 | async-start | bytes 786432 | tf_op jit(solution)/shard_map/all_to_all | solution.py:717
  231.2 7.2 %collective-permute-start.7 = (bf16[1536,256]{1,0:T(8,128)(2,1)S(1)}, bf16[1536,256]{1,0:T(8,128)(2,1)S(1)}, u32[]{:S(2)}, u32[]{:S(2)}) collective-permute-start(bf16[1536,256]{1,0:T(8,128)(2,1)S(1)} %get-tuple-element.135), channel_id=1, source_target_pairs={{0,64},{64,0},{1,65},{65,1},{2,66},{66,2},{3,67},{67,3},{4,68},{68... | collective-permute-start | bytes 2359304 | tf_op jit(solution)/shard_map/ppermute | solution.py:721
  239.4 16.0 %all-to-all-start.12 = ((bf16[8,192,256]{2,1,0:T(8,128)(2,1)}), bf16[8,192,256]{2,1,0:T(8,128)(2,1)S(1)}, u32[]{:S(2)}, u32[]{:S(2)}) async-start(bf16[8,192,256]{2,1,0:T(8,128)(2,1)} %bitcast.20), calls=%async_computation.12 | async-start | bytes 1572864 | tf_op jit(solution)/shard_map/all_to_all | solution.py:717
  243.0 33.5 %collective-permute-start.8 = (bf16[1024,512]{1,0:T(8,128)(2,1)}, bf16[1024,512]{1,0:T(8,128)(2,1)S(1)}, u32[]{:S(2)}, u32[]{:S(2)}) collective-permute-start(bf16[1024,512]{1,0:T(8,128)(2,1)} %get-tuple-element.141), channel_id=1, source_target_pairs={{0,64},{64,0},{1,65},{65,1},{2,66},{66,2},{3,67},{67,3},{4,68},{68... | collective-permute-start | bytes 3145736 | tf_op jit(solution)/shard_map/ppermute | solution.py:721
  257.9 11.2 %all-to-all-start.13 = ((bf16[8,24,1024]{2,1,0:T(8,128)(2,1)}), bf16[8,24,1024]{2,1,0:T(8,128)(2,1)S(1)}, u32[]{:S(2)}, u32[]{:S(2)}) async-start(bf16[8,24,1024]{2,1,0:T(8,128)(2,1)} %bitcast.21), calls=%async_computation.13 | async-start | bytes 786432 | tf_op jit(solution)/shard_map/all_to_all | solution.py:717
  264.3 12.2 %collective-permute-start.9 = (bf16[1024,256]{1,0:T(8,128)(2,1)S(1)}, bf16[1024,256]{1,0:T(8,128)(2,1)S(1)}, u32[]{:S(2)}, u32[]{:S(2)}) collective-permute-start(bf16[1024,256]{1,0:T(8,128)(2,1)S(1)} %get-tuple-element.142), channel_id=1, source_target_pairs={{0,64},{64,0},{1,65},{65,1},{2,66},{66,2},{3,67},{67,3},{4,68},{68... | collective-permute-start | bytes 1572872 | tf_op jit(solution)/shard_map/ppermute | solution.py:721
  271.8 12.5 %all-to-all-start.14 = ((bf16[8,24,1024]{2,1,0:T(8,128)(2,1)}), bf16[8,24,1024]{2,1,0:T(8,128)(2,1)S(1)}, u32[]{:S(2)}, u32[]{:S(2)}) async-start(bf16[8,24,1024]{2,1,0:T(8,128)(2,1)} %get-tuple-element.140), calls=%async_computation.14 | async-start | bytes 786432 | tf_op jit(solution)/shard_map/all_to_all | solution.py:717
  276.4 83.2 %reduce-scatter.3.cloned.1.call-start = ((), (), s32[]{:S(2)}) async-start(), calls=%async_computation.26 | async-start | bytes 1769472 | tf_op jit(solution)/shard_map/reduce_scatter | solution.py:855
  288.1 12.2 %all-to-all-start.15 = ((bf16[8,24,1024]{2,1,0:T(8,128)(2,1)}), bf16[8,24,1024]{2,1,0:T(8,128)(2,1)S(1)}, u32[]{:S(2)}, u32[]{:S(2)}) async-start(bf16[8,24,1024]{2,1,0:T(8,128)(2,1)} %bitcast.23), calls=%async_computation.15 | async-start | bytes 786432 | tf_op jit(solution)/shard_map/all_to_all | solution.py:717
  303.2 7.4 %collective-permute-start.10 = (bf16[1024,512]{1,0:T(8,128)(2,1)S(1)}, bf16[1024,512]{1,0:T(8,128)(2,1)S(1)}, u32[]{:S(2)}, u32[]{:S(2)}) collective-permute-start(bf16[1024,512]{1,0:T(8,128)(2,1)S(1)} %get-tuple-element.151), channel_id=1, source_target_pairs={{0,64},{64,0},{1,65},{65,1},{2,66},{66,2},{3,67},{67,3},{4,68},{68... | collective-permute-start | bytes 3145736 | tf_op jit(solution)/shard_map/ppermute | solution.py:721
  306.8 15.4 %all-to-all-start.16 = ((bf16[8,24,1024]{2,1,0:T(8,128)(2,1)}), bf16[8,24,1024]{2,1,0:T(8,128)(2,1)S(1)}, u32[]{:S(2)}, u32[]{:S(2)}) async-start(bf16[8,24,1024]{2,1,0:T(8,128)(2,1)} %get-tuple-element.150), calls=%async_computation.16 | async-start | bytes 786432 | tf_op jit(solution)/shard_map/all_to_all | solution.py:717
  327.3 2.9 collective-permute-start.11
  331.2 15.7 %all-to-all-start.17 = ((bf16[8,192,256]{2,1,0:T(8,128)(2,1)}), bf16[8,192,256]{2,1,0:T(8,128)(2,1)S(1)}, u32[]{:S(2)}, u32[]{:S(2)}) async-start(bf16[8,192,256]{2,1,0:T(8,128)(2,1)} %bitcast.25), calls=%async_computation.17 | async-start | bytes 1572864 | tf_op jit(solution)/shard_map/all_to_all | solution.py:717
  349.9 16.5 %all-to-all-start.18 = ((bf16[8,48,1024]{2,1,0:T(8,128)(2,1)}), bf16[8,48,1024]{2,1,0:T(8,128)(2,1)S(1)}, u32[]{:S(2)}, u32[]{:S(2)}) async-start(bf16[8,48,1024]{2,1,0:T(8,128)(2,1)} %get-tuple-element.160), calls=%async_computation.18 | async-start | bytes 1572864 | tf_op jit(solution)/shard_map/all_to_all | solution.py:717
  354.2 61.3 %reduce-scatter.5.cloned.1.call-start = ((), (), s32[]{:S(2)}) async-start(), calls=%async_computation.27 | async-start | bytes 1179648 | tf_op jit(solution)/shard_map/reduce_scatter | solution.py:866
  357.8 8.6 %collective-permute-start.13 = (bf16[1024,256]{1,0:T(8,128)(2,1)S(1)}, bf16[1024,256]{1,0:T(8,128)(2,1)S(1)}, u32[]{:S(2)}, u32[]{:S(2)}) collective-permute-start(bf16[1024,256]{1,0:T(8,128)(2,1)S(1)} %get-tuple-element.164), channel_id=1, source_target_pairs={{0,64},{64,0},{1,65},{65,1},{2,66},{66,2},{3,67},{67,3},{4,68},{68... | collective-permute-start | bytes 1572872 | tf_op jit(solution)/shard_map/ppermute | solution.py:721
  368.5 16.5 %all-to-all-start.19 = ((bf16[8,160,256]{2,1,0:T(8,128)(2,1)}), bf16[8,160,256]{2,1,0:T(8,128)(2,1)S(1)}, u32[]{:S(2)}, u32[]{:S(2)}) async-start(bf16[8,160,256]{2,1,0:T(8,128)(2,1)} %get-tuple-element.166), calls=%async_computation.20 | async-start | bytes 1310720 | tf_op jit(solution)/shard_map/all_to_all | solution.py:717
  373.9 12.0 %collective-permute-start.15 = (f32[24,1024]{1,0:T(8,128)S(1)}, f32[24,1024]{1,0:T(8,128)S(1)}, u32[]{:S(2)}, u32[]{:S(2)}) collective-permute-start(f32[24,1024]{1,0:T(8,128)S(1)} %get-tuple-element.170), channel_id=1, source_target_pairs={{0,64},{64,0},{1,65},{65,1},{2,66},{66,2},{3,67},{67,3},{4,68},{68... | collective-permute-start | bytes 294920 | tf_op jit(solution)/shard_map/ppermute | solution.py:721
  388.3 21.8 %all-to-all-start.20 = ((bf16[8,56,1024]{2,1,0:T(8,128)(2,1)}), bf16[8,56,1024]{2,1,0:T(8,128)(2,1)S(1)}, u32[]{:S(2)}, u32[]{:S(2)}) async-start(bf16[8,56,1024]{2,1,0:T(8,128)(2,1)} %get-tuple-element.171), calls=%async_computation.21 | async-start | bytes 1835008 | tf_op jit(solution)/shard_map/all_to_all | solution.py:717
  410.9 10.0 %all-to-all-start.21 = ((f32[8,8,1024]{2,1,0:T(8,128)}), f32[8,8,1024]{2,1,0:T(8,128)S(1)}, u32[]{:S(2)}, u32[]{:S(2)}) async-start(f32[8,8,1024]{2,1,0:T(8,128)} %shard_map.189), calls=%async_computation.22 | async-start | bytes 524288 | tf_op jit(solution)/shard_map/all_to_all | solution.py:717
  416.5 2.1 collective-permute-start.16
  420.9 3.0 collective-permute-start.18
  (14 other events, 242.6 us)
Sparse Core Ops, SparseCore 0:
  17.1 43.4 all-gather.2
  62.8 57.1 all-gather.4
  280.2 52.6 reduce-scatter.2
  357.7 50.0 reduce-scatter.4
